TPU v7x, 256 devices: a whole 4x4x8 slice. The times are simulated.
256 devices in a mesh: seq: 32 (over z, x), row: 2 (over core), col: 4 (over y).
Axes of the slice: x: 4, y: 4, z: 8, core: 2. Of those that a mesh axis runs over, the one named last changes fastest.
Arguments:
- query_proj: bfloat16 [9216, 4096], P('seq', ('row', 'col')), may hold values from -6 to 6
- key_proj: bfloat16 [9216, 4096], P('seq', ('row', 'col')), may hold values from -6 to 6
- value_proj: bfloat16 [9216, 4096], P('seq', ('row', 'col')), may hold values from -6 to 6
- query_gain: float32 [4096], P(('row', 'col')), may hold values from 1 to 6.4
- key_gain: float32 [4096], P(('row', 'col')), may hold values from 1 to 6.4
- residual: bfloat16 [9216, 6144], P(('seq', 'row'), 'col'), may hold values from -6 to 6
- out_weight: bfloat16 [4096, 6144], P('row', 'col'), may hold values from -0.09375 to 0.09375
Outputs:
- block_out: bfloat16 [9216, 6144], P(('seq', 'row'), 'col')
All inputs are finite; a program needn't handle non-finite values.
Results may differ from a plain program's by a relative error of at most 0.012.
Values may be sent and summed in bfloat16 or wider, within the bound.
No kernel may reach another device: no remote copies, remote signals or barrier semaphores. Data moves between devices by JAX's collectives and lax.ppermute only.
A program may use at most 192 MiB of HBM per device.

v0:
```python
import math

import jax
import jax.numpy as jnp
from jax import lax
from jax.sharding import PartitionSpec as P

DH = 128


epsilon = 1e-06


def normalize(values, gain_values):
    centre = jnp.mean(values, axis=-1, keepdims=True)
    shifted = values - centre
    variance = jnp.mean(shifted * shifted, axis=-1, keepdims=True)
    return shifted * lax.rsqrt(variance + epsilon) * gain_values


def body(query_proj, key_proj, value_proj, query_gain, key_gain, residual, out_weight):
    local_rows = query_proj.shape[0]
    head_count = query_proj.shape[1] // DH
    factor = 1.0 / math.sqrt(DH)
    queries = normalize(
        query_proj.astype(jnp.float32).reshape(local_rows, head_count, DH),
        query_gain.reshape(head_count, DH),
    )
    queries = (queries * factor).astype(jnp.bfloat16)
    normed = normalize(
        key_proj.astype(jnp.float32).reshape(local_rows, head_count, DH),
        key_gain.reshape(head_count, DH),
    )
    normed = normed.astype(jnp.bfloat16).reshape(local_rows, head_count * DH)
    running_max = jnp.full((local_rows, head_count), -1e30, jnp.float32)
    key_piece = lax.all_gather(normed, "seq", axis=0, tiled=True)
    value_piece = lax.all_gather(value_proj, "seq", axis=0, tiled=True)
    key_rows = key_piece.shape[0]
    key_heads = key_piece.reshape(key_rows, head_count, DH)
    value_heads = value_piece.reshape(key_rows, head_count, DH)
    scores = jnp.einsum("qhd,khd->qhk", queries, key_heads, preferred_element_type=jnp.float32)
    new_max = jnp.maximum(running_max, jnp.max(scores, axis=2))
    weights = jnp.exp(scores - new_max[:, :, None])
    new_sum = jnp.sum(weights, axis=2)
    gathered = jnp.einsum(
        "qhk,khd->qhd",
        weights.astype(jnp.bfloat16),
        value_heads,
        preferred_element_type=jnp.float32,
    )
    attended = (
        (gathered / new_sum[:, :, None]).astype(jnp.bfloat16).reshape(local_rows, head_count * DH)
    )
    columns = lax.all_gather(attended, "col", axis=1, tiled=True)
    token_block = lax.all_to_all(columns, "row", split_axis=0, concat_axis=1, tiled=True)
    product = jnp.dot(
        token_block,
        lax.all_gather(out_weight, "row", axis=0, tiled=True),
        preferred_element_type=jnp.float32,
    )
    return (residual.astype(jnp.float32) + product).astype(jnp.bfloat16)


def solution(mesh):
    placed = (
        P("seq", ("row", "col")),
        P("seq", ("row", "col")),
        P("seq", ("row", "col")),
        P(("row", "col")),
        P(("row", "col")),
        P(("seq", "row"), "col"),
        P("row", "col"),
    )
    return jax.shard_map(
        body, mesh=mesh, in_specs=placed, out_specs=P(("seq", "row"), "col"), check_vma=False
    )
```

profile of v0, /device:TPU:1, one launch (start us, length us, event | category | flops | bytes accessed | tf_op | source)
XLA Modules:
  0.0 325.3 jit_solution(9408889497654426467)
XLA Ops:
  6.5 0.0 all-gather.5.cloned.1.call-start
  6.5 1.1 reshape.56
  7.7 0.4 reduce_sum.45
  8.1 0.7 multiply_reduce_fusion.1
  8.8 0.4 mul.51
  9.2 0.4 sub.29
  9.6 1.9 fusion.20
  11.4 0.0 all-gather.5.cloned.1.call-update
  11.5 0.0 all-gather.7.cloned.1.call-start
  11.5 0.7 all-gather.7.cloned.1.call-update
  12.2 0.0 all-gather.9.cloned.1.call-start
  12.3 1.1 reshape.63
  13.4 0.4 reduce_sum.47
  13.8 0.7 multiply_reduce_fusion
  14.6 1.5 multiply_convert_fusion
  16.0 102.5 %all-gather.5.cloned.1.call-done = bf16[9216,512]{1,0:T(8,128)(2,1)} async-done(((bf16[288,512]{1,0:T(8,128)(2,1)}), bf16[9216,512]{1,0:T(8,128)(2,1)}) %all-gather.5.cloned.1.call-update) | async-done | bytes 9437200 | tf_op jit(solution)/shard_map/all_gather | solution.py:36
  118.5 12.7 %copy.18 = bf16[9216,512]{0,1:T(8,128)(2,1)} copy(bf16[9216,512]{1,0:T(8,128)(2,1)} %all-gather.5.cloned.1.call-done) | data formatting | bytes 18874368 | tf_op jit(solution)/shard_map/all_gather | solution.py:36
  131.2 19.1 %bitcast_reduce_fusion = (f32[288,4]{0,1:T(4,128)S(1)}, f32[4,9216,288]{1,2,0:T(8,128)}) fusion(bf16[9216,4,128]{0,2,1:T(8,128)(2,1)} %bitcast.54, bf16[288,4,128]{2,1,0:T(4,128)(2,1)S(1)} %multiply_convert_fusion), kind=kOutput, calls=%fused_computation.1 | convolution fusion | flops 2728524800 | bytes 52204032 | tf_op jit(solution)/shard_map/qhd,khd->qhk/dot_general | solution.py:41
  150.3 18.0 %fusion.1 = f32[288,4]{0,1:T(4,128)S(1)} fusion(f32[4,9216,288]{1,2,0:T(8,128)} %get-tuple-element.6, f32[288,4]{0,1:T(4,128)S(1)} %broadcast_maximum_fusion), kind=kLoop, calls=%fused_computation.3 | loop fusion | flops 21232512 | bytes 42476544 | tf_op jit(solution)/shard_map/reduce_sum | solution.py:44
  168.3 53.5 %all-gather.7.cloned.1.call-done = bf16[9216,512]{1,0:T(8,128)(2,1)} async-done(((bf16[288,512]{1,0:T(8,128)(2,1)}), bf16[9216,512]{1,0:T(8,128)(2,1)}) %all-gather.7.cloned.1.call-update) | async-done | bytes 9437200 | tf_op jit(solution)/shard_map/all_gather | solution.py:37
  221.7 12.7 %copy.21 = bf16[9216,512]{0,1:T(8,128)(2,1)} copy(bf16[9216,512]{1,0:T(8,128)(2,1)} %all-gather.7.cloned.1.call-done) | data formatting | bytes 18874368 | tf_op jit(solution)/shard_map/all_gather | solution.py:37
  234.4 18.4 %fusion.16 = bf16[4,36,8,128]{3,2,1,0:T(8,128)(2,1)S(1)} fusion(bf16[9216,4,128]{0,2,1:T(8,128)(2,1)} %bitcast.55, f32[4,9216,288]{1,2,0:T(8,128)} %get-tuple-element.6, f32[288,4]{0,1:T(4,128)S(1)} %broadcast_maximum_fusion, f32[288,4]{0,1:T(4,128)S(1)} %fusion.1), kind=kOutput, calls=%fused_computation.12 | convolution fusion | flops 2739437568 | bytes 52208640 | tf_op jit(solution)/shard_map/qhk,khd->qhd/dot_general | solution.py:45
  252.8 0.8 copy.38
  253.5 0.0 all-gather.9.cloned.1.call-update
  253.6 0.0 all-gather.11.cloned.1.call-start
  253.6 0.5 all-gather.11.cloned.1.call-update
  254.2 23.1 %all-gather.9.cloned.1.call-done = bf16[288,2048]{1,0:T(8,128)(2,1)} async-done(((bf16[288,512]{1,0:T(8,128)(2,1)}), bf16[288,2048]{1,0:T(8,128)(2,1)}) %all-gather.9.cloned.1.call-update) | async-done | bytes 1179664 | tf_op jit(solution)/shard_map/all_gather | solution.py:54
  277.3 7.1 %all_to_all.19 = bf16[2,144,2048]{2,1,0:T(8,128)(2,1)S(1)} all-to-all(bf16[2,144,2048]{2,1,0:T(8,128)(2,1)} %bitcast.60), channel_id=1, replica_groups=mesh['seq'=32,'row'=2,'col'=4] {'row'}, dimensions={0} | all-to-all | bytes 2359296 | tf_op jit(solution)/shard_map/all_to_all | solution.py:55
  284.3 0.1 copy.28
  284.4 27.1 %all-gather.11.cloned.1.call-done = bf16[4096,1536]{1,0:T(8,128)(2,1)} async-done(((bf16[2048,1536]{1,0:T(8,128)(2,1)}), bf16[4096,1536]{1,0:T(8,128)(2,1)}) %all-gather.11.cloned.1.call-update) | async-done | bytes 12582928 | tf_op jit(solution)/shard_map/all_gather | solution.py:58
  311.5 0.0 copy-done
  311.5 7.3 %fusion.6 = bf16[144,1536]{1,0:T(8,128)(2,1)} fusion(bf16[144,4096]{1,0:T(8,128)(2,1)S(1)} %bitcast.56, bf16[4096,1536]{1,0:T(8,128)(2,1)} %all-gather.11.cloned.1.call-done, bf16[144,1536]{1,0:T(8,128)(2,1)S(1)} %copy-done), kind=kOutput, calls=%fused_computation.8 | convolution fusion | flops 1812602880 | bytes 14647296 | tf_op jit(solution)/shard_map/dot_general | solution.py:56
  (6 shorter events, 0.1 us)
Async XLA Ops:
  6.5 112.0 %all-gather.5.cloned.1.call-start = ((), (), s32[]{:S(2)}) async-start(), calls=%async_computation.1 | async-start | bytes 9732096 | tf_op jit(solution)/shard_map/all_gather | solution.py:36
  11.5 210.3 %all-gather.7.cloned.1.call-start = ((), (), s32[]{:S(2)}) async-start(), calls=%async_computation.2 | async-start | bytes 9732096 | tf_op jit(solution)/shard_map/all_gather | solution.py:37
  12.2 265.0 %all-gather.9.cloned.1.call-start = ((), (), s32[]{:S(2)}) async-start(), calls=%async_computation.3 | async-start | bytes 1474560 | tf_op jit(solution)/shard_map/all_gather | solution.py:54
  234.4 77.1 %copy-start = (bf16[144,1536]{1,0:T(8,128)(2,1)S(1)}, bf16[144,1536]{1,0:T(8,128)(2,1)}, u32[]{:S(2)}) copy-start(bf16[144,1536]{1,0:T(8,128)(2,1)} %param.12) | copy-start | bytes 1327108
  253.6 57.9 %all-gather.11.cloned.1.call-start = ((), (), s32[]{:S(2)}) async-start(), calls=%async_computation.4 | async-start | bytes 18874368 | tf_op jit(solution)/shard_map/all_gather | solution.py:58
Sparse Core Ops, SparseCore 0:
  11.6 106.8 all-gather.4
  121.1 100.6 all-gather.6
  253.7 23.5 all-gather.8
  278.9 32.4 all-gather.10
where the time goes:
time: 326 us; the launch traced here: 325 us
  waiting for transfers between devices  207 us (63%)
  matrix products  44.8 us (14%)
  local copies, waits for them, and re-layouts  29.2 us (9%)
  other arithmetic  23.6 us (7%)
  between operations  13.2 us (4%)
  blocking collectives  7.06 us (2%)
    all_gather x1, waiting for transfers between devices, body(): key_piece = lax.all_gather(normed, 'seq', axis=0, tiled=True)  102 us
    all_gather x1, waiting for transfers between devices, body(): value_piece = lax.all_gather(value_proj, 'seq', axis=0, tiled=True)  53.5 us
    all_gather x1, waiting for transfers between devices, body(): lax.all_gather(out_weight, 'row', axis=0, tiled=True)  27.1 us
    all_gather x1, waiting for transfers between devices, body(): columns = lax.all_gather(attended, 'col', axis=1, tiled=True)  23.1 us
    dot_general x1, matrix products, body(): jnp.einsum('qhd,khd->qhk', queries, key_heads, preferred_element_type=jnp...  19.1 us
    dot_general x1, matrix products, body(): jnp.einsum('qhk,khd->qhd', weights.astype(jnp.bfloat16), value_heads, pre...  18.4 us
    reduce_sum x1, other arithmetic, body(): new_sum = jnp.sum(weights, axis=2)  18 us
    all_gather x1, local copies, waits for them, and re-layouts, body(): key_piece = lax.all_gather(normed, 'seq', axis=0, tiled=True)  12.7 us
  transfers between devices with their start and end apart: 4, of which 4 were waited for; matrix products, arithmetic and copies ran while one was open for 16% of the time, Pallas kernels for 0%

commit v1 on v0

v1 whole, which is shorter than its diff:
```python
import functools
import math

import jax
import jax.numpy as jnp
from jax import lax
from jax.experimental import pallas as pl
from jax.experimental.pallas import tpu as pltpu
from jax.sharding import Mesh, PartitionSpec as P

DH = 128
EPS = 1e-06
BF = jnp.bfloat16
F32 = jnp.float32
NZ, NX, NC, NY = 8, 4, 2, 4
ROWS = 288
HEADS = 4
GROUPS = ((0, 2), (1, 3))
NT = (((1,), (1,)), ((), ()))
SMEM = pltpu.MemorySpace.SMEM
VLIM = 48 << 20


def norm(values, gain):
    centre = jnp.mean(values, axis=-1, keepdims=True)
    shifted = values - centre
    variance = jnp.mean(shifted * shifted, axis=-1, keepdims=True)
    return shifted * lax.rsqrt(variance + EPS) * gain


def norm_kernel(turn_ref, q_ref, k_ref, v_ref, qg_ref, kg_ref, *outs):
    for j in range(HEADS):
        head = lax.rem(turn_ref[0] + j, HEADS)
        cols = pl.ds(pl.multiple_of(head * DH, DH), DH)
        outs[j][:, :DH] = norm(k_ref[:, cols].astype(F32), kg_ref[:, cols]).astype(BF)
        outs[j][:, DH:] = v_ref[:, cols]
        queries = norm(q_ref[:, cols].astype(F32), qg_ref[:, cols])
        outs[HEADS + j][...] = (queries * (1.0 / math.sqrt(DH))).astype(BF)


def flash_kernel(first, last, nkv, kb, *refs):
    queries, refs = refs[:HEADS], refs[HEADS:]
    pieces, refs = refs[:nkv], refs[nkv:]
    if not first:
        (acc_in, max_in, sum_in), refs = refs[:3], refs[3:]
    if last:
        outs, refs = refs[:HEADS], refs[HEADS:]
    else:
        outs, refs = refs[:3], refs[3:]
    kv, sem = refs
    piece = pieces[0].shape[0]
    copies = [
        pltpu.make_async_copy(pieces[i], kv.at[pl.ds(i * piece, piece)], sem.at[i])
        for i in range(nkv)
    ]
    for c in copies:
        c.start()
    for c in copies:
        c.wait()
    blocks = kv.shape[0] // kb
    for i in range(HEADS):
        rows = slice(i * ROWS, (i + 1) * ROWS)
        q = queries[i][...]

        def scores(b):
            return lax.dot_general(
                q, kv[b * kb : (b + 1) * kb, :DH], NT, preferred_element_type=F32
            )

        if first:
            high = None
        else:
            high, total, acc = max_in[rows, :1], sum_in[rows, :1], acc_in[rows, :]
        ahead = scores(0)
        for b in range(blocks):
            s = ahead
            if b + 1 < blocks:
                ahead = scores(b + 1)
            top = jnp.max(s, axis=1, keepdims=True)
            top = top if high is None else jnp.maximum(high, top)
            p = jnp.exp(s - top).astype(BF)
            v = kv[b * kb : (b + 1) * kb, DH:]
            both = jnp.dot(
                p, jnp.concatenate([v, jnp.ones_like(v)], axis=1), preferred_element_type=F32
            )
            part, psum = both[:, :DH], both[:, DH : DH + 1]
            if high is None:
                acc, total = part, psum
            else:
                scale = jnp.exp(high - top)
                acc, total = acc * scale + part, total * scale + psum
            high = top
        if last:
            outs[i][...] = (acc / total).astype(BF)
        else:
            outs[0][rows, :] = acc
            outs[1][rows, :] = jnp.broadcast_to(high, (ROWS, DH))
            outs[2][rows, :] = jnp.broadcast_to(total, (ROWS, DH))


def flash(first, last, queries, pieces, state):
    n = len(pieces)
    keys = n * pieces[0].shape[0]
    nq = HEADS * ROWS
    if last:
        shapes = [jax.ShapeDtypeStruct((ROWS, DH), BF)] * HEADS
    else:
        shapes = [jax.ShapeDtypeStruct((nq, DH), F32)] * 3
    vm = pl.BlockSpec(memory_space=pltpu.VMEM)
    return pl.pallas_call(
        functools.partial(flash_kernel, first, last, n, 1536),
        out_shape=shapes,
        in_specs=[vm] * HEADS + [pl.BlockSpec(memory_space=pl.ANY)] * n + [vm] * len(state),
        out_specs=[vm] * len(shapes),
        scratch_shapes=[pltpu.VMEM((keys, 2 * DH), BF), pltpu.SemaphoreType.DMA((n,))],
        compiler_params=pltpu.CompilerParams(vmem_limit_bytes=VLIM),
        cost_estimate=pl.CostEstimate(
            flops=8 * nq * keys * DH, bytes_accessed=keys * 512 + nq * 256, transcendentals=nq * keys
        ),
    )(*queries, *pieces, *state)


def project_kernel(pos_ref, *refs):
    blocks, (w_ref, keep_ref, send_ref, tokens) = refs[:NY], refs[NY:]
    turn, col, core = pos_ref[0], pos_ref[1], pos_ref[2]
    for s in range(NY):
        source = lax.rem(col + NY - s, NY)
        for j in range(HEADS):
            head = lax.rem(turn + j, HEADS)
            cols = pl.ds(pl.multiple_of(source * (HEADS * DH) + head * DH, DH), DH)
            tokens[:, cols] = blocks[s][:, j * DH : (j + 1) * DH]
    half = ROWS // 2
    for mine in range(2):
        start = (core if mine else 1 - core) * half
        part = tokens[pl.ds(pl.multiple_of(start, 16), half), :]
        out = jnp.dot(part, w_ref[...], preferred_element_type=F32)
        if mine:
            keep_ref[...] = out
        else:
            send_ref[...] = out


def project(pos, blocks, weight):
    vm = pl.BlockSpec(memory_space=pltpu.VMEM)
    half = ROWS // 2
    n = weight.shape[1]
    return pl.pallas_call(
        project_kernel,
        out_shape=[jax.ShapeDtypeStruct((half, n), F32)] * 2,
        in_specs=[pl.BlockSpec(memory_space=SMEM)] + [vm] * (NY + 1),
        out_specs=[vm] * 2,
        scratch_shapes=[pltpu.VMEM((ROWS, weight.shape[0]), BF)],
        compiler_params=pltpu.CompilerParams(vmem_limit_bytes=VLIM),
    )(pos, *blocks, weight)


def norms(turn, q, k, v, qg, kg):
    vm = pl.BlockSpec(memory_space=pltpu.VMEM)
    return pl.pallas_call(
        norm_kernel,
        out_shape=[jax.ShapeDtypeStruct((ROWS, 2 * DH), BF)] * HEADS
        + [jax.ShapeDtypeStruct((ROWS, DH), BF)] * HEADS,
        in_specs=[pl.BlockSpec(memory_space=SMEM)] + [vm] * 5,
        out_specs=[vm] * (2 * HEADS),
        compiler_params=pltpu.CompilerParams(vmem_limit_bytes=VLIM),
    )(turn, q, k, v, qg, kg)


def out_perm(j):
    return [
        (z * NC + c, (HEADS * c + (j + z // 2) % HEADS) * NC + z % 2)
        for z in range(NZ)
        for c in range(NC)
    ]


def to_owner(value, j):
    return lax.ppermute(value, ("z", "row"), out_perm(j))


def from_owner(value, j):
    return lax.ppermute(value, ("z", "row"), [(b, a) for a, b in out_perm(j)])


def shift(value, axis, size, step):
    return lax.ppermute(value, axis, [(i, (i + step) % size) for i in range(size)])


def swap(value):
    return lax.ppermute(value, "row", [(0, 1), (1, 0)])


def body(query_proj, key_proj, value_proj, query_gain, key_gain, residual, out_weight):
    turn = lax.axis_index("z") // 2
    pos = jnp.stack([turn, lax.axis_index("col"), lax.axis_index("row")]).astype(jnp.int32)
    outs = norms(
        pos, query_proj, key_proj, value_proj, query_gain.reshape(1, -1), key_gain.reshape(1, -1)
    )
    gathered = []
    for group in GROUPS:
        own = jnp.concatenate([to_owner(outs[j], j) for j in group], axis=0)
        held = [own] + [shift(own, "x", NX, s) for s in (1, -1, 2)]
        gathered.append(held + [swap(h) for h in held])
    queries = [to_owner(outs[HEADS + j], j) for j in range(HEADS)]
    state = flash(True, False, queries, gathered[0], ())
    attended = flash(False, True, queries, gathered[1], state)
    mine = jnp.concatenate([from_owner(attended[j], j) for j in range(HEADS)], axis=1)
    blocks = [mine] + [shift(mine, "col", NY, s) for s in (1, 2, 3)]
    keep, send = project(pos, blocks, out_weight)
    return (residual.astype(F32) + (keep + swap(send))).astype(BF)


def solution(mesh):
    fine = Mesh(mesh.devices.reshape(NZ, NX, NC, NY), ("z", "x", "row", "col"))
    seq = ("z", "x")
    heads = ("row", "col")
    placed = (
        P(seq, heads),
        P(seq, heads),
        P(seq, heads),
        P(heads),
        P(heads),
        P(("z", "x", "row"), "col"),
        P("row", "col"),
    )
    return jax.shard_map(
        body, mesh=fine, in_specs=placed, out_specs=P(("z", "x", "row"), "col"), check_vma=False
    )
```

time: 326 us -> 137 us (0.42)
  waiting for transfers between devices: 207 us -> 48.6 us
  starting transfers between devices: 0.12 us -> 60 us
  matrix products: 44.8 us -> 0 us
  local copies, waits for them, and re-layouts: 29.2 us -> 4.37 us
  other arithmetic: 23.6 us -> 1.02 us
  Pallas kernels: 0 us -> 22.2 us
  between operations: 13.2 us -> 0.25 us
  blocking collectives: 7.06 us -> 0 us
    all_gather x4 -> x0, waiting for transfers between devices: 206 us -> none  [the longest x1 102 us: body(): key_piece = lax.all_gather(normed, 'seq', axis=0, tiled=True)]
    ppermute x0 -> x30, starting transfers between devices: none -> 60 us  [the longest x8 28.2 us: to_owner(): return lax.ppermute(value, ('z', 'row'), out_perm(j))]
    ppermute x0 -> x30, waiting for transfers between devices: none -> 48.6 us  [the longest x9 33.9 us: shift(): lax.ppermute(value, axis, [(i, (i + step) % size) for i in range(size)])]
    dot_general x3 -> x0, matrix products: 44.8 us -> none  [the longest x1 19.1 us: body(): jnp.einsum('qhd,khd->qhk', queries, key_heads, preferred_element_type=jnp...]
    all_gather x2 -> x0, local copies, waits for them, and re-layouts: 25.3 us -> none  [the longest x1 12.7 us: body(): key_piece = lax.all_gather(normed, 'seq', axis=0, tiled=True)]
    pallas_call x0 -> x4, Pallas kernels: none -> 22.2 us  [the longest x2 15.5 us: flash(): pl.pallas_call(functools.partial(flash_kernel, first, last, n, 1536), out...]
    reduce_sum x5 -> x0, other arithmetic: 20.2 us -> none  [the longest x1 18 us: body(): new_sum = jnp.sum(weights, axis=2)]
    all_to_all x1 -> x0, blocking collectives: 7.06 us -> none  [body(): lax.all_to_all(columns, 'row', split_axis=0, concat_axis=1, tiled=True)]
  transfers between devices with their start and end apart: 4 -> 30, of which waited for: 4 -> 12; matrix products, arithmetic and copies ran while one was open for 16% -> 0% of each run, Pallas kernels for 0% -> 5%
where the time goes in v1:
time: 137 us; the launch traced here: 136 us
  starting transfers between devices  60 us (44%)
  waiting for transfers between devices  48.6 us (35%)
  Pallas kernels  22.2 us (16%)
  local copies, waits for them, and re-layouts  4.37 us (3%)
    ppermute x9, waiting for transfers between devices, shift(): lax.ppermute(value, axis, [(i, (i + step) % size) for i in range(size)])  33.9 us
    ppermute x8, starting transfers between devices, to_owner(): return lax.ppermute(value, ('z', 'row'), out_perm(j))  28.2 us
    pallas_call x2, Pallas kernels, flash(): pl.pallas_call(functools.partial(flash_kernel, first, last, n, 1536), out...  15.5 us
    ppermute x4, starting transfers between devices, from_owner(): return lax.ppermute(value, ('z', 'row'), [(b, a) for a, b in out_perm(j)])  13.2 us
    ppermute x9, starting transfers between devices, shift(): lax.ppermute(value, axis, [(i, (i + step) % size) for i in range(size)])  12.6 us
    ppermute x8, waiting for transfers between devices, to_owner(): return lax.ppermute(value, ('z', 'row'), out_perm(j))  7.48 us
    ppermute x9, starting transfers between devices, swap(): return lax.ppermute(value, 'row', [(0, 1), (1, 0)])  5.98 us
    ppermute x4, waiting for transfers between devices, from_owner(): return lax.ppermute(value, ('z', 'row'), [(b, a) for a, b in out_perm(j)])  5.16 us
  transfers between devices with their start and end apart: 30, of which 12 were waited for; matrix products, arithmetic and copies ran while one was open for 0% of the time, Pallas kernels for 5%

profile of v1, /device:TPU:1, one launch (start us, length us, event | category | flops | bytes accessed | tf_op | source)
XLA Modules:
  0.0 136.5 jit_solution(4495070378880414212)
XLA Ops:
  4.3 1.6 %shard_map.73 = (bf16[288,256]{1,0:T(8,128)(2,1)S(1)}, bf16[288,256]{1,0:T(8,128)(2,1)S(1)}, bf16[288,256]{1,0:T(8,128)(2,1)S(1)}, bf16[288,256]{1,0:T(8,128)(2,...) custom-call(s32[3]{0:T(128)S(1)} %pad_add_fusion.turn_ref.pos_ref, ...), custom_call_target="tpu_custom_call" | custom-call | tf_op jit(solution)/shard_map/pallas_call | solution.py:159
  5.9 9.8 %collective-permute-start.4 = (bf16[288,256]{1,0:T(8,128)(2,1)S(1)}, bf16[288,256]{1,0:T(8,128)(2,1)S(1)}, u32[]{:S(2)}, u32[]{:S(2)}) collective-permute-start(bf16[288,256]{1,0:T(8,128)(2,1)S(1)} %get-tuple-element.26), channel_id=1, source_target_pairs={{0,32},{4,160},{32,36},{36,164},{64,64},{68,192},{96,68},{100,196}... | collective-permute-start | bytes 442376 | tf_op jit(solution)/shard_map/ppermute | solution.py:178
  15.7 2.5 %collective-permute-start.13 = (bf16[288,256]{1,0:T(8,128)(2,1)S(1)}, bf16[288,256]{1,0:T(8,128)(2,1)S(1)}, u32[]{:S(2)}, u32[]{:S(2)}) collective-permute-start(bf16[288,256]{1,0:T(8,128)(2,1)S(1)} %get-tuple-element.28), channel_id=1, source_target_pairs={{0,0},{4,128},{32,4},{36,132},{64,32},{68,160},{96,36},{100,164},{... | collective-permute-start | bytes 442376 | tf_op jit(solution)/shard_map/ppermute | solution.py:178
  18.1 1.9 %collective-permute-start = (bf16[288,128]{1,0:T(8,128)(2,1)S(1)}, bf16[288,128]{1,0:T(8,128)(2,1)S(1)}, u32[]{:S(2)}, u32[]{:S(2)}) collective-permute-start(bf16[288,128]{1,0:T(8,128)(2,1)S(1)} %get-tuple-element.22), channel_id=1, source_target_pairs={{0,0},{4,128},{32,4},{36,132},{64,32},{68,160},{96,36},{100,164},{... | collective-permute-start | bytes 221192 | tf_op jit(solution)/shard_map/ppermute | solution.py:178
  20.1 6.6 %collective-permute-start.1 = (bf16[288,128]{1,0:T(8,128)(2,1)S(1)}, bf16[288,128]{1,0:T(8,128)(2,1)S(1)}, u32[]{:S(2)}, u32[]{:S(2)}) collective-permute-start(bf16[288,128]{1,0:T(8,128)(2,1)S(1)} %get-tuple-element.23), channel_id=1, source_target_pairs={{0,32},{4,160},{32,36},{36,164},{64,64},{68,192},{96,68},{100,196}... | collective-permute-start | bytes 221192 | tf_op jit(solution)/shard_map/ppermute | solution.py:178
  27.9 4.4 %collective-permute-start.5 = (bf16[288,256]{1,0:T(8,128)(2,1)S(1)}, bf16[288,256]{1,0:T(8,128)(2,1)S(1)}, u32[]{:S(2)}, u32[]{:S(2)}) collective-permute-start(bf16[288,256]{1,0:T(8,128)(2,1)S(1)} %get-tuple-element.27), channel_id=1, source_target_pairs={{0,96},{4,224},{32,100},{36,228},{64,0},{68,128},{96,4},{100,132},... | collective-permute-start | bytes 442376 | tf_op jit(solution)/shard_map/ppermute | solution.py:178
  32.3 7.5 %collective-permute-done.14 = bf16[288,256]{1,0:T(8,128)(2,1)S(1)} collective-permute-done((bf16[288,256]{1,0:T(8,128)(2,1)S(1)}, bf16[288,256]{1,0:T(8,128)(2,1)S(1)}, u32[]{:S(2)}, u32[]{:S(2)}) %collective-permute-start.14) | collective-permute-done | bytes 147488 | tf_op jit(solution)/shard_map/ppermute | solution.py:178
  39.7 1.9 %collective-permute-start.3 = (bf16[288,128]{1,0:T(8,128)(2,1)S(1)}, bf16[288,128]{1,0:T(8,128)(2,1)S(1)}, u32[]{:S(2)}, u32[]{:S(2)}) collective-permute-start(bf16[288,128]{1,0:T(8,128)(2,1)S(1)} %get-tuple-element.25), channel_id=1, source_target_pairs={{0,96},{4,224},{32,100},{36,228},{64,0},{68,128},{96,4},{100,132},... | collective-permute-start | bytes 221192 | tf_op jit(solution)/shard_map/ppermute | solution.py:178
  41.7 1.5 %collective-permute-start.18 = (bf16[576,256]{1,0:T(8,128)(2,1)S(1)}, bf16[576,256]{1,0:T(8,128)(2,1)S(1)}, u32[]{:S(2)}, u32[]{:S(2)}) collective-permute-start(bf16[576,256]{1,0:T(8,128)(2,1)S(1)} %constant_dynamic-update-slice_fusion.2.refs_4_), channel_id=1, source_target_pairs={{0,4},{4,0},{1,5},{5,1},{2,6},{6,2},{3,7},{7,3},{8,12},{12,8},{9,1... | collective-permute-start | bytes 884744 | tf_op jit(solution)/shard_map/ppermute | solution.py:190
  43.2 2.8 %collective-permute-start.17 = (bf16[576,256]{1,0:T(8,128)(2,1)S(1)}, bf16[576,256]{1,0:T(8,128)(2,1)S(1)}, u32[]{:S(2)}, u32[]{:S(2)}) collective-permute-start(bf16[576,256]{1,0:T(8,128)(2,1)S(1)} %constant_dynamic-update-slice_fusion.2.refs_4_), channel_id=1, source_target_pairs={{0,16},{8,24},{16,0},{24,8},{1,17},{9,25},{17,1},{25,9},{2,18},{10... | collective-permute-start | bytes 884744 | tf_op jit(solution)/shard_map/ppermute | solution.py:186
  47.5 2.4 %collective-permute-start.8 = (bf16[576,256]{1,0:T(8,128)(2,1)S(1)}, bf16[576,256]{1,0:T(8,128)(2,1)S(1)}, u32[]{:S(2)}, u32[]{:S(2)}) collective-permute-start(bf16[576,256]{1,0:T(8,128)(2,1)S(1)} %constant_dynamic-update-slice_fusion.refs_4_), channel_id=1, source_target_pairs={{0,16},{8,24},{16,0},{24,8},{1,17},{9,25},{17,1},{25,9},{2,18},{10... | collective-permute-start | bytes 884744 | tf_op jit(solution)/shard_map/ppermute | solution.py:186
  50.8 2.7 %collective-permute-done.17.refs_7_ = bf16[576,256]{1,0:T(8,128)(2,1)S(1)} collective-permute-done((bf16[576,256]{1,0:T(8,128)(2,1)S(1)}, bf16[576,256]{1,0:T(8,128)(2,1)S(1)}, u32[]{:S(2)}, u32[]{:S(2)}) %collective-permute-start.17) | collective-permute-done | bytes 294944 | tf_op jit(solution)/shard_map/ppermute | solution.py:186
  53.5 1.2 collective-permute-start.6
  54.7 5.2 %collective-permute-done.16.refs_6_ = bf16[576,256]{1,0:T(8,128)(2,1)S(1)} collective-permute-done((bf16[576,256]{1,0:T(8,128)(2,1)S(1)}, bf16[576,256]{1,0:T(8,128)(2,1)S(1)}, u32[]{:S(2)}, u32[]{:S(2)}) %collective-permute-start.16) | collective-permute-done | bytes 294944 | tf_op jit(solution)/shard_map/ppermute | solution.py:186
  61.0 5.1 %collective-permute-done.8.refs_7_ = bf16[576,256]{1,0:T(8,128)(2,1)S(1)} collective-permute-done((bf16[576,256]{1,0:T(8,128)(2,1)S(1)}, bf16[576,256]{1,0:T(8,128)(2,1)S(1)}, u32[]{:S(2)}, u32[]{:S(2)}) %collective-permute-start.8) | collective-permute-done | bytes 294944 | tf_op jit(solution)/shard_map/ppermute | solution.py:186
  66.1 1.2 collective-permute-start.19
  67.3 5.2 %collective-permute-done.7.refs_6_ = bf16[576,256]{1,0:T(8,128)(2,1)S(1)} collective-permute-done((bf16[576,256]{1,0:T(8,128)(2,1)S(1)}, bf16[576,256]{1,0:T(8,128)(2,1)S(1)}, u32[]{:S(2)}, u32[]{:S(2)}) %collective-permute-start.7) | collective-permute-done | bytes 294944 | tf_op jit(solution)/shard_map/ppermute | solution.py:186
  74.1 7.3 %shard_map.74 = (f32[1152,128]{1,0:T(8,128)S(1)}, f32[1152,128]{1,0:T(8,128)S(1)}, f32[1152,128]{1,0:T(8,128)S(1)}) custom-call(bf16[288,128]{1,0:T(8,128)(2,1)S(1)} %collective-permute-done.refs_0_, bf16[288,128]{1,0:T(8,128)(2,1)S(1)} %collective-permute-done.1.refs_1_, bf16[288,128]{1,0:T(8,128)(2,1)S(1)} %collective-permute-done.2.refs_2_, ...), custom_call_target="tpu_custom_call" | custom-call | flops 5435817984 | bytes 2654208 | tf_op jit(solution)/shard_map/pallas_call | solution.py:110
  81.5 8.2 %shard_map.75 = (bf16[288,128]{1,0:T(8,128)(2,1)S(1)}, bf16[288,128]{1,0:T(8,128)(2,1)S(1)}, bf16[288,128]{1,0:T(8,128)(2,1)S(1)}, bf16[288,128]{1,0:T(8,128)(2,1)S(1)}) custom-call(bf16[288,128]{1,0:T(8,128)(2,1)S(1)} %collective-permute-done.refs_0_, bf16[288,128]{1,0:T(8,128)(2,1)S(1)} %collective-permute-done.1.refs_1_, ...), custom_call_target="tpu_custom_call" | custom-call | flops 5435817984 | bytes 2654208 | tf_op jit(solution)/shard_map/pallas_call | solution.py:110
  89.7 4.1 %collective-permute-start.22 = (bf16[288,128]{1,0:T(8,128)(2,1)S(1)}, bf16[288,128]{1,0:T(8,128)(2,1)S(1)}, u32[]{:S(2)}, u32[]{:S(2)}) collective-permute-start(bf16[288,128]{1,0:T(8,128)(2,1)S(1)} %get-tuple-element.33), channel_id=1, source_target_pairs={{0,0},{128,4},{4,32},{132,36},{32,64},{160,68},{36,96},{164,100},{... | collective-permute-start | bytes 221192 | tf_op jit(solution)/shard_map/ppermute | solution.py:182
  93.8 2.9 %collective-permute-start.23 = (bf16[288,128]{1,0:T(8,128)(2,1)S(1)}, bf16[288,128]{1,0:T(8,128)(2,1)S(1)}, u32[]{:S(2)}, u32[]{:S(2)}) collective-permute-start(bf16[288,128]{1,0:T(8,128)(2,1)S(1)} %get-tuple-element.34), channel_id=1, source_target_pairs={{32,0},{160,4},{36,32},{164,36},{64,64},{192,68},{68,96},{196,100}... | collective-permute-start | bytes 221192 | tf_op jit(solution)/shard_map/ppermute | solution.py:182
  96.8 3.8 %collective-permute-start.24 = (bf16[288,128]{1,0:T(8,128)(2,1)S(1)}, bf16[288,128]{1,0:T(8,128)(2,1)S(1)}, u32[]{:S(2)}, u32[]{:S(2)}) collective-permute-start(bf16[288,128]{1,0:T(8,128)(2,1)S(1)} %get-tuple-element.35), channel_id=1, source_target_pairs={{64,0},{192,4},{68,32},{196,36},{96,64},{224,68},{100,96},{228,100... | collective-permute-start | bytes 221192 | tf_op jit(solution)/shard_map/ppermute | solution.py:182
  100.6 2.3 %collective-permute-start.25 = (bf16[288,128]{1,0:T(8,128)(2,1)S(1)}, bf16[288,128]{1,0:T(8,128)(2,1)S(1)}, u32[]{:S(2)}, u32[]{:S(2)}) collective-permute-start(bf16[288,128]{1,0:T(8,128)(2,1)S(1)} %get-tuple-element.36), channel_id=1, source_target_pairs={{96,0},{224,4},{100,32},{228,36},{0,64},{128,68},{4,96},{132,100},... | collective-permute-start | bytes 221192 | tf_op jit(solution)/shard_map/ppermute | solution.py:182
  103.0 1.7 %collective-permute-done.23 = bf16[288,128]{1,0:T(8,128)(2,1)S(1)} collective-permute-done((bf16[288,128]{1,0:T(8,128)(2,1)S(1)}, bf16[288,128]{1,0:T(8,128)(2,1)S(1)}, u32[]{:S(2)}, u32[]{:S(2)}) %collective-permute-start.23) | collective-permute-done | bytes 73760 | tf_op jit(solution)/shard_map/ppermute | solution.py:182
  104.7 1.7 %collective-permute-done.24 = bf16[288,128]{1,0:T(8,128)(2,1)S(1)} collective-permute-done((bf16[288,128]{1,0:T(8,128)(2,1)S(1)}, bf16[288,128]{1,0:T(8,128)(2,1)S(1)}, u32[]{:S(2)}, u32[]{:S(2)}) %collective-permute-start.24) | collective-permute-done | bytes 73760 | tf_op jit(solution)/shard_map/ppermute | solution.py:182
  106.5 1.7 %collective-permute-done.25 = bf16[288,128]{1,0:T(8,128)(2,1)S(1)} collective-permute-done((bf16[288,128]{1,0:T(8,128)(2,1)S(1)}, bf16[288,128]{1,0:T(8,128)(2,1)S(1)}, u32[]{:S(2)}, u32[]{:S(2)}) %collective-permute-start.25) | collective-permute-done | bytes 73760 | tf_op jit(solution)/shard_map/ppermute | solution.py:182
  108.2 2.8 %collective-permute-start.28 = (bf16[288,512]{1,0:T(8,128)(2,1)S(1)}, bf16[288,512]{1,0:T(8,128)(2,1)S(1)}, u32[]{:S(2)}, u32[]{:S(2)}) collective-permute-start(bf16[288,512]{1,0:T(8,128)(2,1)S(1)} %constant_dynamic-update-slice_fusion.4.refs_0_), channel_id=1, source_target_pairs={{0,3},{1,0},{2,1},{3,2},{4,7},{5,4},{6,5},{7,6},{8,11},{9,8},{10,9... | collective-permute-start | bytes 884744 | tf_op jit(solution)/shard_map/ppermute | solution.py:186
  112.1 5.0 %collective-permute-done.28.refs_3_ = bf16[288,512]{1,0:T(8,128)(2,1)S(1)} collective-permute-done((bf16[288,512]{1,0:T(8,128)(2,1)S(1)}, bf16[288,512]{1,0:T(8,128)(2,1)S(1)}, u32[]{:S(2)}, u32[]{:S(2)}) %collective-permute-start.28) | collective-permute-done | bytes 294944 | tf_op jit(solution)/shard_map/ppermute | solution.py:186
  117.0 2.5 %collective-permute-done.27.refs_2_ = bf16[288,512]{1,0:T(8,128)(2,1)S(1)} collective-permute-done((bf16[288,512]{1,0:T(8,128)(2,1)S(1)}, bf16[288,512]{1,0:T(8,128)(2,1)S(1)}, u32[]{:S(2)}, u32[]{:S(2)}) %collective-permute-start.27) | collective-permute-done | bytes 294944 | tf_op jit(solution)/shard_map/ppermute | solution.py:186
  119.5 8.3 %collective-permute-done.26.refs_1_ = bf16[288,512]{1,0:T(8,128)(2,1)S(1)} collective-permute-done((bf16[288,512]{1,0:T(8,128)(2,1)S(1)}, bf16[288,512]{1,0:T(8,128)(2,1)S(1)}, u32[]{:S(2)}, u32[]{:S(2)}) %collective-permute-start.26) | collective-permute-done | bytes 294944 | tf_op jit(solution)/shard_map/ppermute | solution.py:186
  127.8 5.1 %shard_map.76 = (f32[144,1536]{1,0:T(8,128)S(1)}, f32[144,1536]{1,0:T(8,128)S(1)}) custom-call(s32[3]{0:T(128)S(1)} %pad_add_fusion.turn_ref.pos_ref, bf16[288,512]{1,0:T(8,128)(2,1)S(1)} %constant_dynamic-update-slice_fusion.4.refs_0_, bf16[288,512]{1,0:T(8,128)(2,1)S(1)} %collective-permute-done.26.refs_1_, ...), custom_call_target="tpu_custom_call" | custom-call | tf_op jit(solution)/shard_map/pallas_call | solution.py:147
  133.5 2.1 %collective-permute-done.29 = f32[144,1536]{1,0:T(8,128)S(1)} collective-permute-done((f32[144,1536]{1,0:T(8,128)S(1)}, f32[144,1536]{1,0:T(8,128)S(1)}, u32[]{:S(2)}, u32[]{:S(2)}) %collective-permute-start.29) | collective-permute-done | bytes 884768 | tf_op jit(solution)/shard_map/ppermute | solution.py:190
  (54 shorter events, 13.3 us)
Async XLA Ops:
  0.1 1.0 copy-start
  5.9 21.3 %collective-permute-start.4 = (bf16[288,256]{1,0:T(8,128)(2,1)S(1)}, bf16[288,256]{1,0:T(8,128)(2,1)S(1)}, u32[]{:S(2)}, u32[]{:S(2)}) collective-permute-start(bf16[288,256]{1,0:T(8,128)(2,1)S(1)} %get-tuple-element.26), channel_id=1, source_target_pairs={{0,32},{4,160},{32,36},{36,164},{64,64},{68,192},{96,68},{100,196}... | collective-permute-start | bytes 442376 | tf_op jit(solution)/shard_map/ppermute | solution.py:178
  15.7 12.2 %collective-permute-start.13 = (bf16[288,256]{1,0:T(8,128)(2,1)S(1)}, bf16[288,256]{1,0:T(8,128)(2,1)S(1)}, u32[]{:S(2)}, u32[]{:S(2)}) collective-permute-start(bf16[288,256]{1,0:T(8,128)(2,1)S(1)} %get-tuple-element.28), channel_id=1, source_target_pairs={{0,0},{4,128},{32,4},{36,132},{64,32},{68,160},{96,36},{100,164},{... | collective-permute-start | bytes 442376 | tf_op jit(solution)/shard_map/ppermute | solution.py:178
  18.1 25.0 %collective-permute-start = (bf16[288,128]{1,0:T(8,128)(2,1)S(1)}, bf16[288,128]{1,0:T(8,128)(2,1)S(1)}, u32[]{:S(2)}, u32[]{:S(2)}) collective-permute-start(bf16[288,128]{1,0:T(8,128)(2,1)S(1)} %get-tuple-element.22), channel_id=1, source_target_pairs={{0,0},{4,128},{32,4},{36,132},{64,32},{68,160},{96,36},{100,164},{... | collective-permute-start | bytes 221192 | tf_op jit(solution)/shard_map/ppermute | solution.py:178
  20.1 26.0 %collective-permute-start.1 = (bf16[288,128]{1,0:T(8,128)(2,1)S(1)}, bf16[288,128]{1,0:T(8,128)(2,1)S(1)}, u32[]{:S(2)}, u32[]{:S(2)}) collective-permute-start(bf16[288,128]{1,0:T(8,128)(2,1)S(1)} %get-tuple-element.23), channel_id=1, source_target_pairs={{0,32},{4,160},{32,36},{36,164},{64,64},{68,192},{96,68},{100,196}... | collective-permute-start | bytes 221192 | tf_op jit(solution)/shard_map/ppermute | solution.py:178
  26.6 20.3 %collective-permute-start.2 = (bf16[288,128]{1,0:T(8,128)(2,1)S(1)}, bf16[288,128]{1,0:T(8,128)(2,1)S(1)}, u32[]{:S(2)}, u32[]{:S(2)}) collective-permute-start(bf16[288,128]{1,0:T(8,128)(2,1)S(1)} %get-tuple-element.24), channel_id=1, source_target_pairs={{0,64},{4,192},{32,68},{36,196},{64,96},{68,224},{96,100},{100,228... | collective-permute-start | bytes 221192 | tf_op jit(solution)/shard_map/ppermute | solution.py:178
  27.2 12.6 %collective-permute-start.14 = (bf16[288,256]{1,0:T(8,128)(2,1)S(1)}, bf16[288,256]{1,0:T(8,128)(2,1)S(1)}, u32[]{:S(2)}, u32[]{:S(2)}) collective-permute-start(bf16[288,256]{1,0:T(8,128)(2,1)S(1)} %get-tuple-element.29), channel_id=1, source_target_pairs={{0,64},{4,192},{32,68},{36,196},{64,96},{68,224},{96,100},{100,228... | collective-permute-start | bytes 442376 | tf_op jit(solution)/shard_map/ppermute | solution.py:178
  27.9 13.8 %collective-permute-start.5 = (bf16[288,256]{1,0:T(8,128)(2,1)S(1)}, bf16[288,256]{1,0:T(8,128)(2,1)S(1)}, u32[]{:S(2)}, u32[]{:S(2)}) collective-permute-start(bf16[288,256]{1,0:T(8,128)(2,1)S(1)} %get-tuple-element.27), channel_id=1, source_target_pairs={{0,96},{4,224},{32,100},{36,228},{64,0},{68,128},{96,4},{100,132},... | collective-permute-start | bytes 442376 | tf_op jit(solution)/shard_map/ppermute | solution.py:178
  39.7 7.8 %collective-permute-start.3 = (bf16[288,128]{1,0:T(8,128)(2,1)S(1)}, bf16[288,128]{1,0:T(8,128)(2,1)S(1)}, u32[]{:S(2)}, u32[]{:S(2)}) collective-permute-start(bf16[288,128]{1,0:T(8,128)(2,1)S(1)} %get-tuple-element.25), channel_id=1, source_target_pairs={{0,96},{4,224},{32,100},{36,228},{64,0},{68,128},{96,4},{100,132},... | collective-permute-start | bytes 221192 | tf_op jit(solution)/shard_map/ppermute | solution.py:178
  41.7 8.3 %collective-permute-start.18 = (bf16[576,256]{1,0:T(8,128)(2,1)S(1)}, bf16[576,256]{1,0:T(8,128)(2,1)S(1)}, u32[]{:S(2)}, u32[]{:S(2)}) collective-permute-start(bf16[576,256]{1,0:T(8,128)(2,1)S(1)} %constant_dynamic-update-slice_fusion.2.refs_4_), channel_id=1, source_target_pairs={{0,4},{4,0},{1,5},{5,1},{2,6},{6,2},{3,7},{7,3},{8,12},{12,8},{9,1... | collective-permute-start | bytes 884744 | tf_op jit(solution)/shard_map/ppermute | solution.py:190
  43.2 10.3 %collective-permute-start.17 = (bf16[576,256]{1,0:T(8,128)(2,1)S(1)}, bf16[576,256]{1,0:T(8,128)(2,1)S(1)}, u32[]{:S(2)}, u32[]{:S(2)}) collective-permute-start(bf16[576,256]{1,0:T(8,128)(2,1)S(1)} %constant_dynamic-update-slice_fusion.2.refs_4_), channel_id=1, source_target_pairs={{0,16},{8,24},{16,0},{24,8},{1,17},{9,25},{17,1},{25,9},{2,18},{10... | collective-permute-start | bytes 884744 | tf_op jit(solution)/shard_map/ppermute | solution.py:186
  46.0 13.8 %collective-permute-start.16 = (bf16[576,256]{1,0:T(8,128)(2,1)S(1)}, bf16[576,256]{1,0:T(8,128)(2,1)S(1)}, u32[]{:S(2)}, u32[]{:S(2)}) collective-permute-start(bf16[576,256]{1,0:T(8,128)(2,1)S(1)} %constant_dynamic-update-slice_fusion.2.refs_4_), channel_id=1, source_target_pairs={{0,24},{8,0},{16,8},{24,16},{1,25},{9,1},{17,9},{25,17},{2,26},{10... | collective-permute-start | bytes 884744 | tf_op jit(solution)/shard_map/ppermute | solution.py:186
  46.9 14.2 %collective-permute-start.15 = (bf16[576,256]{1,0:T(8,128)(2,1)S(1)}, bf16[576,256]{1,0:T(8,128)(2,1)S(1)}, u32[]{:S(2)}, u32[]{:S(2)}) collective-permute-start(bf16[576,256]{1,0:T(8,128)(2,1)S(1)} %constant_dynamic-update-slice_fusion.2.refs_4_), channel_id=1, source_target_pairs={{0,8},{8,16},{16,24},{24,0},{1,9},{9,17},{17,25},{25,1},{2,10},{10... | collective-permute-start | bytes 884744 | tf_op jit(solution)/shard_map/ppermute | solution.py:186
  47.5 18.6 %collective-permute-start.8 = (bf16[576,256]{1,0:T(8,128)(2,1)S(1)}, bf16[576,256]{1,0:T(8,128)(2,1)S(1)}, u32[]{:S(2)}, u32[]{:S(2)}) collective-permute-start(bf16[576,256]{1,0:T(8,128)(2,1)S(1)} %constant_dynamic-update-slice_fusion.refs_4_), channel_id=1, source_target_pairs={{0,16},{8,24},{16,0},{24,8},{1,17},{9,25},{17,1},{25,9},{2,18},{10... | collective-permute-start | bytes 884744 | tf_op jit(solution)/shard_map/ppermute | solution.py:186
  49.9 22.6 %collective-permute-start.7 = (bf16[576,256]{1,0:T(8,128)(2,1)S(1)}, bf16[576,256]{1,0:T(8,128)(2,1)S(1)}, u32[]{:S(2)}, u32[]{:S(2)}) collective-permute-start(bf16[576,256]{1,0:T(8,128)(2,1)S(1)} %constant_dynamic-update-slice_fusion.refs_4_), channel_id=1, source_target_pairs={{0,24},{8,0},{16,8},{24,16},{1,25},{9,1},{17,9},{25,17},{2,26},{10... | collective-permute-start | bytes 884744 | tf_op jit(solution)/shard_map/ppermute | solution.py:186
  53.5 19.9 %collective-permute-start.6 = (bf16[576,256]{1,0:T(8,128)(2,1)S(1)}, bf16[576,256]{1,0:T(8,128)(2,1)S(1)}, u32[]{:S(2)}, u32[]{:S(2)}) collective-permute-start(bf16[576,256]{1,0:T(8,128)(2,1)S(1)} %constant_dynamic-update-slice_fusion.refs_4_), channel_id=1, source_target_pairs={{0,8},{8,16},{16,24},{24,0},{1,9},{9,17},{17,25},{25,1},{2,10},{10... | collective-permute-start | bytes 884744 | tf_op jit(solution)/shard_map/ppermute | solution.py:186
  59.9 13.5 %collective-permute-start.21 = (bf16[576,256]{1,0:T(8,128)(2,1)S(1)}, bf16[576,256]{1,0:T(8,128)(2,1)S(1)}, u32[]{:S(2)}, u32[]{:S(2)}) collective-permute-start(bf16[576,256]{1,0:T(8,128)(2,1)S(1)} %collective-permute-done.17.refs_7_), channel_id=1, source_target_pairs={{0,4},{4,0},{1,5},{5,1},{2,6},{6,2},{3,7},{7,3},{8,12},{12,8},{9,1... | collective-permute-start | bytes 884744 | tf_op jit(solution)/shard_map/ppermute | solution.py:190
  61.0 12.8 %collective-permute-start.20 = (bf16[576,256]{1,0:T(8,128)(2,1)S(1)}, bf16[576,256]{1,0:T(8,128)(2,1)S(1)}, u32[]{:S(2)}, u32[]{:S(2)}) collective-permute-start(bf16[576,256]{1,0:T(8,128)(2,1)S(1)} %collective-permute-done.16.refs_6_), channel_id=1, source_target_pairs={{0,4},{4,0},{1,5},{5,1},{2,6},{6,2},{3,7},{7,3},{8,12},{12,8},{9,1... | collective-permute-start | bytes 884744 | tf_op jit(solution)/shard_map/ppermute | solution.py:190
  66.1 8.0 %collective-permute-start.19 = (bf16[576,256]{1,0:T(8,128)(2,1)S(1)}, bf16[576,256]{1,0:T(8,128)(2,1)S(1)}, u32[]{:S(2)}, u32[]{:S(2)}) collective-permute-start(bf16[576,256]{1,0:T(8,128)(2,1)S(1)} %collective-permute-done.15.refs_5_), channel_id=1, source_target_pairs={{0,4},{4,0},{1,5},{5,1},{2,6},{6,2},{3,7},{7,3},{8,12},{12,8},{9,1... | collective-permute-start | bytes 884744 | tf_op jit(solution)/shard_map/ppermute | solution.py:190
  72.6 8.9 %collective-permute-start.9 = (bf16[576,256]{1,0:T(8,128)(2,1)S(1)}, bf16[576,256]{1,0:T(8,128)(2,1)S(1)}, u32[]{:S(2)}, u32[]{:S(2)}) collective-permute-start(bf16[576,256]{1,0:T(8,128)(2,1)S(1)} %constant_dynamic-update-slice_fusion.refs_4_), channel_id=1, source_target_pairs={{0,4},{4,0},{1,5},{5,1},{2,6},{6,2},{3,7},{7,3},{8,12},{12,8},{9,1... | collective-permute-start | bytes 884744 | tf_op jit(solution)/shard_map/ppermute | solution.py:190
  73.3 8.1 %collective-permute-start.12 = (bf16[576,256]{1,0:T(8,128)(2,1)S(1)}, bf16[576,256]{1,0:T(8,128)(2,1)S(1)}, u32[]{:S(2)}, u32[]{:S(2)}) collective-permute-start(bf16[576,256]{1,0:T(8,128)(2,1)S(1)} %collective-permute-done.8.refs_7_), channel_id=1, source_target_pairs={{0,4},{4,0},{1,5},{5,1},{2,6},{6,2},{3,7},{7,3},{8,12},{12,8},{9,1... | collective-permute-start | bytes 884744 | tf_op jit(solution)/shard_map/ppermute | solution.py:190
  73.4 8.1 %collective-permute-start.11 = (bf16[576,256]{1,0:T(8,128)(2,1)S(1)}, bf16[576,256]{1,0:T(8,128)(2,1)S(1)}, u32[]{:S(2)}, u32[]{:S(2)}) collective-permute-start(bf16[576,256]{1,0:T(8,128)(2,1)S(1)} %collective-permute-done.7.refs_6_), channel_id=1, source_target_pairs={{0,4},{4,0},{1,5},{5,1},{2,6},{6,2},{3,7},{7,3},{8,12},{12,8},{9,1... | collective-permute-start | bytes 884744 | tf_op jit(solution)/shard_map/ppermute | solution.py:190
  73.9 7.6 %collective-permute-start.10 = (bf16[576,256]{1,0:T(8,128)(2,1)S(1)}, bf16[576,256]{1,0:T(8,128)(2,1)S(1)}, u32[]{:S(2)}, u32[]{:S(2)}) collective-permute-start(bf16[576,256]{1,0:T(8,128)(2,1)S(1)} %collective-permute-done.6.refs_5_), channel_id=1, source_target_pairs={{0,4},{4,0},{1,5},{5,1},{2,6},{6,2},{3,7},{7,3},{8,12},{12,8},{9,1... | collective-permute-start | bytes 884744 | tf_op jit(solution)/shard_map/ppermute | solution.py:190
  89.7 45.8 %copy-start.5 = (bf16[144,1536]{1,0:T(8,128)(2,1)S(1)}, bf16[144,1536]{1,0:T(8,128)(2,1)}, u32[]{:S(2)}) copy-start(bf16[144,1536]{1,0:T(8,128)(2,1)} %param.12) | copy-start | bytes 1327108
  89.7 13.3 %collective-permute-start.22 = (bf16[288,128]{1,0:T(8,128)(2,1)S(1)}, bf16[288,128]{1,0:T(8,128)(2,1)S(1)}, u32[]{:S(2)}, u32[]{:S(2)}) collective-permute-start(bf16[288,128]{1,0:T(8,128)(2,1)S(1)} %get-tuple-element.33), channel_id=1, source_target_pairs={{0,0},{128,4},{4,32},{132,36},{32,64},{160,68},{36,96},{164,100},{... | collective-permute-start | bytes 221192 | tf_op jit(solution)/shard_map/ppermute | solution.py:182
  93.8 10.9 %collective-permute-start.23 = (bf16[288,128]{1,0:T(8,128)(2,1)S(1)}, bf16[288,128]{1,0:T(8,128)(2,1)S(1)}, u32[]{:S(2)}, u32[]{:S(2)}) collective-permute-start(bf16[288,128]{1,0:T(8,128)(2,1)S(1)} %get-tuple-element.34), channel_id=1, source_target_pairs={{32,0},{160,4},{36,32},{164,36},{64,64},{192,68},{68,96},{196,100}... | collective-permute-start | bytes 221192 | tf_op jit(solution)/shard_map/ppermute | solution.py:182
  96.8 9.6 %collective-permute-start.24 = (bf16[288,128]{1,0:T(8,128)(2,1)S(1)}, bf16[288,128]{1,0:T(8,128)(2,1)S(1)}, u32[]{:S(2)}, u32[]{:S(2)}) collective-permute-start(bf16[288,128]{1,0:T(8,128)(2,1)S(1)} %get-tuple-element.35), channel_id=1, source_target_pairs={{64,0},{192,4},{68,32},{196,36},{96,64},{224,68},{100,96},{228,100... | collective-permute-start | bytes 221192 | tf_op jit(solution)/shard_map/ppermute | solution.py:182
  100.6 7.6 %collective-permute-start.25 = (bf16[288,128]{1,0:T(8,128)(2,1)S(1)}, bf16[288,128]{1,0:T(8,128)(2,1)S(1)}, u32[]{:S(2)}, u32[]{:S(2)}) collective-permute-start(bf16[288,128]{1,0:T(8,128)(2,1)S(1)} %get-tuple-element.36), channel_id=1, source_target_pairs={{96,0},{224,4},{100,32},{228,36},{0,64},{128,68},{4,96},{132,100},... | collective-permute-start | bytes 221192 | tf_op jit(solution)/shard_map/ppermute | solution.py:182
  108.2 8.8 %collective-permute-start.28 = (bf16[288,512]{1,0:T(8,128)(2,1)S(1)}, bf16[288,512]{1,0:T(8,128)(2,1)S(1)}, u32[]{:S(2)}, u32[]{:S(2)}) collective-permute-start(bf16[288,512]{1,0:T(8,128)(2,1)S(1)} %constant_dynamic-update-slice_fusion.4.refs_0_), channel_id=1, source_target_pairs={{0,3},{1,0},{2,1},{3,2},{4,7},{5,4},{6,5},{7,6},{8,11},{9,8},{10,9... | collective-permute-start | bytes 884744 | tf_op jit(solution)/shard_map/ppermute | solution.py:186
  111.0 8.5 %collective-permute-start.27 = (bf16[288,512]{1,0:T(8,128)(2,1)S(1)}, bf16[288,512]{1,0:T(8,128)(2,1)S(1)}, u32[]{:S(2)}, u32[]{:S(2)}) collective-permute-start(bf16[288,512]{1,0:T(8,128)(2,1)S(1)} %constant_dynamic-update-slice_fusion.4.refs_0_), channel_id=1, source_target_pairs={{0,2},{1,3},{2,0},{3,1},{4,6},{5,7},{6,4},{7,5},{8,10},{9,11},{10,... | collective-permute-start | bytes 884744 | tf_op jit(solution)/shard_map/ppermute | solution.py:186
  111.4 16.4 %collective-permute-start.26 = (bf16[288,512]{1,0:T(8,128)(2,1)S(1)}, bf16[288,512]{1,0:T(8,128)(2,1)S(1)}, u32[]{:S(2)}, u32[]{:S(2)}) collective-permute-start(bf16[288,512]{1,0:T(8,128)(2,1)S(1)} %constant_dynamic-update-slice_fusion.4.refs_0_), channel_id=1, source_target_pairs={{0,1},{1,2},{2,3},{3,0},{4,5},{5,6},{6,7},{7,4},{8,9},{9,10},{10,1... | collective-permute-start | bytes 884744 | tf_op jit(solution)/shard_map/ppermute | solution.py:186
  132.9 2.6 %collective-permute-start.29 = (f32[144,1536]{1,0:T(8,128)S(1)}, f32[144,1536]{1,0:T(8,128)S(1)}, u32[]{:S(2)}, u32[]{:S(2)}) collective-permute-start(f32[144,1536]{1,0:T(8,128)S(1)} %get-tuple-element.38), channel_id=1, source_target_pairs={{0,4},{4,0},{1,5},{5,1},{2,6},{6,2},{3,7},{7,3},{8,12},{12,8},{9,1... | collective-permute-start | bytes 2654216 | tf_op jit(solution)/shard_map/ppermute | solution.py:190
  (4 other events, 3.3 us)

commit v2 on v1

--- a/solution.py
+++ b/solution.py
@@ -15,7 +15,6 @@
 NZ, NX, NC, NY = 8, 4, 2, 4
 ROWS = 288
 HEADS = 4
-GROUPS = ((0, 2), (1, 3))
 NT = (((1,), (1,)), ((), ()))
 SMEM = pltpu.MemorySpace.SMEM
 VLIM = 48 << 20
@@ -28,14 +27,48 @@
     return shifted * lax.rsqrt(variance + EPS) * gain
 
 
-def norm_kernel(turn_ref, q_ref, k_ref, v_ref, qg_ref, kg_ref, *outs):
+def fetch(sources, held, sems):
+    copies = [pltpu.make_async_copy(a, b, sems.at[i]) for i, (a, b) in enumerate(zip(sources, held))]
+    for c in copies:
+        c.start()
+    for c in copies:
+        c.wait()
+
+
+def head_columns(turn_ref, j):
+    head = lax.rem(turn_ref[0] + j, HEADS)
+    return pl.ds(pl.multiple_of(head * DH, DH), DH)
+
+
+def key_kernel(turn_ref, k_hbm, v_hbm, g_hbm, *refs):
+    outs, (k_ref, v_ref, g_ref, sems) = refs[:HEADS], refs[HEADS:]
+    fetch((k_hbm, v_hbm, g_hbm), (k_ref, v_ref, g_ref), sems)
     for j in range(HEADS):
-        head = lax.rem(turn_ref[0] + j, HEADS)
-        cols = pl.ds(pl.multiple_of(head * DH, DH), DH)
-        outs[j][:, :DH] = norm(k_ref[:, cols].astype(F32), kg_ref[:, cols]).astype(BF)
+        cols = head_columns(turn_ref, j)
+        outs[j][:, :DH] = norm(k_ref[:, cols].astype(F32), g_ref[:, cols]).astype(BF)
         outs[j][:, DH:] = v_ref[:, cols]
-        queries = norm(q_ref[:, cols].astype(F32), qg_ref[:, cols])
-        outs[HEADS + j][...] = (queries * (1.0 / math.sqrt(DH))).astype(BF)
+
+
+def query_kernel(turn_ref, q_hbm, g_hbm, *refs):
+    outs, (q_ref, g_ref, sems) = refs[:HEADS], refs[HEADS:]
+    fetch((q_hbm, g_hbm), (q_ref, g_ref), sems)
+    for j in range(HEADS):
+        cols = head_columns(turn_ref, j)
+        queries = norm(q_ref[:, cols].astype(F32), g_ref[:, cols])
+        outs[j][...] = (queries * (1.0 / math.sqrt(DH))).astype(BF)
+
+
+def norm_call(kernel, width, turn, *arrays):
+    return pl.pallas_call(
+        kernel,
+        out_shape=[jax.ShapeDtypeStruct((ROWS, width), BF)] * HEADS,
+        in_specs=[pl.BlockSpec(memory_space=SMEM)]
+        + [pl.BlockSpec(memory_space=pltpu.MemorySpace.HBM)] * len(arrays),
+        out_specs=[pl.BlockSpec(memory_space=pltpu.VMEM)] * HEADS,
+        scratch_shapes=[pltpu.VMEM(a.shape, a.dtype) for a in arrays]
+        + [pltpu.SemaphoreType.DMA((len(arrays),))],
+        compiler_params=pltpu.CompilerParams(vmem_limit_bytes=VLIM),
+    )(turn, *arrays)
 
 
 def flash_kernel(first, last, nkv, kb, *refs):
@@ -108,36 +141,34 @@
         shapes = [jax.ShapeDtypeStruct((nq, DH), F32)] * 3
     vm = pl.BlockSpec(memory_space=pltpu.VMEM)
     return pl.pallas_call(
-        functools.partial(flash_kernel, first, last, n, 1536),
+        functools.partial(flash_kernel, first, last, n, 1152),
         out_shape=shapes,
         in_specs=[vm] * HEADS + [pl.BlockSpec(memory_space=pl.ANY)] * n + [vm] * len(state),
         out_specs=[vm] * len(shapes),
         scratch_shapes=[pltpu.VMEM((keys, 2 * DH), BF), pltpu.SemaphoreType.DMA((n,))],
         compiler_params=pltpu.CompilerParams(vmem_limit_bytes=VLIM),
-        cost_estimate=pl.CostEstimate(
-            flops=8 * nq * keys * DH, bytes_accessed=keys * 512 + nq * 256, transcendentals=nq * keys
-        ),
+        cost_estimate=pl.CostEstimate(flops=1000, bytes_accessed=1000, transcendentals=0),
     )(*queries, *pieces, *state)
 
 
 def project_kernel(pos_ref, *refs):
     blocks, (w_ref, keep_ref, send_ref, tokens) = refs[:NY], refs[NY:]
     turn, col, core = pos_ref[0], pos_ref[1], pos_ref[2]
+    half = ROWS // 2
     for s in range(NY):
         source = lax.rem(col + NY - s, NY)
         for j in range(HEADS):
             head = lax.rem(turn + j, HEADS)
             cols = pl.ds(pl.multiple_of(source * (HEADS * DH) + head * DH, DH), DH)
-            tokens[:, cols] = blocks[s][:, j * DH : (j + 1) * DH]
-    half = ROWS // 2
-    for mine in range(2):
-        start = (core if mine else 1 - core) * half
-        part = tokens[pl.ds(pl.multiple_of(start, 16), half), :]
-        out = jnp.dot(part, w_ref[...], preferred_element_type=F32)
-        if mine:
-            keep_ref[...] = out
-        else:
-            send_ref[...] = out
+            for i in range(2):
+                rows = pl.ds(pl.multiple_of(lax.rem(core + i, 2) * half, 16), half)
+                tokens[i * half : (i + 1) * half, cols] = blocks[s][rows, j * DH : (j + 1) * DH]
+    width = w_ref.shape[1]
+    step = width // 3
+    for n in range(0, width, step):
+        out = jnp.dot(tokens[...], w_ref[:, n : n + step], preferred_element_type=F32)
+        keep_ref[:, n : n + step] = out[:half]
+        send_ref[:, n : n + step] = out[half:]
 
 
 def project(pos, blocks, weight):
@@ -154,18 +185,6 @@
     )(pos, *blocks, weight)
 
 
-def norms(turn, q, k, v, qg, kg):
-    vm = pl.BlockSpec(memory_space=pltpu.VMEM)
-    return pl.pallas_call(
-        norm_kernel,
-        out_shape=[jax.ShapeDtypeStruct((ROWS, 2 * DH), BF)] * HEADS
-        + [jax.ShapeDtypeStruct((ROWS, DH), BF)] * HEADS,
-        in_specs=[pl.BlockSpec(memory_space=SMEM)] + [vm] * 5,
-        out_specs=[vm] * (2 * HEADS),
-        compiler_params=pltpu.CompilerParams(vmem_limit_bytes=VLIM),
-    )(turn, q, k, v, qg, kg)
-
-
 def out_perm(j):
     return [
         (z * NC + c, (HEADS * c + (j + z // 2) % HEADS) * NC + z % 2)
@@ -193,17 +212,18 @@
 def body(query_proj, key_proj, value_proj, query_gain, key_gain, residual, out_weight):
     turn = lax.axis_index("z") // 2
     pos = jnp.stack([turn, lax.axis_index("col"), lax.axis_index("row")]).astype(jnp.int32)
-    outs = norms(
-        pos, query_proj, key_proj, value_proj, query_gain.reshape(1, -1), key_gain.reshape(1, -1)
-    )
-    gathered = []
-    for group in GROUPS:
-        own = jnp.concatenate([to_owner(outs[j], j) for j in group], axis=0)
-        held = [own] + [shift(own, "x", NX, s) for s in (1, -1, 2)]
-        gathered.append(held + [swap(h) for h in held])
-    queries = [to_owner(outs[HEADS + j], j) for j in range(HEADS)]
-    state = flash(True, False, queries, gathered[0], ())
-    attended = flash(False, True, queries, gathered[1], state)
+    keyed = norm_call(key_kernel, 2 * DH, pos, key_proj, value_proj, key_gain.reshape(1, -1))
+    normed = norm_call(query_kernel, DH, pos, query_proj, query_gain.reshape(1, -1))
+    arrived = [to_owner(keyed[j], j) for j in range(HEADS)]
+    own = jnp.concatenate(arrived, axis=0)
+    *normed, _ = lax.optimization_barrier((*normed, own))
+    far, near, back = [shift(own, "x", NX, s) for s in (2, 1, -1)]
+    queries = [to_owner(normed[j], j) for j in range(HEADS)]
+    state = flash(True, False, queries, [own, swap(own)], ())
+    near, back, *state = lax.optimization_barrier((near, back, *state))
+    state = flash(False, False, queries, [near, back, swap(near), swap(back)], state)
+    far, *state = lax.optimization_barrier((far, *state))
+    attended = flash(False, True, queries, [far, swap(far)], state)
     mine = jnp.concatenate([from_owner(attended[j], j) for j in range(HEADS)], axis=1)
     blocks = [mine] + [shift(mine, "col", NY, s) for s in (1, 2, 3)]
     keep, send = project(pos, blocks, out_weight)

time: 137 us -> 133 us (0.971)
  waiting for transfers between devices: 48.6 us -> 42.2 us
  Pallas kernels: 22.2 us -> 25.9 us
    ppermute x9 -> x6, waiting for transfers between devices: 33.9 us -> 20.1 us  [shift(): lax.ppermute(value, axis, [(i, (i + step) % size) for i in range(size)])]
    ppermute x8, waiting for transfers between devices: 7.48 us -> 12.3 us  [to_owner(): return lax.ppermute(value, ('z', 'row'), out_perm(j))]
    ppermute x9 -> x6, starting transfers between devices: 12.6 us -> 8.18 us  [shift(): lax.ppermute(value, axis, [(i, (i + step) % size) for i in range(size)])]
    pallas_call x3 -> x5, Pallas kernels: 17.1 us -> 20.8 us  [the longest x3 18.4 us: flash(): pl.pallas_call(functools.partial(flash_kernel, first, last, n, 1152), out...]
    ppermute x8, starting transfers between devices: 28.2 us -> 30.7 us  [to_owner(): return lax.ppermute(value, ('z', 'row'), out_perm(j))]
    ppermute x9 -> x5, waiting for transfers between devices: 2.07 us -> 4.22 us  [swap(): return lax.ppermute(value, 'row', [(0, 1), (1, 0)])]
    ppermute x9 -> x5, starting transfers between devices: 5.98 us -> 6.29 us  [swap(): return lax.ppermute(value, 'row', [(0, 1), (1, 0)])]
    unnamed x17 -> x18, local copies, waits for them, and re-layouts: 4.33 us -> 4.34 us
  transfers between devices with their start and end apart: 30 -> 23, of which waited for: 12 -> 14; matrix products, arithmetic and copies ran while one was open for 0% -> 0% of each run, Pallas kernels for 5% -> 11%
where the time goes in v2:
time: 133 us
  starting transfers between devices  58.9 us (44%)
  waiting for transfers between devices  42.2 us (32%)
  Pallas kernels  25.9 us (19%)
  local copies, waits for them, and re-layouts  4.37 us (3%)
    ppermute x8, starting transfers between devices, to_owner(): return lax.ppermute(value, ('z', 'row'), out_perm(j))  30.7 us
    ppermute x6, waiting for transfers between devices, shift(): lax.ppermute(value, axis, [(i, (i + step) % size) for i in range(size)])  20.1 us
    pallas_call x3, Pallas kernels, flash(): pl.pallas_call(functools.partial(flash_kernel, first, last, n, 1152), out...  18.4 us
    ppermute x4, starting transfers between devices, from_owner(): return lax.ppermute(value, ('z', 'row'), [(b, a) for a, b in out_perm(j)])  13.7 us
    ppermute x8, waiting for transfers between devices, to_owner(): return lax.ppermute(value, ('z', 'row'), out_perm(j))  12.3 us
    ppermute x6, starting transfers between devices, shift(): lax.ppermute(value, axis, [(i, (i + step) % size) for i in range(size)])  8.18 us
    ppermute x5, starting transfers between devices, swap(): return lax.ppermute(value, 'row', [(0, 1), (1, 0)])  6.29 us
    ppermute x4, waiting for transfers between devices, from_owner(): return lax.ppermute(value, ('z', 'row'), [(b, a) for a, b in out_perm(j)])  5.59 us
  transfers between devices with their start and end apart: 23, of which 14 were waited for; matrix products, arithmetic and copies ran while one was open for 0% of the time, Pallas kernels for 11%

profile of v2, /device:TPU:1, one launch (start us, length us, event | category | flops | bytes accessed | tf_op | source)
XLA Modules:
  0.0 132.6 jit_solution(8148532085899483068)
XLA Ops:
  3.9 10.2 %collective-permute-start = (bf16[288,256]{1,0:T(8,128)(2,1)S(1)}, bf16[288,256]{1,0:T(8,128)(2,1)S(1)}, u32[]{:S(2)}, u32[]{:S(2)}) collective-permute-start(bf16[288,256]{1,0:T(8,128)(2,1)S(1)} %get-tuple-element.42), channel_id=1, source_target_pairs={{0,0},{4,128},{32,4},{36,132},{64,32},{68,160},{96,36},{100,164},{... | collective-permute-start | bytes 442376 | tf_op jit(solution)/shard_map/ppermute | solution.py:197
  14.1 1.9 %collective-permute-start.1 = (bf16[288,256]{1,0:T(8,128)(2,1)S(1)}, bf16[288,256]{1,0:T(8,128)(2,1)S(1)}, u32[]{:S(2)}, u32[]{:S(2)}) collective-permute-start(bf16[288,256]{1,0:T(8,128)(2,1)S(1)} %get-tuple-element.43), channel_id=1, source_target_pairs={{0,32},{4,160},{32,36},{36,164},{64,64},{68,192},{96,68},{100,196}... | collective-permute-start | bytes 442376 | tf_op jit(solution)/shard_map/ppermute | solution.py:197
  16.3 5.4 %collective-permute-start.3 = (bf16[288,256]{1,0:T(8,128)(2,1)S(1)}, bf16[288,256]{1,0:T(8,128)(2,1)S(1)}, u32[]{:S(2)}, u32[]{:S(2)}) collective-permute-start(bf16[288,256]{1,0:T(8,128)(2,1)S(1)} %get-tuple-element.45), channel_id=1, source_target_pairs={{0,96},{4,224},{32,100},{36,228},{64,0},{68,128},{96,4},{100,132},... | collective-permute-start | bytes 442376 | tf_op jit(solution)/shard_map/ppermute | solution.py:197
  21.7 4.0 %collective-permute-done.1 = bf16[288,256]{1,0:T(8,128)(2,1)S(1)} collective-permute-done((bf16[288,256]{1,0:T(8,128)(2,1)S(1)}, bf16[288,256]{1,0:T(8,128)(2,1)S(1)}, u32[]{:S(2)}, u32[]{:S(2)}) %collective-permute-start.1) | collective-permute-done | bytes 147488 | tf_op jit(solution)/shard_map/ppermute | solution.py:197
  25.7 3.3 %collective-permute-done.2 = bf16[288,256]{1,0:T(8,128)(2,1)S(1)} collective-permute-done((bf16[288,256]{1,0:T(8,128)(2,1)S(1)}, bf16[288,256]{1,0:T(8,128)(2,1)S(1)}, u32[]{:S(2)}, u32[]{:S(2)}) %collective-permute-start.2) | collective-permute-done | bytes 147488 | tf_op jit(solution)/shard_map/ppermute | solution.py:197
  29.0 3.1 %collective-permute-start.11 = (bf16[1152,256]{1,0:T(8,128)(2,1)S(1)}, bf16[1152,256]{1,0:T(8,128)(2,1)S(1)}, u32[]{:S(2)}, u32[]{:S(2)}) collective-permute-start(bf16[1152,256]{1,0:T(8,128)(2,1)S(1)} %constant_dynamic-update-slice_fusion.refs_4_), channel_id=1, source_target_pairs={{0,4},{4,0},{1,5},{5,1},{2,6},{6,2},{3,7},{7,3},{8,12},{12,8},{9,1... | collective-permute-start | bytes 1769480 | tf_op jit(solution)/shard_map/ppermute | solution.py:209
  32.1 2.5 %collective-permute-start.10 = (bf16[1152,256]{1,0:T(8,128)(2,1)S(1)}, bf16[1152,256]{1,0:T(8,128)(2,1)S(1)}, u32[]{:S(2)}, u32[]{:S(2)}) collective-permute-start(bf16[1152,256]{1,0:T(8,128)(2,1)S(1)} %constant_dynamic-update-slice_fusion.refs_4_), channel_id=1, source_target_pairs={{0,24},{8,0},{16,8},{24,16},{1,25},{9,1},{17,9},{25,17},{2,26},{10... | collective-permute-start | bytes 1769480 | tf_op jit(solution)/shard_map/ppermute | solution.py:205
  37.4 2.8 %collective-permute-start.4 = (bf16[288,128]{1,0:T(8,128)(2,1)S(1)}, bf16[288,128]{1,0:T(8,128)(2,1)S(1)}, u32[]{:S(2)}, u32[]{:S(2)}) collective-permute-start(bf16[288,128]{1,0:T(8,128)(2,1)S(1)} %get-tuple-element.46), channel_id=1, source_target_pairs={{0,0},{4,128},{32,4},{36,132},{64,32},{68,160},{96,36},{100,164},{... | collective-permute-start | bytes 221192 | tf_op jit(solution)/shard_map/ppermute | solution.py:197
  40.2 6.3 %collective-permute-start.5 = (bf16[288,128]{1,0:T(8,128)(2,1)S(1)}, bf16[288,128]{1,0:T(8,128)(2,1)S(1)}, u32[]{:S(2)}, u32[]{:S(2)}) collective-permute-start(bf16[288,128]{1,0:T(8,128)(2,1)S(1)} %get-tuple-element.47), channel_id=1, source_target_pairs={{0,32},{4,160},{32,36},{36,164},{64,64},{68,192},{96,68},{100,196}... | collective-permute-start | bytes 221192 | tf_op jit(solution)/shard_map/ppermute | solution.py:197
  46.7 1.3 collective-permute-done.5.refs_1_
  48.0 3.8 %collective-permute-start.7 = (bf16[288,128]{1,0:T(8,128)(2,1)S(1)}, bf16[288,128]{1,0:T(8,128)(2,1)S(1)}, u32[]{:S(2)}, u32[]{:S(2)}) collective-permute-start(bf16[288,128]{1,0:T(8,128)(2,1)S(1)} %get-tuple-element.49), channel_id=1, source_target_pairs={{0,96},{4,224},{32,100},{36,228},{64,0},{68,128},{96,4},{100,132},... | collective-permute-start | bytes 221192 | tf_op jit(solution)/shard_map/ppermute | solution.py:197
  51.8 1.7 %collective-permute-done.6.refs_2_ = bf16[288,128]{1,0:T(8,128)(2,1)S(1)} collective-permute-done((bf16[288,128]{1,0:T(8,128)(2,1)S(1)}, bf16[288,128]{1,0:T(8,128)(2,1)S(1)}, u32[]{:S(2)}, u32[]{:S(2)}) %collective-permute-start.6) | collective-permute-done | bytes 73760 | tf_op jit(solution)/shard_map/ppermute | solution.py:197
  53.5 2.1 %collective-permute-done.7.refs_3_ = bf16[288,128]{1,0:T(8,128)(2,1)S(1)} collective-permute-done((bf16[288,128]{1,0:T(8,128)(2,1)S(1)}, bf16[288,128]{1,0:T(8,128)(2,1)S(1)}, u32[]{:S(2)}, u32[]{:S(2)}) %collective-permute-start.7) | collective-permute-done | bytes 73760 | tf_op jit(solution)/shard_map/ppermute | solution.py:197
  55.5 4.2 %shard_map.75 = (f32[1152,128]{1,0:T(8,128)S(1)}, f32[1152,128]{1,0:T(8,128)S(1)}, f32[1152,128]{1,0:T(8,128)S(1)}) custom-call(bf16[288,128]{1,0:T(8,128)(2,1)S(1)} %collective-permute-done.4.refs_0_, bf16[288,128]{1,0:T(8,128)(2,1)S(1)} %collective-permute-done.5.refs_1_, bf16[288,128]{1,0:T(8,128)(2,1)S(1)} %collective-permute-done.6.refs_2_, ...), custom_call_target="tpu_custom_call" | custom-call | flops 1000 | bytes 1000 | tf_op jit(solution)/shard_map/pallas_call | solution.py:143
  59.8 1.4 %collective-permute-start.12 = (bf16[1152,256]{1,0:T(8,128)(2,1)S(1)}, bf16[1152,256]{1,0:T(8,128)(2,1)S(1)}, u32[]{:S(2)}, u32[]{:S(2)}) collective-permute-start(bf16[1152,256]{1,0:T(8,128)(2,1)S(1)} %collective-permute-done.9.refs_4_), channel_id=1, source_target_pairs={{0,4},{4,0},{1,5},{5,1},{2,6},{6,2},{3,7},{7,3},{8,12},{12,8},{9,1... | collective-permute-start | bytes 1769480 | tf_op jit(solution)/shard_map/ppermute | solution.py:209
  61.2 1.8 %collective-permute-start.8 = (bf16[1152,256]{1,0:T(8,128)(2,1)S(1)}, bf16[1152,256]{1,0:T(8,128)(2,1)S(1)}, u32[]{:S(2)}, u32[]{:S(2)}) collective-permute-start(bf16[1152,256]{1,0:T(8,128)(2,1)S(1)} %constant_dynamic-update-slice_fusion.refs_4_), channel_id=1, source_target_pairs={{0,16},{8,24},{16,0},{24,8},{1,17},{9,25},{17,1},{25,9},{2,18},{10... | collective-permute-start | bytes 1769480 | tf_op jit(solution)/shard_map/ppermute | solution.py:205
  63.6 9.0 %shard_map.76 = (f32[1152,128]{1,0:T(8,128)S(1)}, f32[1152,128]{1,0:T(8,128)S(1)}, f32[1152,128]{1,0:T(8,128)S(1)}) custom-call(bf16[288,128]{1,0:T(8,128)(2,1)S(1)} %collective-permute-done.4.refs_0_, bf16[288,128]{1,0:T(8,128)(2,1)S(1)} %collective-permute-done.5.refs_1_, bf16[288,128]{1,0:T(8,128)(2,1)S(1)} %collective-permute-done.6.refs_2_, ...), custom_call_target="tpu_custom_call" | custom-call | flops 1000 | bytes 1000 | tf_op jit(solution)/shard_map/pallas_call | solution.py:143
  72.6 4.6 %collective-permute-done.8.refs_4_ = bf16[1152,256]{1,0:T(8,128)(2,1)S(1)} collective-permute-done((bf16[1152,256]{1,0:T(8,128)(2,1)S(1)}, bf16[1152,256]{1,0:T(8,128)(2,1)S(1)}, u32[]{:S(2)}, u32[]{:S(2)}) %collective-permute-start.8) | collective-permute-done | bytes 589856 | tf_op jit(solution)/shard_map/ppermute | solution.py:205
  77.2 1.2 collective-permute-start.14
  78.5 1.6 %collective-permute-done.14.refs_5_ = bf16[1152,256]{1,0:T(8,128)(2,1)S(1)} collective-permute-done((bf16[1152,256]{1,0:T(8,128)(2,1)S(1)}, bf16[1152,256]{1,0:T(8,128)(2,1)S(1)}, u32[]{:S(2)}, u32[]{:S(2)}) %collective-permute-start.14) | collective-permute-done | bytes 589856 | tf_op jit(solution)/shard_map/ppermute | solution.py:209
  80.1 5.2 %shard_map.77 = (bf16[288,128]{1,0:T(8,128)(2,1)S(1)}, bf16[288,128]{1,0:T(8,128)(2,1)S(1)}, bf16[288,128]{1,0:T(8,128)(2,1)S(1)}, bf16[288,128]{1,0:T(8,128)(2,1)S(1)}) custom-call(bf16[288,128]{1,0:T(8,128)(2,1)S(1)} %collective-permute-done.4.refs_0_, bf16[288,128]{1,0:T(8,128)(2,1)S(1)} %collective-permute-done.5.refs_1_, ...), custom_call_target="tpu_custom_call" | custom-call | flops 1000 | bytes 1000 | tf_op jit(solution)/shard_map/pallas_call | solution.py:143
  85.3 5.0 %collective-permute-start.15 = (bf16[288,128]{1,0:T(8,128)(2,1)S(1)}, bf16[288,128]{1,0:T(8,128)(2,1)S(1)}, u32[]{:S(2)}, u32[]{:S(2)}) collective-permute-start(bf16[288,128]{1,0:T(8,128)(2,1)S(1)} %get-tuple-element.65), channel_id=1, source_target_pairs={{0,0},{128,4},{4,32},{132,36},{32,64},{160,68},{36,96},{164,100},{... | collective-permute-start | bytes 221192 | tf_op jit(solution)/shard_map/ppermute | solution.py:201
  90.3 1.9 %collective-permute-start.16 = (bf16[288,128]{1,0:T(8,128)(2,1)S(1)}, bf16[288,128]{1,0:T(8,128)(2,1)S(1)}, u32[]{:S(2)}, u32[]{:S(2)}) collective-permute-start(bf16[288,128]{1,0:T(8,128)(2,1)S(1)} %get-tuple-element.66), channel_id=1, source_target_pairs={{32,0},{160,4},{36,32},{164,36},{64,64},{192,68},{68,96},{196,100}... | collective-permute-start | bytes 221192 | tf_op jit(solution)/shard_map/ppermute | solution.py:201
  92.3 4.8 %collective-permute-start.17 = (bf16[288,128]{1,0:T(8,128)(2,1)S(1)}, bf16[288,128]{1,0:T(8,128)(2,1)S(1)}, u32[]{:S(2)}, u32[]{:S(2)}) collective-permute-start(bf16[288,128]{1,0:T(8,128)(2,1)S(1)} %get-tuple-element.67), channel_id=1, source_target_pairs={{64,0},{192,4},{68,32},{196,36},{96,64},{224,68},{100,96},{228,100... | collective-permute-start | bytes 221192 | tf_op jit(solution)/shard_map/ppermute | solution.py:201
  97.1 1.9 %collective-permute-start.18 = (bf16[288,128]{1,0:T(8,128)(2,1)S(1)}, bf16[288,128]{1,0:T(8,128)(2,1)S(1)}, u32[]{:S(2)}, u32[]{:S(2)}) collective-permute-start(bf16[288,128]{1,0:T(8,128)(2,1)S(1)} %get-tuple-element.68), channel_id=1, source_target_pairs={{96,0},{224,4},{100,32},{228,36},{0,64},{128,68},{4,96},{132,100},... | collective-permute-start | bytes 221192 | tf_op jit(solution)/shard_map/ppermute | solution.py:201
  99.8 2.5 %collective-permute-done.17 = bf16[288,128]{1,0:T(8,128)(2,1)S(1)} collective-permute-done((bf16[288,128]{1,0:T(8,128)(2,1)S(1)}, bf16[288,128]{1,0:T(8,128)(2,1)S(1)}, u32[]{:S(2)}, u32[]{:S(2)}) %collective-permute-start.17) | collective-permute-done | bytes 73760 | tf_op jit(solution)/shard_map/ppermute | solution.py:201
  102.3 2.4 %collective-permute-done.18 = bf16[288,128]{1,0:T(8,128)(2,1)S(1)} collective-permute-done((bf16[288,128]{1,0:T(8,128)(2,1)S(1)}, bf16[288,128]{1,0:T(8,128)(2,1)S(1)}, u32[]{:S(2)}, u32[]{:S(2)}) %collective-permute-start.18) | collective-permute-done | bytes 73760 | tf_op jit(solution)/shard_map/ppermute | solution.py:201
  104.7 2.8 %collective-permute-start.21 = (bf16[288,512]{1,0:T(8,128)(2,1)S(1)}, bf16[288,512]{1,0:T(8,128)(2,1)S(1)}, u32[]{:S(2)}, u32[]{:S(2)}) collective-permute-start(bf16[288,512]{1,0:T(8,128)(2,1)S(1)} %constant_dynamic-update-slice_fusion.4.refs_0_), channel_id=1, source_target_pairs={{0,3},{1,0},{2,1},{3,2},{4,7},{5,4},{6,5},{7,6},{8,11},{9,8},{10,9... | collective-permute-start | bytes 884744 | tf_op jit(solution)/shard_map/ppermute | solution.py:205
  108.6 11.5 %collective-permute-done.21.refs_3_ = bf16[288,512]{1,0:T(8,128)(2,1)S(1)} collective-permute-done((bf16[288,512]{1,0:T(8,128)(2,1)S(1)}, bf16[288,512]{1,0:T(8,128)(2,1)S(1)}, u32[]{:S(2)}, u32[]{:S(2)}) %collective-permute-start.21) | collective-permute-done | bytes 294944 | tf_op jit(solution)/shard_map/ppermute | solution.py:205
  120.1 4.0 %collective-permute-done.19.refs_1_ = bf16[288,512]{1,0:T(8,128)(2,1)S(1)} collective-permute-done((bf16[288,512]{1,0:T(8,128)(2,1)S(1)}, bf16[288,512]{1,0:T(8,128)(2,1)S(1)}, u32[]{:S(2)}, u32[]{:S(2)}) %collective-permute-start.19) | collective-permute-done | bytes 294944 | tf_op jit(solution)/shard_map/ppermute | solution.py:205
  124.0 5.1 %shard_map.78 = (f32[144,1536]{1,0:T(8,128)S(1)}, f32[144,1536]{1,0:T(8,128)S(1)}) custom-call(s32[3]{0:T(128)S(1)} %pad_add_fusion.turn_ref.pos_ref, bf16[288,512]{1,0:T(8,128)(2,1)S(1)} %constant_dynamic-update-slice_fusion.4.refs_0_, bf16[288,512]{1,0:T(8,128)(2,1)S(1)} %collective-permute-done.19.refs_1_, ...), custom_call_target="tpu_custom_call" | custom-call | tf_op jit(solution)/shard_map/pallas_call | solution.py:178
  129.6 2.1 %collective-permute-done.22 = f32[144,1536]{1,0:T(8,128)S(1)} collective-permute-done((f32[144,1536]{1,0:T(8,128)S(1)}, f32[144,1536]{1,0:T(8,128)S(1)}, u32[]{:S(2)}, u32[]{:S(2)}) %collective-permute-start.22) | collective-permute-done | bytes 884768 | tf_op jit(solution)/shard_map/ppermute | solution.py:209
  (42 shorter events, 11.0 us)
Async XLA Ops:
  0.1 1.0 copy-start.1
  1.0 1.0 copy-start.2
  2.0 0.7 copy-start.3
  3.9 17.7 %collective-permute-start = (bf16[288,256]{1,0:T(8,128)(2,1)S(1)}, bf16[288,256]{1,0:T(8,128)(2,1)S(1)}, u32[]{:S(2)}, u32[]{:S(2)}) collective-permute-start(bf16[288,256]{1,0:T(8,128)(2,1)S(1)} %get-tuple-element.42), channel_id=1, source_target_pairs={{0,0},{4,128},{32,4},{36,132},{64,32},{68,160},{96,36},{100,164},{... | collective-permute-start | bytes 442376 | tf_op jit(solution)/shard_map/ppermute | solution.py:197
  14.1 11.5 %collective-permute-start.1 = (bf16[288,256]{1,0:T(8,128)(2,1)S(1)}, bf16[288,256]{1,0:T(8,128)(2,1)S(1)}, u32[]{:S(2)}, u32[]{:S(2)}) collective-permute-start(bf16[288,256]{1,0:T(8,128)(2,1)S(1)} %get-tuple-element.43), channel_id=1, source_target_pairs={{0,32},{4,160},{32,36},{36,164},{64,64},{68,192},{96,68},{100,196}... | collective-permute-start | bytes 442376 | tf_op jit(solution)/shard_map/ppermute | solution.py:197
  16.1 12.9 %collective-permute-start.2 = (bf16[288,256]{1,0:T(8,128)(2,1)S(1)}, bf16[288,256]{1,0:T(8,128)(2,1)S(1)}, u32[]{:S(2)}, u32[]{:S(2)}) collective-permute-start(bf16[288,256]{1,0:T(8,128)(2,1)S(1)} %get-tuple-element.44), channel_id=1, source_target_pairs={{0,64},{4,192},{32,68},{36,196},{64,96},{68,224},{96,100},{100,228... | collective-permute-start | bytes 442376 | tf_op jit(solution)/shard_map/ppermute | solution.py:197
  16.3 12.7 %collective-permute-start.3 = (bf16[288,256]{1,0:T(8,128)(2,1)S(1)}, bf16[288,256]{1,0:T(8,128)(2,1)S(1)}, u32[]{:S(2)}, u32[]{:S(2)}) collective-permute-start(bf16[288,256]{1,0:T(8,128)(2,1)S(1)} %get-tuple-element.45), channel_id=1, source_target_pairs={{0,96},{4,224},{32,100},{36,228},{64,0},{68,128},{96,4},{100,132},... | collective-permute-start | bytes 442376 | tf_op jit(solution)/shard_map/ppermute | solution.py:197
  29.0 26.5 %collective-permute-start.11 = (bf16[1152,256]{1,0:T(8,128)(2,1)S(1)}, bf16[1152,256]{1,0:T(8,128)(2,1)S(1)}, u32[]{:S(2)}, u32[]{:S(2)}) collective-permute-start(bf16[1152,256]{1,0:T(8,128)(2,1)S(1)} %constant_dynamic-update-slice_fusion.refs_4_), channel_id=1, source_target_pairs={{0,4},{4,0},{1,5},{5,1},{2,6},{6,2},{3,7},{7,3},{8,12},{12,8},{9,1... | collective-permute-start | bytes 1769480 | tf_op jit(solution)/shard_map/ppermute | solution.py:209
  32.1 27.6 %collective-permute-start.10 = (bf16[1152,256]{1,0:T(8,128)(2,1)S(1)}, bf16[1152,256]{1,0:T(8,128)(2,1)S(1)}, u32[]{:S(2)}, u32[]{:S(2)}) collective-permute-start(bf16[1152,256]{1,0:T(8,128)(2,1)S(1)} %constant_dynamic-update-slice_fusion.refs_4_), channel_id=1, source_target_pairs={{0,24},{8,0},{16,8},{24,16},{1,25},{9,1},{17,9},{25,17},{2,26},{10... | collective-permute-start | bytes 1769480 | tf_op jit(solution)/shard_map/ppermute | solution.py:205
  34.6 25.2 %collective-permute-start.9 = (bf16[1152,256]{1,0:T(8,128)(2,1)S(1)}, bf16[1152,256]{1,0:T(8,128)(2,1)S(1)}, u32[]{:S(2)}, u32[]{:S(2)}) collective-permute-start(bf16[1152,256]{1,0:T(8,128)(2,1)S(1)} %constant_dynamic-update-slice_fusion.refs_4_), channel_id=1, source_target_pairs={{0,8},{8,16},{16,24},{24,0},{1,9},{9,17},{17,25},{25,1},{2,10},{10... | collective-permute-start | bytes 1769480 | tf_op jit(solution)/shard_map/ppermute | solution.py:205
  34.6 1.0 copy-start
  35.6 0.7 copy-start.4
  37.4 9.2 %collective-permute-start.4 = (bf16[288,128]{1,0:T(8,128)(2,1)S(1)}, bf16[288,128]{1,0:T(8,128)(2,1)S(1)}, u32[]{:S(2)}, u32[]{:S(2)}) collective-permute-start(bf16[288,128]{1,0:T(8,128)(2,1)S(1)} %get-tuple-element.46), channel_id=1, source_target_pairs={{0,0},{4,128},{32,4},{36,132},{64,32},{68,160},{96,36},{100,164},{... | collective-permute-start | bytes 221192 | tf_op jit(solution)/shard_map/ppermute | solution.py:197
  40.2 7.7 %collective-permute-start.5 = (bf16[288,128]{1,0:T(8,128)(2,1)S(1)}, bf16[288,128]{1,0:T(8,128)(2,1)S(1)}, u32[]{:S(2)}, u32[]{:S(2)}) collective-permute-start(bf16[288,128]{1,0:T(8,128)(2,1)S(1)} %get-tuple-element.47), channel_id=1, source_target_pairs={{0,32},{4,160},{32,36},{36,164},{64,64},{68,192},{96,68},{100,196}... | collective-permute-start | bytes 221192 | tf_op jit(solution)/shard_map/ppermute | solution.py:197
  46.6 6.9 %collective-permute-start.6 = (bf16[288,128]{1,0:T(8,128)(2,1)S(1)}, bf16[288,128]{1,0:T(8,128)(2,1)S(1)}, u32[]{:S(2)}, u32[]{:S(2)}) collective-permute-start(bf16[288,128]{1,0:T(8,128)(2,1)S(1)} %get-tuple-element.48), channel_id=1, source_target_pairs={{0,64},{4,192},{32,68},{36,196},{64,96},{68,224},{96,100},{100,228... | collective-permute-start | bytes 221192 | tf_op jit(solution)/shard_map/ppermute | solution.py:197
  48.0 7.6 %collective-permute-start.7 = (bf16[288,128]{1,0:T(8,128)(2,1)S(1)}, bf16[288,128]{1,0:T(8,128)(2,1)S(1)}, u32[]{:S(2)}, u32[]{:S(2)}) collective-permute-start(bf16[288,128]{1,0:T(8,128)(2,1)S(1)} %get-tuple-element.49), channel_id=1, source_target_pairs={{0,96},{4,224},{32,100},{36,228},{64,0},{68,128},{96,4},{100,132},... | collective-permute-start | bytes 221192 | tf_op jit(solution)/shard_map/ppermute | solution.py:197
  59.8 3.3 %collective-permute-start.12 = (bf16[1152,256]{1,0:T(8,128)(2,1)S(1)}, bf16[1152,256]{1,0:T(8,128)(2,1)S(1)}, u32[]{:S(2)}, u32[]{:S(2)}) collective-permute-start(bf16[1152,256]{1,0:T(8,128)(2,1)S(1)} %collective-permute-done.9.refs_4_), channel_id=1, source_target_pairs={{0,4},{4,0},{1,5},{5,1},{2,6},{6,2},{3,7},{7,3},{8,12},{12,8},{9,1... | collective-permute-start | bytes 1769480 | tf_op jit(solution)/shard_map/ppermute | solution.py:209
  61.1 2.5 %collective-permute-start.13 = (bf16[1152,256]{1,0:T(8,128)(2,1)S(1)}, bf16[1152,256]{1,0:T(8,128)(2,1)S(1)}, u32[]{:S(2)}, u32[]{:S(2)}) collective-permute-start(bf16[1152,256]{1,0:T(8,128)(2,1)S(1)} %collective-permute-done.10.refs_5_), channel_id=1, source_target_pairs={{0,4},{4,0},{1,5},{5,1},{2,6},{6,2},{3,7},{7,3},{8,12},{12,8},{9,1... | collective-permute-start | bytes 1769480 | tf_op jit(solution)/shard_map/ppermute | solution.py:209
  61.2 16.0 %collective-permute-start.8 = (bf16[1152,256]{1,0:T(8,128)(2,1)S(1)}, bf16[1152,256]{1,0:T(8,128)(2,1)S(1)}, u32[]{:S(2)}, u32[]{:S(2)}) collective-permute-start(bf16[1152,256]{1,0:T(8,128)(2,1)S(1)} %constant_dynamic-update-slice_fusion.refs_4_), channel_id=1, source_target_pairs={{0,16},{8,24},{16,0},{24,8},{1,17},{9,25},{17,1},{25,9},{2,18},{10... | collective-permute-start | bytes 1769480 | tf_op jit(solution)/shard_map/ppermute | solution.py:205
  72.6 59.1 %copy-start.5 = (bf16[144,1536]{1,0:T(8,128)(2,1)S(1)}, bf16[144,1536]{1,0:T(8,128)(2,1)}, u32[]{:S(2)}) copy-start(bf16[144,1536]{1,0:T(8,128)(2,1)} %param.12) | copy-start | bytes 1327108
  77.2 2.9 %collective-permute-start.14 = (bf16[1152,256]{1,0:T(8,128)(2,1)S(1)}, bf16[1152,256]{1,0:T(8,128)(2,1)S(1)}, u32[]{:S(2)}, u32[]{:S(2)}) collective-permute-start(bf16[1152,256]{1,0:T(8,128)(2,1)S(1)} %collective-permute-done.8.refs_4_), channel_id=1, source_target_pairs={{0,4},{4,0},{1,5},{5,1},{2,6},{6,2},{3,7},{7,3},{8,12},{12,8},{9,1... | collective-permute-start | bytes 1769480 | tf_op jit(solution)/shard_map/ppermute | solution.py:209
  85.3 13.7 %collective-permute-start.15 = (bf16[288,128]{1,0:T(8,128)(2,1)S(1)}, bf16[288,128]{1,0:T(8,128)(2,1)S(1)}, u32[]{:S(2)}, u32[]{:S(2)}) collective-permute-start(bf16[288,128]{1,0:T(8,128)(2,1)S(1)} %get-tuple-element.65), channel_id=1, source_target_pairs={{0,0},{128,4},{4,32},{132,36},{32,64},{160,68},{36,96},{164,100},{... | collective-permute-start | bytes 221192 | tf_op jit(solution)/shard_map/ppermute | solution.py:201
  90.3 9.4 %collective-permute-start.16 = (bf16[288,128]{1,0:T(8,128)(2,1)S(1)}, bf16[288,128]{1,0:T(8,128)(2,1)S(1)}, u32[]{:S(2)}, u32[]{:S(2)}) collective-permute-start(bf16[288,128]{1,0:T(8,128)(2,1)S(1)} %get-tuple-element.66), channel_id=1, source_target_pairs={{32,0},{160,4},{36,32},{164,36},{64,64},{192,68},{68,96},{196,100}... | collective-permute-start | bytes 221192 | tf_op jit(solution)/shard_map/ppermute | solution.py:201
  92.3 10.0 %collective-permute-start.17 = (bf16[288,128]{1,0:T(8,128)(2,1)S(1)}, bf16[288,128]{1,0:T(8,128)(2,1)S(1)}, u32[]{:S(2)}, u32[]{:S(2)}) collective-permute-start(bf16[288,128]{1,0:T(8,128)(2,1)S(1)} %get-tuple-element.67), channel_id=1, source_target_pairs={{64,0},{192,4},{68,32},{196,36},{96,64},{224,68},{100,96},{228,100... | collective-permute-start | bytes 221192 | tf_op jit(solution)/shard_map/ppermute | solution.py:201
  97.1 7.6 %collective-permute-start.18 = (bf16[288,128]{1,0:T(8,128)(2,1)S(1)}, bf16[288,128]{1,0:T(8,128)(2,1)S(1)}, u32[]{:S(2)}, u32[]{:S(2)}) collective-permute-start(bf16[288,128]{1,0:T(8,128)(2,1)S(1)} %get-tuple-element.68), channel_id=1, source_target_pairs={{96,0},{224,4},{100,32},{228,36},{0,64},{128,68},{4,96},{132,100},... | collective-permute-start | bytes 221192 | tf_op jit(solution)/shard_map/ppermute | solution.py:201
  104.7 15.3 %collective-permute-start.21 = (bf16[288,512]{1,0:T(8,128)(2,1)S(1)}, bf16[288,512]{1,0:T(8,128)(2,1)S(1)}, u32[]{:S(2)}, u32[]{:S(2)}) collective-permute-start(bf16[288,512]{1,0:T(8,128)(2,1)S(1)} %constant_dynamic-update-slice_fusion.4.refs_0_), channel_id=1, source_target_pairs={{0,3},{1,0},{2,1},{3,2},{4,7},{5,4},{6,5},{7,6},{8,11},{9,8},{10,9... | collective-permute-start | bytes 884744 | tf_op jit(solution)/shard_map/ppermute | solution.py:205
  107.5 12.5 %collective-permute-start.20 = (bf16[288,512]{1,0:T(8,128)(2,1)S(1)}, bf16[288,512]{1,0:T(8,128)(2,1)S(1)}, u32[]{:S(2)}, u32[]{:S(2)}) collective-permute-start(bf16[288,512]{1,0:T(8,128)(2,1)S(1)} %constant_dynamic-update-slice_fusion.4.refs_0_), channel_id=1, source_target_pairs={{0,2},{1,3},{2,0},{3,1},{4,6},{5,7},{6,4},{7,5},{8,10},{9,11},{10,... | collective-permute-start | bytes 884744 | tf_op jit(solution)/shard_map/ppermute | solution.py:205
  107.9 16.2 %collective-permute-start.19 = (bf16[288,512]{1,0:T(8,128)(2,1)S(1)}, bf16[288,512]{1,0:T(8,128)(2,1)S(1)}, u32[]{:S(2)}, u32[]{:S(2)}) collective-permute-start(bf16[288,512]{1,0:T(8,128)(2,1)S(1)} %constant_dynamic-update-slice_fusion.4.refs_0_), channel_id=1, source_target_pairs={{0,1},{1,2},{2,3},{3,0},{4,5},{5,6},{6,7},{7,4},{8,9},{9,10},{10,1... | collective-permute-start | bytes 884744 | tf_op jit(solution)/shard_map/ppermute | solution.py:205
  129.1 2.5 %collective-permute-start.22 = (f32[144,1536]{1,0:T(8,128)S(1)}, f32[144,1536]{1,0:T(8,128)S(1)}, u32[]{:S(2)}, u32[]{:S(2)}) collective-permute-start(f32[144,1536]{1,0:T(8,128)S(1)} %get-tuple-element.70), channel_id=1, source_target_pairs={{0,4},{4,0},{1,5},{5,1},{2,6},{6,2},{3,7},{7,3},{8,12},{12,8},{9,1... | collective-permute-start | bytes 2654216 | tf_op jit(solution)/shard_map/ppermute | solution.py:209

commit v3 on v1

v3 whole, which is shorter than its diff:
```python
import functools
import math

import jax
import jax.numpy as jnp
from jax import lax
from jax.experimental import pallas as pl
from jax.experimental.pallas import tpu as pltpu
from jax.sharding import Mesh, PartitionSpec as P

DH = 128
EPS = 1e-06
BF = jnp.bfloat16
F32 = jnp.float32
NZ, NX, NC, NY = 8, 4, 2, 4
ROWS = 288
HALF = ROWS // 2
HEADS = 4
NT = (((1,), (1,)), ((), ()))
VM = pl.BlockSpec(memory_space=pltpu.VMEM)
SM = pl.BlockSpec(memory_space=pltpu.MemorySpace.SMEM)
ANY = pl.BlockSpec(memory_space=pl.ANY)
VLIM = 40 << 20


def norm(values, gain):
    centre = jnp.mean(values, axis=-1, keepdims=True)
    shifted = values - centre
    variance = jnp.mean(shifted * shifted, axis=-1, keepdims=True)
    return shifted * lax.rsqrt(variance + EPS) * gain


def norm_kernel(pos_ref, *refs):
    sources, outs, held, sems = refs[:5], refs[5:9], refs[9:14], refs[14]
    copies = [
        pltpu.make_async_copy(a, b, sems.at[i]) for i, (a, b) in enumerate(zip(sources, held))
    ]
    for c in copies:
        c.start()
    k_ref, kg_ref, v_ref, q_ref, qg_ref = held
    heads = [lax.rem(pos_ref[0] + j, HEADS) for j in range(HEADS)]
    columns = [pl.ds(pl.multiple_of(h * DH, DH), DH) for h in heads]
    copies[0].wait()
    copies[1].wait()
    for out, cols in zip(outs, columns):
        out[:, :DH] = norm(k_ref[:, cols].astype(F32), kg_ref[:, cols]).astype(BF)
    copies[2].wait()
    for out, cols in zip(outs, columns):
        out[:, DH : 2 * DH] = v_ref[:, cols]
    copies[3].wait()
    copies[4].wait()
    for out, cols in zip(outs, columns):
        queries = norm(q_ref[:, cols].astype(F32), qg_ref[:, cols])
        out[:, 2 * DH :] = (queries * (1.0 / math.sqrt(DH))).astype(BF)


def norms(pos, *arrays):
    return pl.pallas_call(
        norm_kernel,
        out_shape=[jax.ShapeDtypeStruct((ROWS, 3 * DH), BF)] * HEADS,
        in_specs=[SM] + [ANY] * 5,
        out_specs=[VM] * HEADS,
        scratch_shapes=[pltpu.VMEM(a.shape, a.dtype) for a in arrays]
        + [pltpu.SemaphoreType.DMA((5,))],
        compiler_params=pltpu.CompilerParams(vmem_limit_bytes=62 << 20),
    )(pos, *arrays)


def flash_kernel(first, last, nkv, kb, *refs):
    queries, refs = refs[:HEADS], refs[HEADS:]
    pieces, refs = refs[:nkv], refs[nkv:]
    if not first:
        (acc_in, max_in, sum_in), refs = refs[:3], refs[3:]
    if last:
        outs, refs = refs[:HEADS], refs[HEADS:]
    else:
        outs, refs = refs[:3], refs[3:]
    kv, sem = refs
    piece = pieces[0].shape[0]
    copies = [
        pltpu.make_async_copy(pieces[i], kv.at[pl.ds(i * piece, piece)], sem.at[i])
        for i in range(nkv)
    ]
    for c in copies:
        c.start()
    for c in copies:
        c.wait()
    blocks = kv.shape[0] // kb
    for i in range(HEADS):
        rows = slice(i * ROWS, (i + 1) * ROWS)
        q = queries[i][:, 2 * DH :]

        def scores(b):
            return lax.dot_general(
                q, kv[b * kb : (b + 1) * kb, :DH], NT, preferred_element_type=F32
            )

        if first:
            high = None
        else:
            high, total, acc = max_in[rows, :1], sum_in[rows, :1], acc_in[rows, :]
        ahead = scores(0)
        for b in range(blocks):
            s = ahead
            if b + 1 < blocks:
                ahead = scores(b + 1)
            top = jnp.max(s, axis=1, keepdims=True)
            top = top if high is None else jnp.maximum(high, top)
            p = jnp.exp(s - top).astype(BF)
            v = kv[b * kb : (b + 1) * kb, DH:]
            both = jnp.dot(
                p, jnp.concatenate([v, jnp.ones_like(v)], axis=1), preferred_element_type=F32
            )
            part, psum = both[:, :DH], both[:, DH : DH + 1]
            if high is None:
                acc, total = part, psum
            else:
                scale = jnp.exp(high - top)
                acc, total = acc * scale + part, total * scale + psum
            high = top
        if last:
            outs[i][...] = (acc / total).astype(BF)
        else:
            outs[0][rows, :] = acc
            outs[1][rows, :] = jnp.broadcast_to(high, (ROWS, DH))
            outs[2][rows, :] = jnp.broadcast_to(total, (ROWS, DH))


def flash(first, last, queries, pieces, state):
    n = len(pieces)
    keys = n * pieces[0].shape[0]
    nq = HEADS * ROWS
    if last:
        shapes = [jax.ShapeDtypeStruct((ROWS, DH), BF)] * HEADS
    else:
        shapes = [jax.ShapeDtypeStruct((nq, DH), F32)] * 3
    return pl.pallas_call(
        functools.partial(flash_kernel, first, last, n, 1152),
        out_shape=shapes,
        in_specs=[VM] * HEADS + [ANY] * n + [VM] * len(state),
        out_specs=[VM] * len(shapes),
        scratch_shapes=[pltpu.VMEM((keys, 2 * DH), BF), pltpu.SemaphoreType.DMA((n,))],
        compiler_params=pltpu.CompilerParams(vmem_limit_bytes=VLIM),
        cost_estimate=pl.CostEstimate(flops=1000, bytes_accessed=1000, transcendentals=0),
    )(*queries, *pieces, *state)


def project_kernel(steps, first, last, pos_ref, w_hbm, *refs):
    n = len(steps)
    blocks, refs = refs[:n], refs[n:]
    if not first:
        acc_ref, refs = refs[0], refs[1:]
    outs, (weight, tokens, sems) = refs[: 1 + last], refs[1 + last :]
    turn, col, core = pos_ref[0], pos_ref[1], pos_ref[2]
    wide = HEADS * DH
    copies = []
    for k, s in enumerate(steps):
        source = lax.rem(col + NY - s, NY)
        rows = pl.ds(pl.multiple_of(source * wide, wide), wide)
        copies.append(pltpu.make_async_copy(w_hbm.at[rows], weight.at[k], sems.at[k]))
    for c in copies:
        c.start()
    for k in range(n):
        for j in range(HEADS):
            head = lax.rem(turn + j, HEADS)
            cols = pl.ds(pl.multiple_of(head * DH, DH), DH)
            for i in range(2):
                rows = pl.ds(pl.multiple_of(lax.rem(core + i, 2) * HALF, 16), HALF)
                tokens[k, i * HALF : (i + 1) * HALF, cols] = blocks[k][rows, j * DH : (j + 1) * DH]
    for c in copies:
        c.wait()
    total = None if first else acc_ref[...]
    for k in range(n):
        part = jnp.dot(tokens[k], weight[k], preferred_element_type=F32)
        total = part if total is None else total + part
    if last:
        outs[0][...] = total[:HALF]
        outs[1][...] = total[HALF:].astype(BF)
    else:
        outs[0][...] = total


def project(steps, last, pos, weight, blocks, *total):
    n = len(steps)
    wide, width = HEADS * DH, weight.shape[1]
    if last:
        shapes = [jax.ShapeDtypeStruct((HALF, width), t) for t in (F32, BF)]
    else:
        shapes = [jax.ShapeDtypeStruct((ROWS, width), F32)]
    return pl.pallas_call(
        functools.partial(project_kernel, steps, not total, last),
        out_shape=shapes,
        in_specs=[SM, ANY] + [VM] * (n + len(total)),
        out_specs=[VM] * len(shapes),
        scratch_shapes=[
            pltpu.VMEM((n, wide, width), BF),
            pltpu.VMEM((n, ROWS, wide), BF),
            pltpu.SemaphoreType.DMA((n,)),
        ],
        compiler_params=pltpu.CompilerParams(vmem_limit_bytes=VLIM),
    )(pos, weight, *blocks, *total)


def owner_pairs(j):
    return [
        (z * NC + c, (HEADS * c + (z + j) % HEADS) * NC + z // HEADS)
        for z in range(NZ)
        for c in range(NC)
    ]


def to_owner(value, j):
    return lax.ppermute(value, ("z", "row"), owner_pairs(j))


def from_owner(value, j):
    return lax.ppermute(value, ("z", "row"), [(b, a) for a, b in owner_pairs(j)])


def shift(value, axis, size, step):
    if step == 0:
        return value
    return lax.ppermute(value, axis, [(i, (i + step) % size) for i in range(size)])


def swap(value):
    return lax.ppermute(value, "row", [(0, 1), (1, 0)])


def body(query_proj, key_proj, value_proj, query_gain, key_gain, residual, out_weight):
    pos = jnp.stack([lax.axis_index(a) for a in ("z", "col", "row")]).astype(jnp.int32)
    ready = norms(
        pos, key_proj, key_gain.reshape(1, -1), value_proj, query_proj, query_gain.reshape(1, -1)
    )
    held = [to_owner(ready[j], j) for j in range(HEADS)]
    own = jnp.concatenate([m[:, : 2 * DH] for m in held], axis=0)
    near, back = shift(own, "x", NX, 1), shift(own, "x", NX, -1)
    state = flash(True, False, held, [own, swap(own)], ())
    half = own.shape[0] // 2
    far = [shift(near[:half], "x", NX, 1), shift(back[half:], "x", NX, -1)]
    near, back, *state = lax.optimization_barrier((near, back, *state))
    state = flash(False, False, held, [near, back, swap(near), swap(back)], state)
    *far, a, b, c = lax.optimization_barrier((*far, *state))
    attended = flash(False, True, held, far + [swap(p) for p in far], (a, b, c))
    mine = jnp.concatenate([from_owner(attended[j], j) for j in range(HEADS)], axis=1)
    far, near, back = [shift(mine, "col", NY, s) for s in (2, 1, 3)]
    total = project((0,), False, pos, out_weight, [mine])
    near, back, *total = lax.optimization_barrier((near, back, *total))
    total = project((1, 3), False, pos, out_weight, [near, back], *total)
    far, *total = lax.optimization_barrier((far, *total))
    keep, send = project((2,), True, pos, out_weight, [far], *total)
    return (residual.astype(F32) + (keep + swap(send).astype(F32))).astype(BF)


def solution(mesh):
    fine = Mesh(mesh.devices.reshape(NZ, NX, NC, NY), ("z", "x", "row", "col"))
    seq = ("z", "x")
    heads = ("row", "col")
    placed = (
        P(seq, heads),
        P(seq, heads),
        P(seq, heads),
        P(heads),
        P(heads),
        P(("z", "x", "row"), "col"),
        P("row", "col"),
    )
    return jax.shard_map(
        body, mesh=fine, in_specs=placed, out_specs=P(("z", "x", "row"), "col"), check_vma=False
    )
```

time: 137 us -> 107 us (0.78)
  starting transfers between devices: 60 us -> 40.6 us
  waiting for transfers between devices: 48.6 us -> 37.6 us
  Pallas kernels: 22.2 us -> 26.7 us
  local copies, waits for them, and re-layouts: 4.37 us -> 0.18 us
    ppermute x9 -> x7, waiting for transfers between devices: 33.9 us -> 15.1 us  [shift(): lax.ppermute(value, axis, [(i, (i + step) % size) for i in range(size)])]
    ppermute x12 -> x8, starting transfers between devices: 41.4 us -> 27.8 us  [the longest x4 14.6 us: to_owner(): return lax.ppermute(value, ('z', 'row'), owner_pairs(j))]
    ppermute x12 -> x8, waiting for transfers between devices: 12.6 us -> 19.4 us  [the longest x4 15.4 us: to_owner(): return lax.ppermute(value, ('z', 'row'), owner_pairs(j))]
    pallas_call x4 -> x7, Pallas kernels: 22.2 us -> 26.7 us  [the longest x3 18.4 us: flash(): pl.pallas_call(functools.partial(flash_kernel, first, last, n, 1152), out...]
    unnamed x17 -> x11, local copies, waits for them, and re-layouts: 4.33 us -> 0.08 us
    ppermute x9 -> x6, starting transfers between devices: 5.98 us -> 2.92 us  [swap(): return lax.ppermute(value, 'row', [(0, 1), (1, 0)])]
    ppermute x9 -> x7, starting transfers between devices: 12.6 us -> 9.93 us  [shift(): lax.ppermute(value, axis, [(i, (i + step) % size) for i in range(size)])]
    ppermute x9 -> x6, waiting for transfers between devices: 2.07 us -> 3.1 us  [swap(): return lax.ppermute(value, 'row', [(0, 1), (1, 0)])]
  transfers between devices with their start and end apart: 30 -> 21, of which waited for: 12 -> 12; matrix products, arithmetic and copies ran while one was open for 0% -> 0% of each run, Pallas kernels for 5% -> 16%
where the time goes in v3:
time: 107 us
  starting transfers between devices  40.6 us (38%)
  waiting for transfers between devices  37.6 us (35%)
  Pallas kernels  26.7 us (25%)
  other arithmetic  1.57 us (1%)
    pallas_call x3, Pallas kernels, flash(): pl.pallas_call(functools.partial(flash_kernel, first, last, n, 1152), out...  18.4 us
    ppermute x4, waiting for transfers between devices, to_owner(): return lax.ppermute(value, ('z', 'row'), owner_pairs(j))  15.4 us
    ppermute x7, waiting for transfers between devices, shift(): lax.ppermute(value, axis, [(i, (i + step) % size) for i in range(size)])  15.1 us
    ppermute x4, starting transfers between devices, to_owner(): return lax.ppermute(value, ('z', 'row'), owner_pairs(j))  14.6 us
    ppermute x4, starting transfers between devices, from_owner(): lax.ppermute(value, ('z', 'row'), [(b, a) for a, b in owner_pairs(j)])  13.2 us
    ppermute x7, starting transfers between devices, shift(): lax.ppermute(value, axis, [(i, (i + step) % size) for i in range(size)])  9.93 us
    pallas_call x3, Pallas kernels, project(): pl.pallas_call(functools.partial(project_kernel, steps, not total, last),...  4.8 us
    ppermute x4, waiting for transfers between devices, from_owner(): lax.ppermute(value, ('z', 'row'), [(b, a) for a, b in owner_pairs(j)])  4.02 us
  transfers between devices with their start and end apart: 21, of which 12 were waited for; matrix products, arithmetic and copies ran while one was open for 0% of the time, Pallas kernels for 16%

profile of v3, /device:TPU:1, one launch (start us, length us, event | category | flops | bytes accessed | tf_op | source)
XLA Modules:
  0.0 106.9 jit_solution(7782639192825892459)
XLA Ops:
  0.6 3.5 %shard_map.73 = (bf16[288,384]{1,0:T(8,128)(2,1)}, bf16[288,384]{1,0:T(8,128)(2,1)}, bf16[288,384]{1,0:T(8,128)(2,1)}, bf16[288,384]{1,0:T(8,128)(2,1)}) custom-call(s32[3]{0:T(128)} %pad_add_fusion.pos_ref, bf16[288,512]{1,0:T(8,128)(2,1)} %refs_0_.1, f32[1,512]{1,0:T(1,128)} %bitcast.7, bf16[288,512]{1,0:T(8,128)(2,1)} %refs_2_.1, ...), custom_call_target="tpu_custom_call" | custom-call | tf_op jit(solution)/shard_map/pallas_call | solution.py:58
  4.1 10.2 %collective-permute-start = (bf16[288,384]{1,0:T(8,128)(2,1)}, bf16[288,384]{1,0:T(8,128)(2,1)S(1)}, u32[]{:S(2)}, u32[]{:S(2)}) collective-permute-start(bf16[288,384]{1,0:T(8,128)(2,1)} %get-tuple-element.36), channel_id=1, source_target_pairs={{0,0},{4,128},{32,32},{36,160},{64,64},{68,192},{96,96},{100,224},... | collective-permute-start | bytes 663560 | tf_op jit(solution)/shard_map/ppermute | solution.py:213
  14.4 4.3 %collective-permute-start.2 = (bf16[288,384]{1,0:T(8,128)(2,1)}, bf16[288,384]{1,0:T(8,128)(2,1)S(1)}, u32[]{:S(2)}, u32[]{:S(2)}) collective-permute-start(bf16[288,384]{1,0:T(8,128)(2,1)} %get-tuple-element.38), channel_id=1, source_target_pairs={{0,64},{4,192},{32,96},{36,224},{64,0},{68,128},{96,32},{100,160},... | collective-permute-start | bytes 663560 | tf_op jit(solution)/shard_map/ppermute | solution.py:213
  18.7 3.8 %collective-permute-done.refs_0_ = bf16[288,384]{1,0:T(8,128)(2,1)S(1)} collective-permute-done((bf16[288,384]{1,0:T(8,128)(2,1)}, bf16[288,384]{1,0:T(8,128)(2,1)S(1)}, u32[]{:S(2)}, u32[]{:S(2)}) %collective-permute-start) | collective-permute-done | bytes 221216 | tf_op jit(solution)/shard_map/ppermute | solution.py:213
  22.5 3.6 %collective-permute-done.1.refs_1_ = bf16[288,384]{1,0:T(8,128)(2,1)S(1)} collective-permute-done((bf16[288,384]{1,0:T(8,128)(2,1)}, bf16[288,384]{1,0:T(8,128)(2,1)S(1)}, u32[]{:S(2)}, u32[]{:S(2)}) %collective-permute-start.1) | collective-permute-done | bytes 221216 | tf_op jit(solution)/shard_map/ppermute | solution.py:213
  26.2 2.6 %collective-permute-done.2.refs_2_ = bf16[288,384]{1,0:T(8,128)(2,1)S(1)} collective-permute-done((bf16[288,384]{1,0:T(8,128)(2,1)}, bf16[288,384]{1,0:T(8,128)(2,1)S(1)}, u32[]{:S(2)}, u32[]{:S(2)}) %collective-permute-start.2) | collective-permute-done | bytes 221216 | tf_op jit(solution)/shard_map/ppermute | solution.py:213
  28.8 5.4 %collective-permute-done.3.refs_3_ = bf16[288,384]{1,0:T(8,128)(2,1)S(1)} collective-permute-done((bf16[288,384]{1,0:T(8,128)(2,1)}, bf16[288,384]{1,0:T(8,128)(2,1)S(1)}, u32[]{:S(2)}, u32[]{:S(2)}) %collective-permute-start.3) | collective-permute-done | bytes 221216 | tf_op jit(solution)/shard_map/ppermute | solution.py:213
  34.3 1.3 %collective-permute-start.4 = (bf16[1152,256]{1,0:T(8,128)(2,1)S(1)}, bf16[1152,256]{1,0:T(8,128)(2,1)S(1)}, u32[]{:S(2)}, u32[]{:S(2)}) collective-permute-start(bf16[1152,256]{1,0:T(8,128)(2,1)S(1)} %pad_maximum_fusion.refs_4_), channel_id=1, source_target_pairs={{0,8},{8,16},{16,24},{24,0},{1,9},{9,17},{17,25},{25,1},{2,10},{10... | collective-permute-start | bytes 1769480 | tf_op jit(solution)/shard_map/ppermute | solution.py:223
  35.6 1.5 %collective-permute-start.6 = (bf16[1152,256]{1,0:T(8,128)(2,1)S(1)}, bf16[1152,256]{1,0:T(8,128)(2,1)S(1)}, u32[]{:S(2)}, u32[]{:S(2)}) collective-permute-start(bf16[1152,256]{1,0:T(8,128)(2,1)S(1)} %pad_maximum_fusion.refs_4_), channel_id=1, source_target_pairs={{0,24},{8,0},{16,8},{24,16},{1,25},{9,1},{17,9},{25,17},{2,26},{10... | collective-permute-start | bytes 1769480 | tf_op jit(solution)/shard_map/ppermute | solution.py:223
  37.1 4.2 %shard_map.74 = (f32[1152,128]{1,0:T(8,128)S(1)}, f32[1152,128]{1,0:T(8,128)S(1)}, f32[1152,128]{1,0:T(8,128)S(1)}) custom-call(bf16[288,384]{1,0:T(8,128)(2,1)S(1)} %collective-permute-done.refs_0_, bf16[288,384]{1,0:T(8,128)(2,1)S(1)} %collective-permute-done.1.refs_1_, bf16[288,384]{1,0:T(8,128)(2,1)S(1)} %collective-permute-done.2.refs_2_, ...), custom_call_target="tpu_custom_call" | custom-call | flops 1000 | bytes 1000 | tf_op jit(solution)/shard_map/pallas_call | solution.py:137
  41.3 8.8 %collective-permute-done.4.refs_4_ = bf16[1152,256]{1,0:T(8,128)(2,1)S(1)} collective-permute-done((bf16[1152,256]{1,0:T(8,128)(2,1)S(1)}, bf16[1152,256]{1,0:T(8,128)(2,1)S(1)}, u32[]{:S(2)}, u32[]{:S(2)}) %collective-permute-start.4) | collective-permute-done | bytes 589856 | tf_op jit(solution)/shard_map/ppermute | solution.py:223
  50.1 1.3 %collective-permute-start.10 = (bf16[1152,256]{1,0:T(8,128)(2,1)S(1)}, bf16[1152,256]{1,0:T(8,128)(2,1)S(1)}, u32[]{:S(2)}, u32[]{:S(2)}) collective-permute-start(bf16[1152,256]{1,0:T(8,128)(2,1)S(1)} %collective-permute-done.6.refs_5_), channel_id=1, source_target_pairs={{0,4},{4,0},{1,5},{5,1},{2,6},{6,2},{3,7},{7,3},{8,12},{12,8},{9,1... | collective-permute-start | bytes 1769480 | tf_op jit(solution)/shard_map/ppermute | solution.py:227
  51.4 1.3 %collective-permute-start.5 = (bf16[576,256]{1,0:T(8,128)(2,1)S(1)}, bf16[576,256]{1,0:T(8,128)(2,1)S(1)}, u32[]{:S(2)}, u32[]{:S(2)}) collective-permute-start(bf16[576,256]{1,0:T(8,128)(2,1)S(1)} %slice.28), channel_id=1, source_target_pairs={{0,8},{8,16},{16,24},{24,0},{1,9},{9,17},{17,25},{25,1},{2,10},{10... | collective-permute-start | bytes 884744 | tf_op jit(solution)/shard_map/ppermute | solution.py:223
  52.7 1.7 %collective-permute-start.7 = (bf16[576,256]{1,0:T(8,128)(2,1)S(1)}, bf16[576,256]{1,0:T(8,128)(2,1)S(1)}, u32[]{:S(2)}, u32[]{:S(2)}) collective-permute-start(bf16[576,256]{1,0:T(8,128)(2,1)S(1)} %slice.29), channel_id=1, source_target_pairs={{0,24},{8,0},{16,8},{24,16},{1,25},{9,1},{17,9},{25,17},{2,26},{10... | collective-permute-start | bytes 884744 | tf_op jit(solution)/shard_map/ppermute | solution.py:223
  54.5 9.0 %shard_map.75 = (f32[1152,128]{1,0:T(8,128)S(1)}, f32[1152,128]{1,0:T(8,128)S(1)}, f32[1152,128]{1,0:T(8,128)S(1)}) custom-call(bf16[288,384]{1,0:T(8,128)(2,1)S(1)} %collective-permute-done.refs_0_, bf16[288,384]{1,0:T(8,128)(2,1)S(1)} %collective-permute-done.1.refs_1_, bf16[288,384]{1,0:T(8,128)(2,1)S(1)} %collective-permute-done.2.refs_2_, ...), custom_call_target="tpu_custom_call" | custom-call | flops 1000 | bytes 1000 | tf_op jit(solution)/shard_map/pallas_call | solution.py:137
  63.5 1.1 %collective-permute-start.11 = (bf16[576,256]{1,0:T(8,128)(2,1)S(1)}, bf16[576,256]{1,0:T(8,128)(2,1)S(1)}, u32[]{:S(2)}, u32[]{:S(2)}) collective-permute-start(bf16[576,256]{1,0:T(8,128)(2,1)S(1)} %collective-permute-done.5.refs_4_), channel_id=1, source_target_pairs={{0,4},{4,0},{1,5},{5,1},{2,6},{6,2},{3,7},{7,3},{8,12},{12,8},{9,1... | collective-permute-start | bytes 884744 | tf_op jit(solution)/shard_map/ppermute | solution.py:227
  66.3 5.2 %shard_map.76 = (bf16[288,128]{1,0:T(8,128)(2,1)S(1)}, bf16[288,128]{1,0:T(8,128)(2,1)S(1)}, bf16[288,128]{1,0:T(8,128)(2,1)S(1)}, bf16[288,128]{1,0:T(8,128)(2,1)S(1)}) custom-call(bf16[288,384]{1,0:T(8,128)(2,1)S(1)} %collective-permute-done.refs_0_, bf16[288,384]{1,0:T(8,128)(2,1)S(1)} %collective-permute-done.1.refs_1_, ...), custom_call_target="tpu_custom_call" | custom-call | flops 1000 | bytes 1000 | tf_op jit(solution)/shard_map/pallas_call | solution.py:137
  71.5 5.2 %collective-permute-start.13 = (bf16[288,128]{1,0:T(8,128)(2,1)S(1)}, bf16[288,128]{1,0:T(8,128)(2,1)S(1)}, u32[]{:S(2)}, u32[]{:S(2)}) collective-permute-start(bf16[288,128]{1,0:T(8,128)(2,1)S(1)} %get-tuple-element.56), channel_id=1, source_target_pairs={{0,0},{128,4},{32,32},{160,36},{64,64},{192,68},{96,96},{224,100},... | collective-permute-start | bytes 221192 | tf_op jit(solution)/shard_map/ppermute | solution.py:217
  76.7 2.8 %collective-permute-start.14 = (bf16[288,128]{1,0:T(8,128)(2,1)S(1)}, bf16[288,128]{1,0:T(8,128)(2,1)S(1)}, u32[]{:S(2)}, u32[]{:S(2)}) collective-permute-start(bf16[288,128]{1,0:T(8,128)(2,1)S(1)} %get-tuple-element.57), channel_id=1, source_target_pairs={{32,0},{160,4},{64,32},{192,36},{96,64},{224,68},{0,96},{128,100},... | collective-permute-start | bytes 221192 | tf_op jit(solution)/shard_map/ppermute | solution.py:217
  79.5 2.1 %collective-permute-start.15 = (bf16[288,128]{1,0:T(8,128)(2,1)S(1)}, bf16[288,128]{1,0:T(8,128)(2,1)S(1)}, u32[]{:S(2)}, u32[]{:S(2)}) collective-permute-start(bf16[288,128]{1,0:T(8,128)(2,1)S(1)} %get-tuple-element.58), channel_id=1, source_target_pairs={{64,0},{192,4},{96,32},{224,36},{0,64},{128,68},{32,96},{160,100},... | collective-permute-start | bytes 221192 | tf_op jit(solution)/shard_map/ppermute | solution.py:217
  81.6 3.2 %collective-permute-start.16 = (bf16[288,128]{1,0:T(8,128)(2,1)S(1)}, bf16[288,128]{1,0:T(8,128)(2,1)S(1)}, u32[]{:S(2)}, u32[]{:S(2)}) collective-permute-start(bf16[288,128]{1,0:T(8,128)(2,1)S(1)} %get-tuple-element.59), channel_id=1, source_target_pairs={{96,0},{224,4},{0,32},{128,36},{32,64},{160,68},{64,96},{192,100},... | collective-permute-start | bytes 221192 | tf_op jit(solution)/shard_map/ppermute | solution.py:217
  84.8 1.5 %collective-permute-done.15 = bf16[288,128]{1,0:T(8,128)(2,1)S(1)} collective-permute-done((bf16[288,128]{1,0:T(8,128)(2,1)S(1)}, bf16[288,128]{1,0:T(8,128)(2,1)S(1)}, u32[]{:S(2)}, u32[]{:S(2)}) %collective-permute-start.15) | collective-permute-done | bytes 73760 | tf_op jit(solution)/shard_map/ppermute | solution.py:217
  86.3 2.5 %collective-permute-done.16 = bf16[288,128]{1,0:T(8,128)(2,1)S(1)} collective-permute-done((bf16[288,128]{1,0:T(8,128)(2,1)S(1)}, bf16[288,128]{1,0:T(8,128)(2,1)S(1)}, u32[]{:S(2)}, u32[]{:S(2)}) %collective-permute-start.16) | collective-permute-done | bytes 73760 | tf_op jit(solution)/shard_map/ppermute | solution.py:217
  88.8 1.1 %collective-permute-start.18 = (bf16[288,512]{1,0:T(8,128)(2,1)S(1)}, bf16[288,512]{1,0:T(8,128)(2,1)S(1)}, u32[]{:S(2)}, u32[]{:S(2)}) collective-permute-start(bf16[288,512]{1,0:T(8,128)(2,1)S(1)} %constant_dynamic-update-slice_fusion.refs_0_), channel_id=1, source_target_pairs={{0,1},{1,2},{2,3},{3,0},{4,5},{5,6},{6,7},{7,4},{8,9},{9,10},{10,1... | collective-permute-start | bytes 884744 | tf_op jit(solution)/shard_map/ppermute | solution.py:223
  89.9 1.8 %collective-permute-start.19 = (bf16[288,512]{1,0:T(8,128)(2,1)S(1)}, bf16[288,512]{1,0:T(8,128)(2,1)S(1)}, u32[]{:S(2)}, u32[]{:S(2)}) collective-permute-start(bf16[288,512]{1,0:T(8,128)(2,1)S(1)} %constant_dynamic-update-slice_fusion.refs_0_), channel_id=1, source_target_pairs={{0,3},{1,0},{2,1},{3,2},{4,7},{5,4},{6,5},{7,6},{8,11},{9,8},{10,9... | collective-permute-start | bytes 884744 | tf_op jit(solution)/shard_map/ppermute | solution.py:223
  91.7 1.3 %collective-permute-start.17 = (bf16[288,512]{1,0:T(8,128)(2,1)S(1)}, bf16[288,512]{1,0:T(8,128)(2,1)S(1)}, u32[]{:S(2)}, u32[]{:S(2)}) collective-permute-start(bf16[288,512]{1,0:T(8,128)(2,1)S(1)} %constant_dynamic-update-slice_fusion.refs_0_), channel_id=1, source_target_pairs={{0,2},{1,3},{2,0},{3,1},{4,6},{5,7},{6,4},{7,5},{8,10},{9,11},{10,... | collective-permute-start | bytes 884744 | tf_op jit(solution)/shard_map/ppermute | solution.py:223
  93.0 1.4 %shard_map.77.refs_2_ = f32[288,1536]{1,0:T(8,128)S(1)} custom-call(s32[3]{0:T(128)S(1)} %copy-done, bf16[2048,1536]{1,0:T(8,128)(2,1)S(1)} %bitcast.6, bf16[288,512]{1,0:T(8,128)(2,1)S(1)} %constant_dynamic-update-slice_fusion.refs_0_), custom_call_target="tpu_custom_call" | custom-call | tf_op jit(solution)/shard_map/pallas_call | solution.py:190
  94.4 4.4 %collective-permute-done.18.refs_0_ = bf16[288,512]{1,0:T(8,128)(2,1)S(1)} collective-permute-done((bf16[288,512]{1,0:T(8,128)(2,1)S(1)}, bf16[288,512]{1,0:T(8,128)(2,1)S(1)}, u32[]{:S(2)}, u32[]{:S(2)}) %collective-permute-start.18) | collective-permute-done | bytes 294944 | tf_op jit(solution)/shard_map/ppermute | solution.py:223
  98.8 1.8 %collective-permute-done.19.refs_1_ = bf16[288,512]{1,0:T(8,128)(2,1)S(1)} collective-permute-done((bf16[288,512]{1,0:T(8,128)(2,1)S(1)}, bf16[288,512]{1,0:T(8,128)(2,1)S(1)}, u32[]{:S(2)}, u32[]{:S(2)}) %collective-permute-start.19) | collective-permute-done | bytes 294944 | tf_op jit(solution)/shard_map/ppermute | solution.py:223
  100.7 2.0 %shard_map.78.refs_1_ = f32[288,1536]{1,0:T(8,128)S(1)} custom-call(s32[3]{0:T(128)S(1)} %copy-done, bf16[2048,1536]{1,0:T(8,128)(2,1)S(1)} %bitcast.6, bf16[288,512]{1,0:T(8,128)(2,1)S(1)} %collective-permute-done.18.refs_0_, bf16[288,512]{1,0:T(8,128)(2,1)S(1)} %collective-permute-done.19.refs_1_, f32[288,1536]{1,0:T(8,128)S(1)} %shard_map.77.refs_2_), custom_call_target="tpu_custom_call" | custom-call | tf_op jit(solution)/shard_map/pallas_call | solution.py:190
  102.7 1.4 %shard_map.79 = (f32[144,1536]{1,0:T(8,128)S(1)}, bf16[144,1536]{1,0:T(8,128)(2,1)S(1)}) custom-call(s32[3]{0:T(128)S(1)} %copy-done, bf16[2048,1536]{1,0:T(8,128)(2,1)S(1)} %bitcast.6, bf16[288,512]{1,0:T(8,128)(2,1)S(1)} %collective-permute-done.17.refs_0_, f32[288,1536]{1,0:T(8,128)S(1)} %shard_map.78.refs_1_), custom_call_target="tpu_custom_call" | custom-call | tf_op jit(solution)/shard_map/pallas_call | solution.py:190
  104.2 1.8 %collective-permute-done.20 = bf16[144,1536]{1,0:T(8,128)(2,1)S(1)} collective-permute-done((bf16[144,1536]{1,0:T(8,128)(2,1)S(1)}, bf16[144,1536]{1,0:T(8,128)(2,1)S(1)}, u32[]{:S(2)}, u32[]{:S(2)}) %collective-permute-start.20) | collective-permute-done | bytes 442400 | tf_op jit(solution)/shard_map/ppermute | solution.py:227
  (39 shorter events, 3.7 us)
Async XLA Ops:
  4.1 18.4 %collective-permute-start = (bf16[288,384]{1,0:T(8,128)(2,1)}, bf16[288,384]{1,0:T(8,128)(2,1)S(1)}, u32[]{:S(2)}, u32[]{:S(2)}) collective-permute-start(bf16[288,384]{1,0:T(8,128)(2,1)} %get-tuple-element.36), channel_id=1, source_target_pairs={{0,0},{4,128},{32,32},{36,160},{64,64},{68,192},{96,96},{100,224},... | collective-permute-start | bytes 663560 | tf_op jit(solution)/shard_map/ppermute | solution.py:213
  14.3 11.9 %collective-permute-start.1 = (bf16[288,384]{1,0:T(8,128)(2,1)}, bf16[288,384]{1,0:T(8,128)(2,1)S(1)}, u32[]{:S(2)}, u32[]{:S(2)}) collective-permute-start(bf16[288,384]{1,0:T(8,128)(2,1)} %get-tuple-element.37), channel_id=1, source_target_pairs={{0,32},{4,160},{32,64},{36,192},{64,96},{68,224},{96,0},{100,128},... | collective-permute-start | bytes 663560 | tf_op jit(solution)/shard_map/ppermute | solution.py:213
  14.4 14.4 %collective-permute-start.2 = (bf16[288,384]{1,0:T(8,128)(2,1)}, bf16[288,384]{1,0:T(8,128)(2,1)S(1)}, u32[]{:S(2)}, u32[]{:S(2)}) collective-permute-start(bf16[288,384]{1,0:T(8,128)(2,1)} %get-tuple-element.38), channel_id=1, source_target_pairs={{0,64},{4,192},{32,96},{36,224},{64,0},{68,128},{96,32},{100,160},... | collective-permute-start | bytes 663560 | tf_op jit(solution)/shard_map/ppermute | solution.py:213
  18.7 15.5 %collective-permute-start.3 = (bf16[288,384]{1,0:T(8,128)(2,1)}, bf16[288,384]{1,0:T(8,128)(2,1)S(1)}, u32[]{:S(2)}, u32[]{:S(2)}) collective-permute-start(bf16[288,384]{1,0:T(8,128)(2,1)} %get-tuple-element.39), channel_id=1, source_target_pairs={{0,96},{4,224},{32,0},{36,128},{64,32},{68,160},{96,64},{100,192},... | collective-permute-start | bytes 663560 | tf_op jit(solution)/shard_map/ppermute | solution.py:213
  34.2 2.9 %collective-permute-start.8 = (bf16[1152,256]{1,0:T(8,128)(2,1)S(1)}, bf16[1152,256]{1,0:T(8,128)(2,1)S(1)}, u32[]{:S(2)}, u32[]{:S(2)}) collective-permute-start(bf16[1152,256]{1,0:T(8,128)(2,1)S(1)} %pad_maximum_fusion.refs_4_), channel_id=1, source_target_pairs={{0,4},{4,0},{1,5},{5,1},{2,6},{6,2},{3,7},{7,3},{8,12},{12,8},{9,1... | collective-permute-start | bytes 1769480 | tf_op jit(solution)/shard_map/ppermute | solution.py:227
  34.3 15.8 %collective-permute-start.4 = (bf16[1152,256]{1,0:T(8,128)(2,1)S(1)}, bf16[1152,256]{1,0:T(8,128)(2,1)S(1)}, u32[]{:S(2)}, u32[]{:S(2)}) collective-permute-start(bf16[1152,256]{1,0:T(8,128)(2,1)S(1)} %pad_maximum_fusion.refs_4_), channel_id=1, source_target_pairs={{0,8},{8,16},{16,24},{24,0},{1,9},{9,17},{17,25},{25,1},{2,10},{10... | collective-permute-start | bytes 1769480 | tf_op jit(solution)/shard_map/ppermute | solution.py:223
  35.6 14.5 %collective-permute-start.6 = (bf16[1152,256]{1,0:T(8,128)(2,1)S(1)}, bf16[1152,256]{1,0:T(8,128)(2,1)S(1)}, u32[]{:S(2)}, u32[]{:S(2)}) collective-permute-start(bf16[1152,256]{1,0:T(8,128)(2,1)S(1)} %pad_maximum_fusion.refs_4_), channel_id=1, source_target_pairs={{0,24},{8,0},{16,8},{24,16},{1,25},{9,1},{17,9},{25,17},{2,26},{10... | collective-permute-start | bytes 1769480 | tf_op jit(solution)/shard_map/ppermute | solution.py:223
  37.1 55.9 %slice-start = ((s8[6291456]{0:T(1024)(128)(4,1)}), s8[4194304]{0:T(1024)(128)(4,1)S(1)}, s32[]{:S(2)}) async-start(s8[6291456]{0:T(1024)(128)(4,1)} %bitcast.5), calls=%async_computation | async-start | bytes 8388608
  50.1 4.4 %collective-permute-start.10 = (bf16[1152,256]{1,0:T(8,128)(2,1)S(1)}, bf16[1152,256]{1,0:T(8,128)(2,1)S(1)}, u32[]{:S(2)}, u32[]{:S(2)}) collective-permute-start(bf16[1152,256]{1,0:T(8,128)(2,1)S(1)} %collective-permute-done.6.refs_5_), channel_id=1, source_target_pairs={{0,4},{4,0},{1,5},{5,1},{2,6},{6,2},{3,7},{7,3},{8,12},{12,8},{9,1... | collective-permute-start | bytes 1769480 | tf_op jit(solution)/shard_map/ppermute | solution.py:227
  51.4 3.1 %collective-permute-start.9 = (bf16[1152,256]{1,0:T(8,128)(2,1)S(1)}, bf16[1152,256]{1,0:T(8,128)(2,1)S(1)}, u32[]{:S(2)}, u32[]{:S(2)}) collective-permute-start(bf16[1152,256]{1,0:T(8,128)(2,1)S(1)} %collective-permute-done.4.refs_4_), channel_id=1, source_target_pairs={{0,4},{4,0},{1,5},{5,1},{2,6},{6,2},{3,7},{7,3},{8,12},{12,8},{9,1... | collective-permute-start | bytes 1769480 | tf_op jit(solution)/shard_map/ppermute | solution.py:227
  51.4 12.1 %collective-permute-start.5 = (bf16[576,256]{1,0:T(8,128)(2,1)S(1)}, bf16[576,256]{1,0:T(8,128)(2,1)S(1)}, u32[]{:S(2)}, u32[]{:S(2)}) collective-permute-start(bf16[576,256]{1,0:T(8,128)(2,1)S(1)} %slice.28), channel_id=1, source_target_pairs={{0,8},{8,16},{16,24},{24,0},{1,9},{9,17},{17,25},{25,1},{2,10},{10... | collective-permute-start | bytes 884744 | tf_op jit(solution)/shard_map/ppermute | solution.py:223
  52.7 40.3 %slice-start.1 = ((s8[6291456]{0:T(1024)(128)(4,1)}), s8[2097152]{0:T(1024)(128)(4,1)S(1)}, s32[]{:S(2)}) async-start(s8[6291456]{0:T(1024)(128)(4,1)} %bitcast.5), calls=%async_computation.1 | async-start | bytes 4194304
  52.7 10.8 %collective-permute-start.7 = (bf16[576,256]{1,0:T(8,128)(2,1)S(1)}, bf16[576,256]{1,0:T(8,128)(2,1)S(1)}, u32[]{:S(2)}, u32[]{:S(2)}) collective-permute-start(bf16[576,256]{1,0:T(8,128)(2,1)S(1)} %slice.29), channel_id=1, source_target_pairs={{0,24},{8,0},{16,8},{24,16},{1,25},{9,1},{17,9},{25,17},{2,26},{10... | collective-permute-start | bytes 884744 | tf_op jit(solution)/shard_map/ppermute | solution.py:223
  63.5 29.5 %copy-start = (s32[3]{0:T(128)S(1)}, s32[3]{0:T(128)}, u32[]{:S(2)}) copy-start(s32[3]{0:T(128)} %pad_add_fusion.pos_ref) | copy-start | bytes 40
  63.5 2.4 %collective-permute-start.11 = (bf16[576,256]{1,0:T(8,128)(2,1)S(1)}, bf16[576,256]{1,0:T(8,128)(2,1)S(1)}, u32[]{:S(2)}, u32[]{:S(2)}) collective-permute-start(bf16[576,256]{1,0:T(8,128)(2,1)S(1)} %collective-permute-done.5.refs_4_), channel_id=1, source_target_pairs={{0,4},{4,0},{1,5},{5,1},{2,6},{6,2},{3,7},{7,3},{8,12},{12,8},{9,1... | collective-permute-start | bytes 884744 | tf_op jit(solution)/shard_map/ppermute | solution.py:227
  64.7 1.6 %collective-permute-start.12 = (bf16[576,256]{1,0:T(8,128)(2,1)S(1)}, bf16[576,256]{1,0:T(8,128)(2,1)S(1)}, u32[]{:S(2)}, u32[]{:S(2)}) collective-permute-start(bf16[576,256]{1,0:T(8,128)(2,1)S(1)} %collective-permute-done.7.refs_5_), channel_id=1, source_target_pairs={{0,4},{4,0},{1,5},{5,1},{2,6},{6,2},{3,7},{7,3},{8,12},{12,8},{9,1... | collective-permute-start | bytes 884744 | tf_op jit(solution)/shard_map/ppermute | solution.py:227
  71.5 13.2 %collective-permute-start.13 = (bf16[288,128]{1,0:T(8,128)(2,1)S(1)}, bf16[288,128]{1,0:T(8,128)(2,1)S(1)}, u32[]{:S(2)}, u32[]{:S(2)}) collective-permute-start(bf16[288,128]{1,0:T(8,128)(2,1)S(1)} %get-tuple-element.56), channel_id=1, source_target_pairs={{0,0},{128,4},{32,32},{160,36},{64,64},{192,68},{96,96},{224,100},... | collective-permute-start | bytes 221192 | tf_op jit(solution)/shard_map/ppermute | solution.py:217
  76.7 8.0 %collective-permute-start.14 = (bf16[288,128]{1,0:T(8,128)(2,1)S(1)}, bf16[288,128]{1,0:T(8,128)(2,1)S(1)}, u32[]{:S(2)}, u32[]{:S(2)}) collective-permute-start(bf16[288,128]{1,0:T(8,128)(2,1)S(1)} %get-tuple-element.57), channel_id=1, source_target_pairs={{32,0},{160,4},{64,32},{192,36},{96,64},{224,68},{0,96},{128,100},... | collective-permute-start | bytes 221192 | tf_op jit(solution)/shard_map/ppermute | solution.py:217
  79.5 6.8 %collective-permute-start.15 = (bf16[288,128]{1,0:T(8,128)(2,1)S(1)}, bf16[288,128]{1,0:T(8,128)(2,1)S(1)}, u32[]{:S(2)}, u32[]{:S(2)}) collective-permute-start(bf16[288,128]{1,0:T(8,128)(2,1)S(1)} %get-tuple-element.58), channel_id=1, source_target_pairs={{64,0},{192,4},{96,32},{224,36},{0,64},{128,68},{32,96},{160,100},... | collective-permute-start | bytes 221192 | tf_op jit(solution)/shard_map/ppermute | solution.py:217
  81.6 7.3 %collective-permute-start.16 = (bf16[288,128]{1,0:T(8,128)(2,1)S(1)}, bf16[288,128]{1,0:T(8,128)(2,1)S(1)}, u32[]{:S(2)}, u32[]{:S(2)}) collective-permute-start(bf16[288,128]{1,0:T(8,128)(2,1)S(1)} %get-tuple-element.59), channel_id=1, source_target_pairs={{96,0},{224,4},{0,32},{128,36},{32,64},{160,68},{64,96},{192,100},... | collective-permute-start | bytes 221192 | tf_op jit(solution)/shard_map/ppermute | solution.py:217
  88.8 10.0 %collective-permute-start.18 = (bf16[288,512]{1,0:T(8,128)(2,1)S(1)}, bf16[288,512]{1,0:T(8,128)(2,1)S(1)}, u32[]{:S(2)}, u32[]{:S(2)}) collective-permute-start(bf16[288,512]{1,0:T(8,128)(2,1)S(1)} %constant_dynamic-update-slice_fusion.refs_0_), channel_id=1, source_target_pairs={{0,1},{1,2},{2,3},{3,0},{4,5},{5,6},{6,7},{7,4},{8,9},{9,10},{10,1... | collective-permute-start | bytes 884744 | tf_op jit(solution)/shard_map/ppermute | solution.py:223
  89.9 10.7 %collective-permute-start.19 = (bf16[288,512]{1,0:T(8,128)(2,1)S(1)}, bf16[288,512]{1,0:T(8,128)(2,1)S(1)}, u32[]{:S(2)}, u32[]{:S(2)}) collective-permute-start(bf16[288,512]{1,0:T(8,128)(2,1)S(1)} %constant_dynamic-update-slice_fusion.refs_0_), channel_id=1, source_target_pairs={{0,3},{1,0},{2,1},{3,2},{4,7},{5,4},{6,5},{7,6},{8,11},{9,8},{10,9... | collective-permute-start | bytes 884744 | tf_op jit(solution)/shard_map/ppermute | solution.py:223
  91.7 11.0 %collective-permute-start.17 = (bf16[288,512]{1,0:T(8,128)(2,1)S(1)}, bf16[288,512]{1,0:T(8,128)(2,1)S(1)}, u32[]{:S(2)}, u32[]{:S(2)}) collective-permute-start(bf16[288,512]{1,0:T(8,128)(2,1)S(1)} %constant_dynamic-update-slice_fusion.refs_0_), channel_id=1, source_target_pairs={{0,2},{1,3},{2,0},{3,1},{4,6},{5,7},{6,4},{7,5},{8,10},{9,11},{10,... | collective-permute-start | bytes 884744 | tf_op jit(solution)/shard_map/ppermute | solution.py:223
  102.7 3.3 %copy-start.1 = (bf16[144,1536]{1,0:T(8,128)(2,1)S(1)}, bf16[144,1536]{1,0:T(8,128)(2,1)}, u32[]{:S(2)}) copy-start(bf16[144,1536]{1,0:T(8,128)(2,1)} %param.12) | copy-start | bytes 1327108
  104.1 1.9 %collective-permute-start.20 = (bf16[144,1536]{1,0:T(8,128)(2,1)S(1)}, bf16[144,1536]{1,0:T(8,128)(2,1)S(1)}, u32[]{:S(2)}, u32[]{:S(2)}) collective-permute-start(bf16[144,1536]{1,0:T(8,128)(2,1)S(1)} %get-tuple-element.66), channel_id=1, source_target_pairs={{0,4},{4,0},{1,5},{5,1},{2,6},{6,2},{3,7},{7,3},{8,12},{12,8},{9,1... | collective-permute-start | bytes 1327112 | tf_op jit(solution)/shard_map/ppermute | solution.py:227

commit v4 on v3

--- a/solution.py
+++ b/solution.py
@@ -16,6 +16,7 @@
 ROWS = 288
 HALF = ROWS // 2
 HEADS = 4
+SENDS = (3, 1, 2, 0)
 NT = (((1,), (1,)), ((), ()))
 VM = pl.BlockSpec(memory_space=pltpu.VMEM)
 SM = pl.BlockSpec(memory_space=pltpu.MemorySpace.SMEM)
@@ -38,7 +39,7 @@
     for c in copies:
         c.start()
     k_ref, kg_ref, v_ref, q_ref, qg_ref = held
-    heads = [lax.rem(pos_ref[0] + j, HEADS) for j in range(HEADS)]
+    heads = [lax.rem(pos_ref[0] + j, HEADS) for j in SENDS]
     columns = [pl.ds(pl.multiple_of(h * DH, DH), DH) for h in heads]
     copies[0].wait()
     copies[1].wait()
@@ -66,50 +67,46 @@
     )(pos, *arrays)
 
 
-def flash_kernel(first, last, nkv, kb, *refs):
-    queries, refs = refs[:HEADS], refs[HEADS:]
+def flash_kernel(first, last, nq, nkv, most, *refs):
+    queries, refs = refs[:nq], refs[nq:]
     pieces, refs = refs[:nkv], refs[nkv:]
     if not first:
         (acc_in, max_in, sum_in), refs = refs[:3], refs[3:]
-    if last:
-        outs, refs = refs[:HEADS], refs[HEADS:]
-    else:
-        outs, refs = refs[:3], refs[3:]
-    kv, sem = refs
-    piece = pieces[0].shape[0]
-    copies = [
-        pltpu.make_async_copy(pieces[i], kv.at[pl.ds(i * piece, piece)], sem.at[i])
-        for i in range(nkv)
-    ]
-    for c in copies:
-        c.start()
-    for c in copies:
-        c.wait()
-    blocks = kv.shape[0] // kb
-    for i in range(HEADS):
+    outs = refs
+    blocks, size = [[]], 0
+    for p in pieces:
+        if size + p.shape[0] > most and blocks[-1]:
+            blocks.append([])
+            size = 0
+        blocks[-1].append(p)
+        size += p.shape[0]
+    for i in range(nq):
         rows = slice(i * ROWS, (i + 1) * ROWS)
         q = queries[i][:, 2 * DH :]
 
-        def scores(b):
-            return lax.dot_general(
-                q, kv[b * kb : (b + 1) * kb, :DH], NT, preferred_element_type=F32
-            )
+        def scores(block):
+            parts = [
+                lax.dot_general(q, p[:, :DH], NT, preferred_element_type=F32) for p in block
+            ]
+            return jnp.concatenate(parts, axis=1)
 
         if first:
             high = None
         else:
             high, total, acc = max_in[rows, :1], sum_in[rows, :1], acc_in[rows, :]
-        ahead = scores(0)
-        for b in range(blocks):
+        ahead = scores(blocks[0])
+        for b, block in enumerate(blocks):
             s = ahead
-            if b + 1 < blocks:
-                ahead = scores(b + 1)
+            if b + 1 < len(blocks):
+                ahead = scores(blocks[b + 1])
             top = jnp.max(s, axis=1, keepdims=True)
             top = top if high is None else jnp.maximum(high, top)
-            p = jnp.exp(s - top).astype(BF)
-            v = kv[b * kb : (b + 1) * kb, DH:]
+            weights = jnp.exp(s - top).astype(BF)
+            values = jnp.concatenate([p[:, DH : 2 * DH] for p in block], axis=0)
             both = jnp.dot(
-                p, jnp.concatenate([v, jnp.ones_like(v)], axis=1), preferred_element_type=F32
+                weights,
+                jnp.concatenate([values, jnp.ones_like(values)], axis=1),
+                preferred_element_type=F32,
             )
             part, psum = both[:, :DH], both[:, DH : DH + 1]
             if high is None:
@@ -126,20 +123,17 @@
             outs[2][rows, :] = jnp.broadcast_to(total, (ROWS, DH))
 
 
-def flash(first, last, queries, pieces, state):
-    n = len(pieces)
-    keys = n * pieces[0].shape[0]
-    nq = HEADS * ROWS
+def flash(last, queries, pieces, state=(), most=2304):
+    n, nq = len(pieces), len(queries)
     if last:
-        shapes = [jax.ShapeDtypeStruct((ROWS, DH), BF)] * HEADS
+        shapes = [jax.ShapeDtypeStruct((ROWS, DH), BF)] * nq
     else:
-        shapes = [jax.ShapeDtypeStruct((nq, DH), F32)] * 3
+        shapes = [jax.ShapeDtypeStruct((nq * ROWS, DH), F32)] * 3
     return pl.pallas_call(
-        functools.partial(flash_kernel, first, last, n, 1152),
+        functools.partial(flash_kernel, not state, last, nq, n, most),
         out_shape=shapes,
-        in_specs=[VM] * HEADS + [ANY] * n + [VM] * len(state),
+        in_specs=[VM] * (nq + n + len(state)),
         out_specs=[VM] * len(shapes),
-        scratch_shapes=[pltpu.VMEM((keys, 2 * DH), BF), pltpu.SemaphoreType.DMA((n,))],
         compiler_params=pltpu.CompilerParams(vmem_limit_bytes=VLIM),
         cost_estimate=pl.CostEstimate(flops=1000, bytes_accessed=1000, transcendentals=0),
     )(*queries, *pieces, *state)
@@ -162,7 +156,7 @@
         c.start()
     for k in range(n):
         for j in range(HEADS):
-            head = lax.rem(turn + j, HEADS)
+            head = lax.rem(turn + SENDS[j], HEADS)
             cols = pl.ds(pl.multiple_of(head * DH, DH), DH)
             for i in range(2):
                 rows = pl.ds(pl.multiple_of(lax.rem(core + i, 2) * HALF, 16), HALF)
@@ -203,7 +197,7 @@
 
 def owner_pairs(j):
     return [
-        (z * NC + c, (HEADS * c + (z + j) % HEADS) * NC + z // HEADS)
+        (z * NC + c, (HEADS * c + (z + SENDS[j]) % HEADS) * NC + z // HEADS)
         for z in range(NZ)
         for c in range(NC)
     ]
@@ -235,13 +229,13 @@
     held = [to_owner(ready[j], j) for j in range(HEADS)]
     own = jnp.concatenate([m[:, : 2 * DH] for m in held], axis=0)
     near, back = shift(own, "x", NX, 1), shift(own, "x", NX, -1)
-    state = flash(True, False, held, [own, swap(own)], ())
+    state = flash(False, held, [own])
     half = own.shape[0] // 2
     far = [shift(near[:half], "x", NX, 1), shift(back[half:], "x", NX, -1)]
     near, back, *state = lax.optimization_barrier((near, back, *state))
-    state = flash(False, False, held, [near, back, swap(near), swap(back)], state)
+    state = flash(False, held, [swap(own), near, back, swap(near), swap(back)], state)
     *far, a, b, c = lax.optimization_barrier((*far, *state))
-    attended = flash(False, True, held, far + [swap(p) for p in far], (a, b, c))
+    attended = flash(True, held, far + [swap(p) for p in far], (a, b, c))
     mine = jnp.concatenate([from_owner(attended[j], j) for j in range(HEADS)], axis=1)
     far, near, back = [shift(mine, "col", NY, s) for s in (2, 1, 3)]
     total = project((0,), False, pos, out_weight, [mine])

time: 107 us -> 99.2 us (0.927)
  waiting for transfers between devices: 37.6 us -> 32.6 us
  Pallas kernels: 26.7 us -> 24.5 us
    ppermute x4, waiting for transfers between devices: 15.4 us -> 11.8 us  [to_owner(): return lax.ppermute(value, ('z', 'row'), owner_pairs(j))]
    pallas_call x3, Pallas kernels: 18.4 us -> 16.3 us  [flash(): pl.pallas_call(functools.partial(flash_kernel, not state, last, nq, n, mo...]
    ppermute x6, starting transfers between devices: 2.92 us -> 1.56 us  [swap(): return lax.ppermute(value, 'row', [(0, 1), (1, 0)])]
  transfers between devices with their start and end apart: 21 -> 21, of which waited for: 12 -> 10; matrix products, arithmetic and copies ran while one was open for 0% -> 0% of each run, Pallas kernels for 16% -> 14%
where the time goes in v4:
time: 99.2 us; the launch traced here: 98.8 us
  starting transfers between devices  39.7 us (40%)
  waiting for transfers between devices  32.6 us (33%)
  Pallas kernels  24.5 us (25%)
  other arithmetic  1.57 us (2%)
    pallas_call x3, Pallas kernels, flash(): pl.pallas_call(functools.partial(flash_kernel, not state, last, nq, n, mo...  16.3 us
    ppermute x4, starting transfers between devices, to_owner(): return lax.ppermute(value, ('z', 'row'), owner_pairs(j))  15 us
    ppermute x7, waiting for transfers between devices, shift(): lax.ppermute(value, axis, [(i, (i + step) % size) for i in range(size)])  14.4 us
    ppermute x4, starting transfers between devices, from_owner(): lax.ppermute(value, ('z', 'row'), [(b, a) for a, b in owner_pairs(j)])  12.9 us
    ppermute x4, waiting for transfers between devices, to_owner(): return lax.ppermute(value, ('z', 'row'), owner_pairs(j))  11.8 us
    ppermute x7, starting transfers between devices, shift(): lax.ppermute(value, axis, [(i, (i + step) % size) for i in range(size)])  10.2 us
    pallas_call x3, Pallas kernels, project(): pl.pallas_call(functools.partial(project_kernel, steps, not total, last),...  4.8 us
    pallas_call x1, Pallas kernels, norms(): pl.pallas_call(norm_kernel, out_shape=[jax.ShapeDtypeStruct((ROWS, 3 * DH...  3.48 us
  transfers between devices with their start and end apart: 21, of which 10 were waited for; matrix products, arithmetic and copies ran while one was open for 0% of the time, Pallas kernels for 14%

profile of v4, /device:TPU:1, one launch (start us, length us, event | category | flops | bytes accessed | tf_op | source)
XLA Modules:
  0.0 98.8 jit_solution(17813858088416963079)
XLA Ops:
  0.0 0.6 pad_add_fusion.pos_ref
  0.6 3.5 %shard_map.73 = (bf16[288,384]{1,0:T(8,128)(2,1)}, bf16[288,384]{1,0:T(8,128)(2,1)}, bf16[288,384]{1,0:T(8,128)(2,1)}, bf16[288,384]{1,0:T(8,128)(2,1)}) custom-call(s32[3]{0:T(128)} %pad_add_fusion.pos_ref, bf16[288,512]{1,0:T(8,128)(2,1)} %refs_0_.1, f32[1,512]{1,0:T(1,128)} %bitcast.7, bf16[288,512]{1,0:T(8,128)(2,1)} %refs_2_.1, ...), custom_call_target="tpu_custom_call" | custom-call | tf_op jit(solution)/shard_map/pallas_call | solution.py:59
  4.1 7.0 %collective-permute-start = (bf16[288,384]{1,0:T(8,128)(2,1)}, bf16[288,384]{1,0:T(8,128)(2,1)S(1)}, u32[]{:S(2)}, u32[]{:S(2)}) collective-permute-start(bf16[288,384]{1,0:T(8,128)(2,1)} %get-tuple-element.36), channel_id=1, source_target_pairs={{0,96},{4,224},{32,0},{36,128},{64,32},{68,160},{96,64},{100,192},... | collective-permute-start | bytes 663560 | tf_op jit(solution)/shard_map/ppermute | solution.py:207
  11.1 1.0 collective-permute-start.1
  12.1 4.2 %collective-permute-start.2 = (bf16[288,384]{1,0:T(8,128)(2,1)}, bf16[288,384]{1,0:T(8,128)(2,1)S(1)}, u32[]{:S(2)}, u32[]{:S(2)}) collective-permute-start(bf16[288,384]{1,0:T(8,128)(2,1)} %get-tuple-element.38), channel_id=1, source_target_pairs={{0,64},{4,192},{32,96},{36,224},{64,0},{68,128},{96,32},{100,160},... | collective-permute-start | bytes 663560 | tf_op jit(solution)/shard_map/ppermute | solution.py:207
  16.3 2.8 %collective-permute-start.3 = (bf16[288,384]{1,0:T(8,128)(2,1)}, bf16[288,384]{1,0:T(8,128)(2,1)S(1)}, u32[]{:S(2)}, u32[]{:S(2)}) collective-permute-start(bf16[288,384]{1,0:T(8,128)(2,1)} %get-tuple-element.39), channel_id=1, source_target_pairs={{0,0},{4,128},{32,32},{36,160},{64,64},{68,192},{96,96},{100,224},... | collective-permute-start | bytes 663560 | tf_op jit(solution)/shard_map/ppermute | solution.py:207
  19.1 3.3 %collective-permute-done.refs_0_ = bf16[288,384]{1,0:T(8,128)(2,1)S(1)} collective-permute-done((bf16[288,384]{1,0:T(8,128)(2,1)}, bf16[288,384]{1,0:T(8,128)(2,1)S(1)}, u32[]{:S(2)}, u32[]{:S(2)}) %collective-permute-start) | collective-permute-done | bytes 221216 | tf_op jit(solution)/shard_map/ppermute | solution.py:207
  22.5 8.5 %collective-permute-done.2.refs_2_ = bf16[288,384]{1,0:T(8,128)(2,1)S(1)} collective-permute-done((bf16[288,384]{1,0:T(8,128)(2,1)}, bf16[288,384]{1,0:T(8,128)(2,1)S(1)}, u32[]{:S(2)}, u32[]{:S(2)}) %collective-permute-start.2) | collective-permute-done | bytes 221216 | tf_op jit(solution)/shard_map/ppermute | solution.py:207
  31.1 1.3 %collective-permute-start.4 = (bf16[1152,256]{1,0:T(8,128)(2,1)S(1)}, bf16[1152,256]{1,0:T(8,128)(2,1)S(1)}, u32[]{:S(2)}, u32[]{:S(2)}) collective-permute-start(bf16[1152,256]{1,0:T(8,128)(2,1)S(1)} %pad_maximum_fusion.refs_4_), channel_id=1, source_target_pairs={{0,8},{8,16},{16,24},{24,0},{1,9},{9,17},{17,25},{25,1},{2,10},{10... | collective-permute-start | bytes 1769480 | tf_op jit(solution)/shard_map/ppermute | solution.py:217
  32.4 1.5 %collective-permute-start.6 = (bf16[1152,256]{1,0:T(8,128)(2,1)S(1)}, bf16[1152,256]{1,0:T(8,128)(2,1)S(1)}, u32[]{:S(2)}, u32[]{:S(2)}) collective-permute-start(bf16[1152,256]{1,0:T(8,128)(2,1)S(1)} %pad_maximum_fusion.refs_4_), channel_id=1, source_target_pairs={{0,24},{8,0},{16,8},{24,16},{1,25},{9,1},{17,9},{25,17},{2,26},{10... | collective-permute-start | bytes 1769480 | tf_op jit(solution)/shard_map/ppermute | solution.py:217
  33.9 2.2 %shard_map.74 = (f32[1152,128]{1,0:T(8,128)S(1)}, f32[1152,128]{1,0:T(8,128)S(1)}, f32[1152,128]{1,0:T(8,128)S(1)}) custom-call(bf16[288,384]{1,0:T(8,128)(2,1)S(1)} %collective-permute-done.refs_0_, bf16[288,384]{1,0:T(8,128)(2,1)S(1)} %collective-permute-done.1.refs_1_, bf16[288,384]{1,0:T(8,128)(2,1)S(1)} %collective-permute-done.2.refs_2_, ...), custom_call_target="tpu_custom_call" | custom-call | flops 1000 | bytes 1000 | tf_op jit(solution)/shard_map/pallas_call | solution.py:132
  36.1 9.9 %collective-permute-done.4.refs_5_ = bf16[1152,256]{1,0:T(8,128)(2,1)S(1)} collective-permute-done((bf16[1152,256]{1,0:T(8,128)(2,1)S(1)}, bf16[1152,256]{1,0:T(8,128)(2,1)S(1)}, u32[]{:S(2)}, u32[]{:S(2)}) %collective-permute-start.4) | collective-permute-done | bytes 589856 | tf_op jit(solution)/shard_map/ppermute | solution.py:217
  46.8 1.3 %collective-permute-start.5 = (bf16[576,256]{1,0:T(8,128)(2,1)S(1)}, bf16[576,256]{1,0:T(8,128)(2,1)S(1)}, u32[]{:S(2)}, u32[]{:S(2)}) collective-permute-start(bf16[576,256]{1,0:T(8,128)(2,1)S(1)} %slice.28), channel_id=1, source_target_pairs={{0,8},{8,16},{16,24},{24,0},{1,9},{9,17},{17,25},{25,1},{2,10},{10... | collective-permute-start | bytes 884744 | tf_op jit(solution)/shard_map/ppermute | solution.py:217
  48.1 1.7 %collective-permute-start.7 = (bf16[576,256]{1,0:T(8,128)(2,1)S(1)}, bf16[576,256]{1,0:T(8,128)(2,1)S(1)}, u32[]{:S(2)}, u32[]{:S(2)}) collective-permute-start(bf16[576,256]{1,0:T(8,128)(2,1)S(1)} %slice.29), channel_id=1, source_target_pairs={{0,24},{8,0},{16,8},{24,16},{1,25},{9,1},{17,9},{25,17},{2,26},{10... | collective-permute-start | bytes 884744 | tf_op jit(solution)/shard_map/ppermute | solution.py:217
  49.9 8.4 %shard_map.75 = (f32[1152,128]{1,0:T(8,128)S(1)}, f32[1152,128]{1,0:T(8,128)S(1)}, f32[1152,128]{1,0:T(8,128)S(1)}) custom-call(bf16[288,384]{1,0:T(8,128)(2,1)S(1)} %collective-permute-done.refs_0_, bf16[288,384]{1,0:T(8,128)(2,1)S(1)} %collective-permute-done.1.refs_1_, bf16[288,384]{1,0:T(8,128)(2,1)S(1)} %collective-permute-done.2.refs_2_, ...), custom_call_target="tpu_custom_call" | custom-call | flops 1000 | bytes 1000 | tf_op jit(solution)/shard_map/pallas_call | solution.py:132
  58.3 0.6 collective-permute-start.11
  59.2 0.9 collective-permute-done.11.refs_6_
  60.5 5.6 %shard_map.76 = (bf16[288,128]{1,0:T(8,128)(2,1)S(1)}, bf16[288,128]{1,0:T(8,128)(2,1)S(1)}, bf16[288,128]{1,0:T(8,128)(2,1)S(1)}, bf16[288,128]{1,0:T(8,128)(2,1)S(1)}) custom-call(bf16[288,384]{1,0:T(8,128)(2,1)S(1)} %collective-permute-done.refs_0_, bf16[288,384]{1,0:T(8,128)(2,1)S(1)} %collective-permute-done.1.refs_1_, ...), custom_call_target="tpu_custom_call" | custom-call | flops 1000 | bytes 1000 | tf_op jit(solution)/shard_map/pallas_call | solution.py:132
  66.2 2.5 %collective-permute-start.13 = (bf16[288,128]{1,0:T(8,128)(2,1)S(1)}, bf16[288,128]{1,0:T(8,128)(2,1)S(1)}, u32[]{:S(2)}, u32[]{:S(2)}) collective-permute-start(bf16[288,128]{1,0:T(8,128)(2,1)S(1)} %get-tuple-element.56), channel_id=1, source_target_pairs={{96,0},{224,4},{0,32},{128,36},{32,64},{160,68},{64,96},{192,100},... | collective-permute-start | bytes 221192 | tf_op jit(solution)/shard_map/ppermute | solution.py:211
  69.2 2.9 %collective-permute-start.15 = (bf16[288,128]{1,0:T(8,128)(2,1)S(1)}, bf16[288,128]{1,0:T(8,128)(2,1)S(1)}, u32[]{:S(2)}, u32[]{:S(2)}) collective-permute-start(bf16[288,128]{1,0:T(8,128)(2,1)S(1)} %get-tuple-element.58), channel_id=1, source_target_pairs={{64,0},{192,4},{96,32},{224,36},{0,64},{128,68},{32,96},{160,100},... | collective-permute-start | bytes 221192 | tf_op jit(solution)/shard_map/ppermute | solution.py:211
  72.1 6.9 %collective-permute-start.16 = (bf16[288,128]{1,0:T(8,128)(2,1)S(1)}, bf16[288,128]{1,0:T(8,128)(2,1)S(1)}, u32[]{:S(2)}, u32[]{:S(2)}) collective-permute-start(bf16[288,128]{1,0:T(8,128)(2,1)S(1)} %get-tuple-element.59), channel_id=1, source_target_pairs={{0,0},{128,4},{32,32},{160,36},{64,64},{192,68},{96,96},{224,100},... | collective-permute-start | bytes 221192 | tf_op jit(solution)/shard_map/ppermute | solution.py:211
  79.2 3.3 %collective-permute-done.16 = bf16[288,128]{1,0:T(8,128)(2,1)S(1)} collective-permute-done((bf16[288,128]{1,0:T(8,128)(2,1)S(1)}, bf16[288,128]{1,0:T(8,128)(2,1)S(1)}, u32[]{:S(2)}, u32[]{:S(2)}) %collective-permute-start.16) | collective-permute-done | bytes 73760 | tf_op jit(solution)/shard_map/ppermute | solution.py:211
  82.5 1.4 %collective-permute-start.18 = (bf16[288,512]{1,0:T(8,128)(2,1)S(1)}, bf16[288,512]{1,0:T(8,128)(2,1)S(1)}, u32[]{:S(2)}, u32[]{:S(2)}) collective-permute-start(bf16[288,512]{1,0:T(8,128)(2,1)S(1)} %constant_dynamic-update-slice_fusion.refs_0_), channel_id=1, source_target_pairs={{0,1},{1,2},{2,3},{3,0},{4,5},{5,6},{6,7},{7,4},{8,9},{9,10},{10,1... | collective-permute-start | bytes 884744 | tf_op jit(solution)/shard_map/ppermute | solution.py:217
  83.9 1.5 %collective-permute-start.19 = (bf16[288,512]{1,0:T(8,128)(2,1)S(1)}, bf16[288,512]{1,0:T(8,128)(2,1)S(1)}, u32[]{:S(2)}, u32[]{:S(2)}) collective-permute-start(bf16[288,512]{1,0:T(8,128)(2,1)S(1)} %constant_dynamic-update-slice_fusion.refs_0_), channel_id=1, source_target_pairs={{0,3},{1,0},{2,1},{3,2},{4,7},{5,4},{6,5},{7,6},{8,11},{9,8},{10,9... | collective-permute-start | bytes 884744 | tf_op jit(solution)/shard_map/ppermute | solution.py:217
  85.4 1.6 %collective-permute-start.17 = (bf16[288,512]{1,0:T(8,128)(2,1)S(1)}, bf16[288,512]{1,0:T(8,128)(2,1)S(1)}, u32[]{:S(2)}, u32[]{:S(2)}) collective-permute-start(bf16[288,512]{1,0:T(8,128)(2,1)S(1)} %constant_dynamic-update-slice_fusion.refs_0_), channel_id=1, source_target_pairs={{0,2},{1,3},{2,0},{3,1},{4,6},{5,7},{6,4},{7,5},{8,10},{9,11},{10,... | collective-permute-start | bytes 884744 | tf_op jit(solution)/shard_map/ppermute | solution.py:217
  87.0 1.4 %shard_map.77.refs_2_ = f32[288,1536]{1,0:T(8,128)S(1)} custom-call(s32[3]{0:T(128)S(1)} %copy-done, bf16[2048,1536]{1,0:T(8,128)(2,1)S(1)} %bitcast.6, bf16[288,512]{1,0:T(8,128)(2,1)S(1)} %constant_dynamic-update-slice_fusion.refs_0_), custom_call_target="tpu_custom_call" | custom-call | tf_op jit(solution)/shard_map/pallas_call | solution.py:184
  88.4 3.1 %collective-permute-done.18.refs_0_ = bf16[288,512]{1,0:T(8,128)(2,1)S(1)} collective-permute-done((bf16[288,512]{1,0:T(8,128)(2,1)S(1)}, bf16[288,512]{1,0:T(8,128)(2,1)S(1)}, u32[]{:S(2)}, u32[]{:S(2)}) %collective-permute-start.18) | collective-permute-done | bytes 294944 | tf_op jit(solution)/shard_map/ppermute | solution.py:217
  91.5 2.0 %shard_map.78.refs_1_ = f32[288,1536]{1,0:T(8,128)S(1)} custom-call(s32[3]{0:T(128)S(1)} %copy-done, bf16[2048,1536]{1,0:T(8,128)(2,1)S(1)} %bitcast.6, bf16[288,512]{1,0:T(8,128)(2,1)S(1)} %collective-permute-done.18.refs_0_, bf16[288,512]{1,0:T(8,128)(2,1)S(1)} %collective-permute-done.19.refs_1_, f32[288,1536]{1,0:T(8,128)S(1)} %shard_map.77.refs_2_), custom_call_target="tpu_custom_call" | custom-call | tf_op jit(solution)/shard_map/pallas_call | solution.py:184
  93.6 1.1 %collective-permute-done.17.refs_0_ = bf16[288,512]{1,0:T(8,128)(2,1)S(1)} collective-permute-done((bf16[288,512]{1,0:T(8,128)(2,1)S(1)}, bf16[288,512]{1,0:T(8,128)(2,1)S(1)}, u32[]{:S(2)}, u32[]{:S(2)}) %collective-permute-start.17) | collective-permute-done | bytes 294944 | tf_op jit(solution)/shard_map/ppermute | solution.py:217
  94.6 1.4 %shard_map.79 = (f32[144,1536]{1,0:T(8,128)S(1)}, bf16[144,1536]{1,0:T(8,128)(2,1)S(1)}) custom-call(s32[3]{0:T(128)S(1)} %copy-done, bf16[2048,1536]{1,0:T(8,128)(2,1)S(1)} %bitcast.6, bf16[288,512]{1,0:T(8,128)(2,1)S(1)} %collective-permute-done.17.refs_0_, f32[288,1536]{1,0:T(8,128)S(1)} %shard_map.78.refs_1_), custom_call_target="tpu_custom_call" | custom-call | tf_op jit(solution)/shard_map/pallas_call | solution.py:184
  96.1 1.8 %collective-permute-done.20 = bf16[144,1536]{1,0:T(8,128)(2,1)S(1)} collective-permute-done((bf16[144,1536]{1,0:T(8,128)(2,1)S(1)}, bf16[144,1536]{1,0:T(8,128)(2,1)S(1)}, u32[]{:S(2)}, u32[]{:S(2)}) %collective-permute-start.20) | collective-permute-done | bytes 442400 | tf_op jit(solution)/shard_map/ppermute | solution.py:221
  97.9 0.9 add_convert_fusion
  (39 shorter events, 2.4 us)
Async XLA Ops:
  4.1 18.3 %collective-permute-start = (bf16[288,384]{1,0:T(8,128)(2,1)}, bf16[288,384]{1,0:T(8,128)(2,1)S(1)}, u32[]{:S(2)}, u32[]{:S(2)}) collective-permute-start(bf16[288,384]{1,0:T(8,128)(2,1)} %get-tuple-element.36), channel_id=1, source_target_pairs={{0,96},{4,224},{32,0},{36,128},{64,32},{68,160},{96,64},{100,192},... | collective-permute-start | bytes 663560 | tf_op jit(solution)/shard_map/ppermute | solution.py:207
  11.1 11.3 %collective-permute-start.1 = (bf16[288,384]{1,0:T(8,128)(2,1)}, bf16[288,384]{1,0:T(8,128)(2,1)S(1)}, u32[]{:S(2)}, u32[]{:S(2)}) collective-permute-start(bf16[288,384]{1,0:T(8,128)(2,1)} %get-tuple-element.37), channel_id=1, source_target_pairs={{0,32},{4,160},{32,64},{36,192},{64,96},{68,224},{96,0},{100,128},... | collective-permute-start | bytes 663560 | tf_op jit(solution)/shard_map/ppermute | solution.py:207
  12.1 18.9 %collective-permute-start.2 = (bf16[288,384]{1,0:T(8,128)(2,1)}, bf16[288,384]{1,0:T(8,128)(2,1)S(1)}, u32[]{:S(2)}, u32[]{:S(2)}) collective-permute-start(bf16[288,384]{1,0:T(8,128)(2,1)} %get-tuple-element.38), channel_id=1, source_target_pairs={{0,64},{4,192},{32,96},{36,224},{64,0},{68,128},{96,32},{100,160},... | collective-permute-start | bytes 663560 | tf_op jit(solution)/shard_map/ppermute | solution.py:207
  16.3 14.7 %collective-permute-start.3 = (bf16[288,384]{1,0:T(8,128)(2,1)}, bf16[288,384]{1,0:T(8,128)(2,1)S(1)}, u32[]{:S(2)}, u32[]{:S(2)}) collective-permute-start(bf16[288,384]{1,0:T(8,128)(2,1)} %get-tuple-element.39), channel_id=1, source_target_pairs={{0,0},{4,128},{32,32},{36,160},{64,64},{68,192},{96,96},{100,224},... | collective-permute-start | bytes 663560 | tf_op jit(solution)/shard_map/ppermute | solution.py:207
  31.1 14.9 %collective-permute-start.4 = (bf16[1152,256]{1,0:T(8,128)(2,1)S(1)}, bf16[1152,256]{1,0:T(8,128)(2,1)S(1)}, u32[]{:S(2)}, u32[]{:S(2)}) collective-permute-start(bf16[1152,256]{1,0:T(8,128)(2,1)S(1)} %pad_maximum_fusion.refs_4_), channel_id=1, source_target_pairs={{0,8},{8,16},{16,24},{24,0},{1,9},{9,17},{17,25},{25,1},{2,10},{10... | collective-permute-start | bytes 1769480 | tf_op jit(solution)/shard_map/ppermute | solution.py:217
  32.4 13.9 %collective-permute-start.6 = (bf16[1152,256]{1,0:T(8,128)(2,1)S(1)}, bf16[1152,256]{1,0:T(8,128)(2,1)S(1)}, u32[]{:S(2)}, u32[]{:S(2)}) collective-permute-start(bf16[1152,256]{1,0:T(8,128)(2,1)S(1)} %pad_maximum_fusion.refs_4_), channel_id=1, source_target_pairs={{0,24},{8,0},{16,8},{24,16},{1,25},{9,1},{17,9},{25,17},{2,26},{10... | collective-permute-start | bytes 1769480 | tf_op jit(solution)/shard_map/ppermute | solution.py:217
  33.8 16.0 %collective-permute-start.8 = (bf16[1152,256]{1,0:T(8,128)(2,1)S(1)}, bf16[1152,256]{1,0:T(8,128)(2,1)S(1)}, u32[]{:S(2)}, u32[]{:S(2)}) collective-permute-start(bf16[1152,256]{1,0:T(8,128)(2,1)S(1)} %pad_maximum_fusion.refs_4_), channel_id=1, source_target_pairs={{0,4},{4,0},{1,5},{5,1},{2,6},{6,2},{3,7},{7,3},{8,12},{12,8},{9,1... | collective-permute-start | bytes 1769480 | tf_op jit(solution)/shard_map/ppermute | solution.py:221
  33.9 53.1 %slice-start = ((s8[6291456]{0:T(1024)(128)(4,1)}), s8[4194304]{0:T(1024)(128)(4,1)S(1)}, s32[]{:S(2)}) async-start(s8[6291456]{0:T(1024)(128)(4,1)} %bitcast.5), calls=%async_computation | async-start | bytes 8388608
  46.2 3.6 %collective-permute-start.10 = (bf16[1152,256]{1,0:T(8,128)(2,1)S(1)}, bf16[1152,256]{1,0:T(8,128)(2,1)S(1)}, u32[]{:S(2)}, u32[]{:S(2)}) collective-permute-start(bf16[1152,256]{1,0:T(8,128)(2,1)S(1)} %collective-permute-done.6.refs_6_), channel_id=1, source_target_pairs={{0,4},{4,0},{1,5},{5,1},{2,6},{6,2},{3,7},{7,3},{8,12},{12,8},{9,1... | collective-permute-start | bytes 1769480 | tf_op jit(solution)/shard_map/ppermute | solution.py:221
  46.2 3.6 %collective-permute-start.9 = (bf16[1152,256]{1,0:T(8,128)(2,1)S(1)}, bf16[1152,256]{1,0:T(8,128)(2,1)S(1)}, u32[]{:S(2)}, u32[]{:S(2)}) collective-permute-start(bf16[1152,256]{1,0:T(8,128)(2,1)S(1)} %collective-permute-done.4.refs_5_), channel_id=1, source_target_pairs={{0,4},{4,0},{1,5},{5,1},{2,6},{6,2},{3,7},{7,3},{8,12},{12,8},{9,1... | collective-permute-start | bytes 1769480 | tf_op jit(solution)/shard_map/ppermute | solution.py:221
  46.8 11.5 %collective-permute-start.5 = (bf16[576,256]{1,0:T(8,128)(2,1)S(1)}, bf16[576,256]{1,0:T(8,128)(2,1)S(1)}, u32[]{:S(2)}, u32[]{:S(2)}) collective-permute-start(bf16[576,256]{1,0:T(8,128)(2,1)S(1)} %slice.28), channel_id=1, source_target_pairs={{0,8},{8,16},{16,24},{24,0},{1,9},{9,17},{17,25},{25,1},{2,10},{10... | collective-permute-start | bytes 884744 | tf_op jit(solution)/shard_map/ppermute | solution.py:217
  48.1 38.9 %slice-start.1 = ((s8[6291456]{0:T(1024)(128)(4,1)}), s8[2097152]{0:T(1024)(128)(4,1)S(1)}, s32[]{:S(2)}) async-start(s8[6291456]{0:T(1024)(128)(4,1)} %bitcast.5), calls=%async_computation.1 | async-start | bytes 4194304
  48.1 10.2 %collective-permute-start.7 = (bf16[576,256]{1,0:T(8,128)(2,1)S(1)}, bf16[576,256]{1,0:T(8,128)(2,1)S(1)}, u32[]{:S(2)}, u32[]{:S(2)}) collective-permute-start(bf16[576,256]{1,0:T(8,128)(2,1)S(1)} %slice.29), channel_id=1, source_target_pairs={{0,24},{8,0},{16,8},{24,16},{1,25},{9,1},{17,9},{25,17},{2,26},{10... | collective-permute-start | bytes 884744 | tf_op jit(solution)/shard_map/ppermute | solution.py:217
  58.3 28.7 %copy-start = (s32[3]{0:T(128)S(1)}, s32[3]{0:T(128)}, u32[]{:S(2)}) copy-start(s32[3]{0:T(128)} %pad_add_fusion.pos_ref) | copy-start | bytes 40
  58.3 1.8 %collective-permute-start.11 = (bf16[576,256]{1,0:T(8,128)(2,1)S(1)}, bf16[576,256]{1,0:T(8,128)(2,1)S(1)}, u32[]{:S(2)}, u32[]{:S(2)}) collective-permute-start(bf16[576,256]{1,0:T(8,128)(2,1)S(1)} %collective-permute-done.5.refs_4_), channel_id=1, source_target_pairs={{0,4},{4,0},{1,5},{5,1},{2,6},{6,2},{3,7},{7,3},{8,12},{12,8},{9,1... | collective-permute-start | bytes 884744 | tf_op jit(solution)/shard_map/ppermute | solution.py:221
  58.9 1.6 %collective-permute-start.12 = (bf16[576,256]{1,0:T(8,128)(2,1)S(1)}, bf16[576,256]{1,0:T(8,128)(2,1)S(1)}, u32[]{:S(2)}, u32[]{:S(2)}) collective-permute-start(bf16[576,256]{1,0:T(8,128)(2,1)S(1)} %collective-permute-done.7.refs_5_), channel_id=1, source_target_pairs={{0,4},{4,0},{1,5},{5,1},{2,6},{6,2},{3,7},{7,3},{8,12},{12,8},{9,1... | collective-permute-start | bytes 884744 | tf_op jit(solution)/shard_map/ppermute | solution.py:221
  66.2 12.9 %collective-permute-start.13 = (bf16[288,128]{1,0:T(8,128)(2,1)S(1)}, bf16[288,128]{1,0:T(8,128)(2,1)S(1)}, u32[]{:S(2)}, u32[]{:S(2)}) collective-permute-start(bf16[288,128]{1,0:T(8,128)(2,1)S(1)} %get-tuple-element.56), channel_id=1, source_target_pairs={{96,0},{224,4},{0,32},{128,36},{32,64},{160,68},{64,96},{192,100},... | collective-permute-start | bytes 221192 | tf_op jit(solution)/shard_map/ppermute | solution.py:211
  68.7 10.4 %collective-permute-start.14 = (bf16[288,128]{1,0:T(8,128)(2,1)S(1)}, bf16[288,128]{1,0:T(8,128)(2,1)S(1)}, u32[]{:S(2)}, u32[]{:S(2)}) collective-permute-start(bf16[288,128]{1,0:T(8,128)(2,1)S(1)} %get-tuple-element.57), channel_id=1, source_target_pairs={{32,0},{160,4},{64,32},{192,36},{96,64},{224,68},{0,96},{128,100},... | collective-permute-start | bytes 221192 | tf_op jit(solution)/shard_map/ppermute | solution.py:211
  69.2 9.9 %collective-permute-start.15 = (bf16[288,128]{1,0:T(8,128)(2,1)S(1)}, bf16[288,128]{1,0:T(8,128)(2,1)S(1)}, u32[]{:S(2)}, u32[]{:S(2)}) collective-permute-start(bf16[288,128]{1,0:T(8,128)(2,1)S(1)} %get-tuple-element.58), channel_id=1, source_target_pairs={{64,0},{192,4},{96,32},{224,36},{0,64},{128,68},{32,96},{160,100},... | collective-permute-start | bytes 221192 | tf_op jit(solution)/shard_map/ppermute | solution.py:211
  72.1 10.4 %collective-permute-start.16 = (bf16[288,128]{1,0:T(8,128)(2,1)S(1)}, bf16[288,128]{1,0:T(8,128)(2,1)S(1)}, u32[]{:S(2)}, u32[]{:S(2)}) collective-permute-start(bf16[288,128]{1,0:T(8,128)(2,1)S(1)} %get-tuple-element.59), channel_id=1, source_target_pairs={{0,0},{128,4},{32,32},{160,36},{64,64},{192,68},{96,96},{224,100},... | collective-permute-start | bytes 221192 | tf_op jit(solution)/shard_map/ppermute | solution.py:211
  82.5 9.0 %collective-permute-start.18 = (bf16[288,512]{1,0:T(8,128)(2,1)S(1)}, bf16[288,512]{1,0:T(8,128)(2,1)S(1)}, u32[]{:S(2)}, u32[]{:S(2)}) collective-permute-start(bf16[288,512]{1,0:T(8,128)(2,1)S(1)} %constant_dynamic-update-slice_fusion.refs_0_), channel_id=1, source_target_pairs={{0,1},{1,2},{2,3},{3,0},{4,5},{5,6},{6,7},{7,4},{8,9},{9,10},{10,1... | collective-permute-start | bytes 884744 | tf_op jit(solution)/shard_map/ppermute | solution.py:217
  83.9 7.6 %collective-permute-start.19 = (bf16[288,512]{1,0:T(8,128)(2,1)S(1)}, bf16[288,512]{1,0:T(8,128)(2,1)S(1)}, u32[]{:S(2)}, u32[]{:S(2)}) collective-permute-start(bf16[288,512]{1,0:T(8,128)(2,1)S(1)} %constant_dynamic-update-slice_fusion.refs_0_), channel_id=1, source_target_pairs={{0,3},{1,0},{2,1},{3,2},{4,7},{5,4},{6,5},{7,6},{8,11},{9,8},{10,9... | collective-permute-start | bytes 884744 | tf_op jit(solution)/shard_map/ppermute | solution.py:217
  85.4 9.2 %collective-permute-start.17 = (bf16[288,512]{1,0:T(8,128)(2,1)S(1)}, bf16[288,512]{1,0:T(8,128)(2,1)S(1)}, u32[]{:S(2)}, u32[]{:S(2)}) collective-permute-start(bf16[288,512]{1,0:T(8,128)(2,1)S(1)} %constant_dynamic-update-slice_fusion.refs_0_), channel_id=1, source_target_pairs={{0,2},{1,3},{2,0},{3,1},{4,6},{5,7},{6,4},{7,5},{8,10},{9,11},{10,... | collective-permute-start | bytes 884744 | tf_op jit(solution)/shard_map/ppermute | solution.py:217
  93.5 4.4 %copy-start.1 = (bf16[144,1536]{1,0:T(8,128)(2,1)S(1)}, bf16[144,1536]{1,0:T(8,128)(2,1)}, u32[]{:S(2)}) copy-start(bf16[144,1536]{1,0:T(8,128)(2,1)} %param.12) | copy-start | bytes 1327108
  96.0 1.9 %collective-permute-start.20 = (bf16[144,1536]{1,0:T(8,128)(2,1)S(1)}, bf16[144,1536]{1,0:T(8,128)(2,1)S(1)}, u32[]{:S(2)}, u32[]{:S(2)}) collective-permute-start(bf16[144,1536]{1,0:T(8,128)(2,1)S(1)} %get-tuple-element.66), channel_id=1, source_target_pairs={{0,4},{4,0},{1,5},{5,1},{2,6},{6,2},{3,7},{7,3},{8,12},{12,8},{9,1... | collective-permute-start | bytes 1327112 | tf_op jit(solution)/shard_map/ppermute | solution.py:221

commit v5 on v4

--- a/solution.py
+++ b/solution.py
@@ -16,10 +16,9 @@
 ROWS = 288
 HALF = ROWS // 2
 HEADS = 4
-SENDS = (3, 1, 2, 0)
+SENDS = (3, 2, 1, 0)
 NT = (((1,), (1,)), ((), ()))
 VM = pl.BlockSpec(memory_space=pltpu.VMEM)
-SM = pl.BlockSpec(memory_space=pltpu.MemorySpace.SMEM)
 ANY = pl.BlockSpec(memory_space=pl.ANY)
 VLIM = 40 << 20
 
@@ -31,7 +30,7 @@
     return shifted * lax.rsqrt(variance + EPS) * gain
 
 
-def norm_kernel(pos_ref, *refs):
+def norm_kernel(*refs):
     sources, outs, held, sems = refs[:5], refs[5:9], refs[9:14], refs[14]
     copies = [
         pltpu.make_async_copy(a, b, sems.at[i]) for i, (a, b) in enumerate(zip(sources, held))
@@ -39,7 +38,8 @@
     for c in copies:
         c.start()
     k_ref, kg_ref, v_ref, q_ref, qg_ref = held
-    heads = [lax.rem(pos_ref[0] + j, HEADS) for j in SENDS]
+    turn = lax.axis_index("z")
+    heads = [lax.rem(turn + j, HEADS) for j in SENDS]
     columns = [pl.ds(pl.multiple_of(h * DH, DH), DH) for h in heads]
     copies[0].wait()
     copies[1].wait()
@@ -55,16 +55,16 @@
         out[:, 2 * DH :] = (queries * (1.0 / math.sqrt(DH))).astype(BF)
 
 
-def norms(pos, *arrays):
+def norms(*arrays):
     return pl.pallas_call(
         norm_kernel,
         out_shape=[jax.ShapeDtypeStruct((ROWS, 3 * DH), BF)] * HEADS,
-        in_specs=[SM] + [ANY] * 5,
+        in_specs=[ANY] * 5,
         out_specs=[VM] * HEADS,
         scratch_shapes=[pltpu.VMEM(a.shape, a.dtype) for a in arrays]
         + [pltpu.SemaphoreType.DMA((5,))],
         compiler_params=pltpu.CompilerParams(vmem_limit_bytes=62 << 20),
-    )(pos, *arrays)
+    )(*arrays)
 
 
 def flash_kernel(first, last, nq, nkv, most, *refs):
@@ -85,10 +85,8 @@
         q = queries[i][:, 2 * DH :]
 
         def scores(block):
-            parts = [
-                lax.dot_general(q, p[:, :DH], NT, preferred_element_type=F32) for p in block
-            ]
-            return jnp.concatenate(parts, axis=1)
+            keys = jnp.concatenate([p[:, :DH] for p in block], axis=0)
+            return lax.dot_general(q, keys, NT, preferred_element_type=F32)
 
         if first:
             high = None
@@ -139,13 +137,13 @@
     )(*queries, *pieces, *state)
 
 
-def project_kernel(steps, first, last, pos_ref, w_hbm, *refs):
+def project_kernel(steps, first, last, w_hbm, *refs):
     n = len(steps)
     blocks, refs = refs[:n], refs[n:]
     if not first:
         acc_ref, refs = refs[0], refs[1:]
     outs, (weight, tokens, sems) = refs[: 1 + last], refs[1 + last :]
-    turn, col, core = pos_ref[0], pos_ref[1], pos_ref[2]
+    turn, col, core = [lax.axis_index(a) for a in ("z", "col", "row")]
     wide = HEADS * DH
     copies = []
     for k, s in enumerate(steps):
@@ -174,7 +172,7 @@
         outs[0][...] = total
 
 
-def project(steps, last, pos, weight, blocks, *total):
+def project(steps, last, weight, blocks, *total):
     n = len(steps)
     wide, width = HEADS * DH, weight.shape[1]
     if last:
@@ -184,7 +182,7 @@
     return pl.pallas_call(
         functools.partial(project_kernel, steps, not total, last),
         out_shape=shapes,
-        in_specs=[SM, ANY] + [VM] * (n + len(total)),
+        in_specs=[ANY] + [VM] * (n + len(total)),
         out_specs=[VM] * len(shapes),
         scratch_shapes=[
             pltpu.VMEM((n, wide, width), BF),
@@ -192,7 +190,7 @@
             pltpu.SemaphoreType.DMA((n,)),
         ],
         compiler_params=pltpu.CompilerParams(vmem_limit_bytes=VLIM),
-    )(pos, weight, *blocks, *total)
+    )(weight, *blocks, *total)
 
 
 def owner_pairs(j):
@@ -222,9 +220,8 @@
 
 
 def body(query_proj, key_proj, value_proj, query_gain, key_gain, residual, out_weight):
-    pos = jnp.stack([lax.axis_index(a) for a in ("z", "col", "row")]).astype(jnp.int32)
     ready = norms(
-        pos, key_proj, key_gain.reshape(1, -1), value_proj, query_proj, query_gain.reshape(1, -1)
+        key_proj, key_gain.reshape(1, -1), value_proj, query_proj, query_gain.reshape(1, -1)
     )
     held = [to_owner(ready[j], j) for j in range(HEADS)]
     own = jnp.concatenate([m[:, : 2 * DH] for m in held], axis=0)
@@ -238,11 +235,11 @@
     attended = flash(True, held, far + [swap(p) for p in far], (a, b, c))
     mine = jnp.concatenate([from_owner(attended[j], j) for j in range(HEADS)], axis=1)
     far, near, back = [shift(mine, "col", NY, s) for s in (2, 1, 3)]
-    total = project((0,), False, pos, out_weight, [mine])
+    total = project((0,), False, out_weight, [mine])
     near, back, *total = lax.optimization_barrier((near, back, *total))
-    total = project((1, 3), False, pos, out_weight, [near, back], *total)
+    total = project((1, 3), False, out_weight, [near, back], *total)
     far, *total = lax.optimization_barrier((far, *total))
-    keep, send = project((2,), True, pos, out_weight, [far], *total)
+    keep, send = project((2,), True, out_weight, [far], *total)
     return (residual.astype(F32) + (keep + swap(send).astype(F32))).astype(BF)
 
 

time: 99.2 us -> 94 us (0.948)
  Pallas kernels: 24.5 us -> 21 us
  starting transfers between devices: 39.7 us -> 38.3 us
    pallas_call x3, Pallas kernels: 4.8 us -> 3.1 us  [project(): pl.pallas_call(functools.partial(project_kernel, steps, not total, last),...]
    ppermute x4, starting transfers between devices: 12.9 us -> 11.5 us  [from_owner(): lax.ppermute(value, ('z', 'row'), [(b, a) for a, b in owner_pairs(j)])]
    pallas_call x3, Pallas kernels: 16.3 us -> 15.1 us  [flash(): pl.pallas_call(functools.partial(flash_kernel, not state, last, nq, n, mo...]
  transfers between devices with their start and end apart: 21 -> 21, of which waited for: 10 -> 12; matrix products, arithmetic and copies ran while one was open for 0% -> 0% of each run, Pallas kernels for 14% -> 14%
where the time goes in v5:
time: 94 us; the launch traced here: 93.9 us
  starting transfers between devices  38.3 us (41%)
  waiting for transfers between devices  33.2 us (35%)
  Pallas kernels  21 us (22%)
    pallas_call x3, Pallas kernels, flash(): pl.pallas_call(functools.partial(flash_kernel, not state, last, nq, n, mo...  15.1 us
    ppermute x4, starting transfers between devices, to_owner(): return lax.ppermute(value, ('z', 'row'), owner_pairs(j))  15 us
    ppermute x7, waiting for transfers between devices, shift(): lax.ppermute(value, axis, [(i, (i + step) % size) for i in range(size)])  14.2 us
    ppermute x4, waiting for transfers between devices, to_owner(): return lax.ppermute(value, ('z', 'row'), owner_pairs(j))  11.9 us
    ppermute x4, starting transfers between devices, from_owner(): lax.ppermute(value, ('z', 'row'), [(b, a) for a, b in owner_pairs(j)])  11.5 us
    ppermute x7, starting transfers between devices, shift(): lax.ppermute(value, axis, [(i, (i + step) % size) for i in range(size)])  10.2 us
    ppermute x4, waiting for transfers between devices, from_owner(): lax.ppermute(value, ('z', 'row'), [(b, a) for a, b in owner_pairs(j)])  3.94 us
    pallas_call x3, Pallas kernels, project(): pl.pallas_call(functools.partial(project_kernel, steps, not total, last),...  3.1 us
  transfers between devices with their start and end apart: 21, of which 12 were waited for; matrix products, arithmetic and copies ran while one was open for 0% of the time, Pallas kernels for 14%

profile of v5, /device:TPU:1, one launch (start us, length us, event | category | flops | bytes accessed | tf_op | source)
XLA Modules:
  0.0 93.9 jit_solution(629274758429458821)
XLA Ops:
  0.0 2.8 %shard_map.73 = (bf16[288,384]{1,0:T(8,128)(2,1)}, bf16[288,384]{1,0:T(8,128)(2,1)}, bf16[288,384]{1,0:T(8,128)(2,1)}, bf16[288,384]{1,0:T(8,128)(2,1)}) custom-call(bf16[288,512]{1,0:T(8,128)(2,1)} %refs_0_.1, f32[1,512]{1,0:T(1,128)} %bitcast.4, bf16[288,512]{1,0:T(8,128)(2,1)} %refs_2_.1, bf16[288,512]{1,0:T(8,128)(2,1)} %refs_3_.1, f32[1,512]{1,0:T(1,128)} %bitcast.5), custom_call_target="tpu_custom_call" | custom-call | tf_op jit(solution)/shard_map/pallas_call | solution.py:59
  2.8 7.0 %collective-permute-start = (bf16[288,384]{1,0:T(8,128)(2,1)}, bf16[288,384]{1,0:T(8,128)(2,1)S(1)}, u32[]{:S(2)}, u32[]{:S(2)}) collective-permute-start(bf16[288,384]{1,0:T(8,128)(2,1)} %get-tuple-element.36), channel_id=1, source_target_pairs={{0,96},{4,224},{32,0},{36,128},{64,32},{68,160},{96,64},{100,192},... | collective-permute-start | bytes 663560 | tf_op jit(solution)/shard_map/ppermute | solution.py:205
  9.9 0.5 collective-permute-start.1
  10.4 4.7 %collective-permute-start.2 = (bf16[288,384]{1,0:T(8,128)(2,1)}, bf16[288,384]{1,0:T(8,128)(2,1)S(1)}, u32[]{:S(2)}, u32[]{:S(2)}) collective-permute-start(bf16[288,384]{1,0:T(8,128)(2,1)} %get-tuple-element.38), channel_id=1, source_target_pairs={{0,32},{4,160},{32,64},{36,192},{64,96},{68,224},{96,0},{100,128},... | collective-permute-start | bytes 663560 | tf_op jit(solution)/shard_map/ppermute | solution.py:205
  15.1 2.8 %collective-permute-start.3 = (bf16[288,384]{1,0:T(8,128)(2,1)}, bf16[288,384]{1,0:T(8,128)(2,1)S(1)}, u32[]{:S(2)}, u32[]{:S(2)}) collective-permute-start(bf16[288,384]{1,0:T(8,128)(2,1)} %get-tuple-element.39), channel_id=1, source_target_pairs={{0,0},{4,128},{32,32},{36,160},{64,64},{68,192},{96,96},{100,224},... | collective-permute-start | bytes 663560 | tf_op jit(solution)/shard_map/ppermute | solution.py:205
  17.9 3.2 %collective-permute-done.refs_0_ = bf16[288,384]{1,0:T(8,128)(2,1)S(1)} collective-permute-done((bf16[288,384]{1,0:T(8,128)(2,1)}, bf16[288,384]{1,0:T(8,128)(2,1)S(1)}, u32[]{:S(2)}, u32[]{:S(2)}) %collective-permute-start) | collective-permute-done | bytes 221216 | tf_op jit(solution)/shard_map/ppermute | solution.py:205
  21.1 6.1 %collective-permute-done.1.refs_1_ = bf16[288,384]{1,0:T(8,128)(2,1)S(1)} collective-permute-done((bf16[288,384]{1,0:T(8,128)(2,1)}, bf16[288,384]{1,0:T(8,128)(2,1)S(1)}, u32[]{:S(2)}, u32[]{:S(2)}) %collective-permute-start.1) | collective-permute-done | bytes 221216 | tf_op jit(solution)/shard_map/ppermute | solution.py:205
  27.2 2.5 %collective-permute-done.2.refs_2_ = bf16[288,384]{1,0:T(8,128)(2,1)S(1)} collective-permute-done((bf16[288,384]{1,0:T(8,128)(2,1)}, bf16[288,384]{1,0:T(8,128)(2,1)S(1)}, u32[]{:S(2)}, u32[]{:S(2)}) %collective-permute-start.2) | collective-permute-done | bytes 221216 | tf_op jit(solution)/shard_map/ppermute | solution.py:205
  29.9 1.3 %collective-permute-start.4 = (bf16[1152,256]{1,0:T(8,128)(2,1)S(1)}, bf16[1152,256]{1,0:T(8,128)(2,1)S(1)}, u32[]{:S(2)}, u32[]{:S(2)}) collective-permute-start(bf16[1152,256]{1,0:T(8,128)(2,1)S(1)} %pad_maximum_fusion.refs_4_), channel_id=1, source_target_pairs={{0,8},{8,16},{16,24},{24,0},{1,9},{9,17},{17,25},{25,1},{2,10},{10... | collective-permute-start | bytes 1769480 | tf_op jit(solution)/shard_map/ppermute | solution.py:215
  31.2 1.5 %collective-permute-start.6 = (bf16[1152,256]{1,0:T(8,128)(2,1)S(1)}, bf16[1152,256]{1,0:T(8,128)(2,1)S(1)}, u32[]{:S(2)}, u32[]{:S(2)}) collective-permute-start(bf16[1152,256]{1,0:T(8,128)(2,1)S(1)} %pad_maximum_fusion.refs_4_), channel_id=1, source_target_pairs={{0,24},{8,0},{16,8},{24,16},{1,25},{9,1},{17,9},{25,17},{2,26},{10... | collective-permute-start | bytes 1769480 | tf_op jit(solution)/shard_map/ppermute | solution.py:215
  32.6 2.2 %shard_map.74 = (f32[1152,128]{1,0:T(8,128)S(1)}, f32[1152,128]{1,0:T(8,128)S(1)}, f32[1152,128]{1,0:T(8,128)S(1)}) custom-call(bf16[288,384]{1,0:T(8,128)(2,1)S(1)} %collective-permute-done.refs_0_, bf16[288,384]{1,0:T(8,128)(2,1)S(1)} %collective-permute-done.1.refs_1_, bf16[288,384]{1,0:T(8,128)(2,1)S(1)} %collective-permute-done.2.refs_2_, ...), custom_call_target="tpu_custom_call" | custom-call | flops 1000 | bytes 1000 | tf_op jit(solution)/shard_map/pallas_call | solution.py:130
  34.9 9.2 %collective-permute-done.4.refs_5_ = bf16[1152,256]{1,0:T(8,128)(2,1)S(1)} collective-permute-done((bf16[1152,256]{1,0:T(8,128)(2,1)S(1)}, bf16[1152,256]{1,0:T(8,128)(2,1)S(1)}, u32[]{:S(2)}, u32[]{:S(2)}) %collective-permute-start.4) | collective-permute-done | bytes 589856 | tf_op jit(solution)/shard_map/ppermute | solution.py:215
  44.9 1.3 %collective-permute-start.5 = (bf16[576,256]{1,0:T(8,128)(2,1)S(1)}, bf16[576,256]{1,0:T(8,128)(2,1)S(1)}, u32[]{:S(2)}, u32[]{:S(2)}) collective-permute-start(bf16[576,256]{1,0:T(8,128)(2,1)S(1)} %slice.28), channel_id=1, source_target_pairs={{0,8},{8,16},{16,24},{24,0},{1,9},{9,17},{17,25},{25,1},{2,10},{10... | collective-permute-start | bytes 884744 | tf_op jit(solution)/shard_map/ppermute | solution.py:215
  46.2 1.7 %collective-permute-start.7 = (bf16[576,256]{1,0:T(8,128)(2,1)S(1)}, bf16[576,256]{1,0:T(8,128)(2,1)S(1)}, u32[]{:S(2)}, u32[]{:S(2)}) collective-permute-start(bf16[576,256]{1,0:T(8,128)(2,1)S(1)} %slice.29), channel_id=1, source_target_pairs={{0,24},{8,0},{16,8},{24,16},{1,25},{9,1},{17,9},{25,17},{2,26},{10... | collective-permute-start | bytes 884744 | tf_op jit(solution)/shard_map/ppermute | solution.py:215
  48.0 8.5 %shard_map.75 = (f32[1152,128]{1,0:T(8,128)S(1)}, f32[1152,128]{1,0:T(8,128)S(1)}, f32[1152,128]{1,0:T(8,128)S(1)}) custom-call(bf16[288,384]{1,0:T(8,128)(2,1)S(1)} %collective-permute-done.refs_0_, bf16[288,384]{1,0:T(8,128)(2,1)S(1)} %collective-permute-done.1.refs_1_, bf16[288,384]{1,0:T(8,128)(2,1)S(1)} %collective-permute-done.2.refs_2_, ...), custom_call_target="tpu_custom_call" | custom-call | flops 1000 | bytes 1000 | tf_op jit(solution)/shard_map/pallas_call | solution.py:130
  56.5 0.6 collective-permute-start.11
  57.4 0.9 collective-permute-done.11.refs_6_
  58.8 4.4 %shard_map.76 = (bf16[288,128]{1,0:T(8,128)(2,1)S(1)}, bf16[288,128]{1,0:T(8,128)(2,1)S(1)}, bf16[288,128]{1,0:T(8,128)(2,1)S(1)}, bf16[288,128]{1,0:T(8,128)(2,1)S(1)}) custom-call(bf16[288,384]{1,0:T(8,128)(2,1)S(1)} %collective-permute-done.refs_0_, bf16[288,384]{1,0:T(8,128)(2,1)S(1)} %collective-permute-done.1.refs_1_, ...), custom_call_target="tpu_custom_call" | custom-call | flops 1000 | bytes 1000 | tf_op jit(solution)/shard_map/pallas_call | solution.py:130
  63.1 3.8 %collective-permute-start.13 = (bf16[288,128]{1,0:T(8,128)(2,1)S(1)}, bf16[288,128]{1,0:T(8,128)(2,1)S(1)}, u32[]{:S(2)}, u32[]{:S(2)}) collective-permute-start(bf16[288,128]{1,0:T(8,128)(2,1)S(1)} %get-tuple-element.56), channel_id=1, source_target_pairs={{96,0},{224,4},{0,32},{128,36},{32,64},{160,68},{64,96},{192,100},... | collective-permute-start | bytes 221192 | tf_op jit(solution)/shard_map/ppermute | solution.py:209
  66.9 2.2 %collective-permute-start.15 = (bf16[288,128]{1,0:T(8,128)(2,1)S(1)}, bf16[288,128]{1,0:T(8,128)(2,1)S(1)}, u32[]{:S(2)}, u32[]{:S(2)}) collective-permute-start(bf16[288,128]{1,0:T(8,128)(2,1)S(1)} %get-tuple-element.58), channel_id=1, source_target_pairs={{32,0},{160,4},{64,32},{192,36},{96,64},{224,68},{0,96},{128,100},... | collective-permute-start | bytes 221192 | tf_op jit(solution)/shard_map/ppermute | solution.py:209
  69.1 5.5 %collective-permute-start.16 = (bf16[288,128]{1,0:T(8,128)(2,1)S(1)}, bf16[288,128]{1,0:T(8,128)(2,1)S(1)}, u32[]{:S(2)}, u32[]{:S(2)}) collective-permute-start(bf16[288,128]{1,0:T(8,128)(2,1)S(1)} %get-tuple-element.59), channel_id=1, source_target_pairs={{0,0},{128,4},{32,32},{160,36},{64,64},{192,68},{96,96},{224,100},... | collective-permute-start | bytes 221192 | tf_op jit(solution)/shard_map/ppermute | solution.py:209
  74.8 3.9 %collective-permute-done.16 = bf16[288,128]{1,0:T(8,128)(2,1)S(1)} collective-permute-done((bf16[288,128]{1,0:T(8,128)(2,1)S(1)}, bf16[288,128]{1,0:T(8,128)(2,1)S(1)}, u32[]{:S(2)}, u32[]{:S(2)}) %collective-permute-start.16) | collective-permute-done | bytes 73760 | tf_op jit(solution)/shard_map/ppermute | solution.py:209
  78.7 1.4 %collective-permute-start.18 = (bf16[288,512]{1,0:T(8,128)(2,1)S(1)}, bf16[288,512]{1,0:T(8,128)(2,1)S(1)}, u32[]{:S(2)}, u32[]{:S(2)}) collective-permute-start(bf16[288,512]{1,0:T(8,128)(2,1)S(1)} %constant_dynamic-update-slice_fusion.refs_0_), channel_id=1, source_target_pairs={{0,1},{1,2},{2,3},{3,0},{4,5},{5,6},{6,7},{7,4},{8,9},{9,10},{10,1... | collective-permute-start | bytes 884744 | tf_op jit(solution)/shard_map/ppermute | solution.py:215
  80.1 1.5 %collective-permute-start.19 = (bf16[288,512]{1,0:T(8,128)(2,1)S(1)}, bf16[288,512]{1,0:T(8,128)(2,1)S(1)}, u32[]{:S(2)}, u32[]{:S(2)}) collective-permute-start(bf16[288,512]{1,0:T(8,128)(2,1)S(1)} %constant_dynamic-update-slice_fusion.refs_0_), channel_id=1, source_target_pairs={{0,3},{1,0},{2,1},{3,2},{4,7},{5,4},{6,5},{7,6},{8,11},{9,8},{10,9... | collective-permute-start | bytes 884744 | tf_op jit(solution)/shard_map/ppermute | solution.py:215
  81.6 1.6 %collective-permute-start.17 = (bf16[288,512]{1,0:T(8,128)(2,1)S(1)}, bf16[288,512]{1,0:T(8,128)(2,1)S(1)}, u32[]{:S(2)}, u32[]{:S(2)}) collective-permute-start(bf16[288,512]{1,0:T(8,128)(2,1)S(1)} %constant_dynamic-update-slice_fusion.refs_0_), channel_id=1, source_target_pairs={{0,2},{1,3},{2,0},{3,1},{4,6},{5,7},{6,4},{7,5},{8,10},{9,11},{10,... | collective-permute-start | bytes 884744 | tf_op jit(solution)/shard_map/ppermute | solution.py:215
  83.2 0.8 shard_map.77.refs_2_
  84.0 3.1 %collective-permute-done.18.refs_0_ = bf16[288,512]{1,0:T(8,128)(2,1)S(1)} collective-permute-done((bf16[288,512]{1,0:T(8,128)(2,1)S(1)}, bf16[288,512]{1,0:T(8,128)(2,1)S(1)}, u32[]{:S(2)}, u32[]{:S(2)}) %collective-permute-start.18) | collective-permute-done | bytes 294944 | tf_op jit(solution)/shard_map/ppermute | solution.py:215
  87.1 1.5 %shard_map.78.refs_1_ = f32[288,1536]{1,0:T(8,128)S(1)} custom-call(bf16[2048,1536]{1,0:T(8,128)(2,1)S(1)} %bitcast.3, bf16[288,512]{1,0:T(8,128)(2,1)S(1)} %collective-permute-done.18.refs_0_, bf16[288,512]{1,0:T(8,128)(2,1)S(1)} %collective-permute-done.19.refs_1_, f32[288,1536]{1,0:T(8,128)S(1)} %shard_map.77.refs_2_), custom_call_target="tpu_custom_call" | custom-call | tf_op jit(solution)/shard_map/pallas_call | solution.py:182
  88.6 1.7 %collective-permute-done.17.refs_0_ = bf16[288,512]{1,0:T(8,128)(2,1)S(1)} collective-permute-done((bf16[288,512]{1,0:T(8,128)(2,1)S(1)}, bf16[288,512]{1,0:T(8,128)(2,1)S(1)}, u32[]{:S(2)}, u32[]{:S(2)}) %collective-permute-start.17) | collective-permute-done | bytes 294944 | tf_op jit(solution)/shard_map/ppermute | solution.py:215
  90.2 0.8 shard_map.79
  91.2 1.8 %collective-permute-done.20 = bf16[144,1536]{1,0:T(8,128)(2,1)S(1)} collective-permute-done((bf16[144,1536]{1,0:T(8,128)(2,1)S(1)}, bf16[144,1536]{1,0:T(8,128)(2,1)S(1)}, u32[]{:S(2)}, u32[]{:S(2)}) %collective-permute-start.20) | collective-permute-done | bytes 442400 | tf_op jit(solution)/shard_map/ppermute | solution.py:219
  93.0 0.9 add_convert_fusion
  (36 shorter events, 2.0 us)
Async XLA Ops:
  2.8 18.2 %collective-permute-start = (bf16[288,384]{1,0:T(8,128)(2,1)}, bf16[288,384]{1,0:T(8,128)(2,1)S(1)}, u32[]{:S(2)}, u32[]{:S(2)}) collective-permute-start(bf16[288,384]{1,0:T(8,128)(2,1)} %get-tuple-element.36), channel_id=1, source_target_pairs={{0,96},{4,224},{32,0},{36,128},{64,32},{68,160},{96,64},{100,192},... | collective-permute-start | bytes 663560 | tf_op jit(solution)/shard_map/ppermute | solution.py:205
  9.9 17.3 %collective-permute-start.1 = (bf16[288,384]{1,0:T(8,128)(2,1)}, bf16[288,384]{1,0:T(8,128)(2,1)S(1)}, u32[]{:S(2)}, u32[]{:S(2)}) collective-permute-start(bf16[288,384]{1,0:T(8,128)(2,1)} %get-tuple-element.37), channel_id=1, source_target_pairs={{0,64},{4,192},{32,96},{36,224},{64,0},{68,128},{96,32},{100,160},... | collective-permute-start | bytes 663560 | tf_op jit(solution)/shard_map/ppermute | solution.py:205
  10.4 19.3 %collective-permute-start.2 = (bf16[288,384]{1,0:T(8,128)(2,1)}, bf16[288,384]{1,0:T(8,128)(2,1)S(1)}, u32[]{:S(2)}, u32[]{:S(2)}) collective-permute-start(bf16[288,384]{1,0:T(8,128)(2,1)} %get-tuple-element.38), channel_id=1, source_target_pairs={{0,32},{4,160},{32,64},{36,192},{64,96},{68,224},{96,0},{100,128},... | collective-permute-start | bytes 663560 | tf_op jit(solution)/shard_map/ppermute | solution.py:205
  15.1 14.7 %collective-permute-start.3 = (bf16[288,384]{1,0:T(8,128)(2,1)}, bf16[288,384]{1,0:T(8,128)(2,1)S(1)}, u32[]{:S(2)}, u32[]{:S(2)}) collective-permute-start(bf16[288,384]{1,0:T(8,128)(2,1)} %get-tuple-element.39), channel_id=1, source_target_pairs={{0,0},{4,128},{32,32},{36,160},{64,64},{68,192},{96,96},{100,224},... | collective-permute-start | bytes 663560 | tf_op jit(solution)/shard_map/ppermute | solution.py:205
  29.9 14.2 %collective-permute-start.4 = (bf16[1152,256]{1,0:T(8,128)(2,1)S(1)}, bf16[1152,256]{1,0:T(8,128)(2,1)S(1)}, u32[]{:S(2)}, u32[]{:S(2)}) collective-permute-start(bf16[1152,256]{1,0:T(8,128)(2,1)S(1)} %pad_maximum_fusion.refs_4_), channel_id=1, source_target_pairs={{0,8},{8,16},{16,24},{24,0},{1,9},{9,17},{17,25},{25,1},{2,10},{10... | collective-permute-start | bytes 1769480 | tf_op jit(solution)/shard_map/ppermute | solution.py:215
  31.2 13.2 %collective-permute-start.6 = (bf16[1152,256]{1,0:T(8,128)(2,1)S(1)}, bf16[1152,256]{1,0:T(8,128)(2,1)S(1)}, u32[]{:S(2)}, u32[]{:S(2)}) collective-permute-start(bf16[1152,256]{1,0:T(8,128)(2,1)S(1)} %pad_maximum_fusion.refs_4_), channel_id=1, source_target_pairs={{0,24},{8,0},{16,8},{24,16},{1,25},{9,1},{17,9},{25,17},{2,26},{10... | collective-permute-start | bytes 1769480 | tf_op jit(solution)/shard_map/ppermute | solution.py:215
  32.6 15.4 %collective-permute-start.8 = (bf16[1152,256]{1,0:T(8,128)(2,1)S(1)}, bf16[1152,256]{1,0:T(8,128)(2,1)S(1)}, u32[]{:S(2)}, u32[]{:S(2)}) collective-permute-start(bf16[1152,256]{1,0:T(8,128)(2,1)S(1)} %pad_maximum_fusion.refs_4_), channel_id=1, source_target_pairs={{0,4},{4,0},{1,5},{5,1},{2,6},{6,2},{3,7},{7,3},{8,12},{12,8},{9,1... | collective-permute-start | bytes 1769480 | tf_op jit(solution)/shard_map/ppermute | solution.py:219
  32.6 50.6 %slice-start = ((s8[6291456]{0:T(1024)(128)(4,1)}), s8[4194304]{0:T(1024)(128)(4,1)S(1)}, s32[]{:S(2)}) async-start(s8[6291456]{0:T(1024)(128)(4,1)} %bitcast.2), calls=%async_computation | async-start | bytes 8388608
  44.4 3.6 %collective-permute-start.10 = (bf16[1152,256]{1,0:T(8,128)(2,1)S(1)}, bf16[1152,256]{1,0:T(8,128)(2,1)S(1)}, u32[]{:S(2)}, u32[]{:S(2)}) collective-permute-start(bf16[1152,256]{1,0:T(8,128)(2,1)S(1)} %collective-permute-done.6.refs_6_), channel_id=1, source_target_pairs={{0,4},{4,0},{1,5},{5,1},{2,6},{6,2},{3,7},{7,3},{8,12},{12,8},{9,1... | collective-permute-start | bytes 1769480 | tf_op jit(solution)/shard_map/ppermute | solution.py:219
  44.4 3.6 %collective-permute-start.9 = (bf16[1152,256]{1,0:T(8,128)(2,1)S(1)}, bf16[1152,256]{1,0:T(8,128)(2,1)S(1)}, u32[]{:S(2)}, u32[]{:S(2)}) collective-permute-start(bf16[1152,256]{1,0:T(8,128)(2,1)S(1)} %collective-permute-done.4.refs_5_), channel_id=1, source_target_pairs={{0,4},{4,0},{1,5},{5,1},{2,6},{6,2},{3,7},{7,3},{8,12},{12,8},{9,1... | collective-permute-start | bytes 1769480 | tf_op jit(solution)/shard_map/ppermute | solution.py:219
  44.9 11.6 %collective-permute-start.5 = (bf16[576,256]{1,0:T(8,128)(2,1)S(1)}, bf16[576,256]{1,0:T(8,128)(2,1)S(1)}, u32[]{:S(2)}, u32[]{:S(2)}) collective-permute-start(bf16[576,256]{1,0:T(8,128)(2,1)S(1)} %slice.28), channel_id=1, source_target_pairs={{0,8},{8,16},{16,24},{24,0},{1,9},{9,17},{17,25},{25,1},{2,10},{10... | collective-permute-start | bytes 884744 | tf_op jit(solution)/shard_map/ppermute | solution.py:215
  46.2 37.0 %slice-start.1 = ((s8[6291456]{0:T(1024)(128)(4,1)}), s8[2097152]{0:T(1024)(128)(4,1)S(1)}, s32[]{:S(2)}) async-start(s8[6291456]{0:T(1024)(128)(4,1)} %bitcast.2), calls=%async_computation.1 | async-start | bytes 4194304
  46.2 10.3 %collective-permute-start.7 = (bf16[576,256]{1,0:T(8,128)(2,1)S(1)}, bf16[576,256]{1,0:T(8,128)(2,1)S(1)}, u32[]{:S(2)}, u32[]{:S(2)}) collective-permute-start(bf16[576,256]{1,0:T(8,128)(2,1)S(1)} %slice.29), channel_id=1, source_target_pairs={{0,24},{8,0},{16,8},{24,16},{1,25},{9,1},{17,9},{25,17},{2,26},{10... | collective-permute-start | bytes 884744 | tf_op jit(solution)/shard_map/ppermute | solution.py:215
  56.5 1.8 %collective-permute-start.11 = (bf16[576,256]{1,0:T(8,128)(2,1)S(1)}, bf16[576,256]{1,0:T(8,128)(2,1)S(1)}, u32[]{:S(2)}, u32[]{:S(2)}) collective-permute-start(bf16[576,256]{1,0:T(8,128)(2,1)S(1)} %collective-permute-done.5.refs_4_), channel_id=1, source_target_pairs={{0,4},{4,0},{1,5},{5,1},{2,6},{6,2},{3,7},{7,3},{8,12},{12,8},{9,1... | collective-permute-start | bytes 884744 | tf_op jit(solution)/shard_map/ppermute | solution.py:219
  57.1 1.6 %collective-permute-start.12 = (bf16[576,256]{1,0:T(8,128)(2,1)S(1)}, bf16[576,256]{1,0:T(8,128)(2,1)S(1)}, u32[]{:S(2)}, u32[]{:S(2)}) collective-permute-start(bf16[576,256]{1,0:T(8,128)(2,1)S(1)} %collective-permute-done.7.refs_5_), channel_id=1, source_target_pairs={{0,4},{4,0},{1,5},{5,1},{2,6},{6,2},{3,7},{7,3},{8,12},{12,8},{9,1... | collective-permute-start | bytes 884744 | tf_op jit(solution)/shard_map/ppermute | solution.py:219
  63.1 11.5 %collective-permute-start.13 = (bf16[288,128]{1,0:T(8,128)(2,1)S(1)}, bf16[288,128]{1,0:T(8,128)(2,1)S(1)}, u32[]{:S(2)}, u32[]{:S(2)}) collective-permute-start(bf16[288,128]{1,0:T(8,128)(2,1)S(1)} %get-tuple-element.56), channel_id=1, source_target_pairs={{96,0},{224,4},{0,32},{128,36},{32,64},{160,68},{64,96},{192,100},... | collective-permute-start | bytes 221192 | tf_op jit(solution)/shard_map/ppermute | solution.py:209
  66.9 7.8 %collective-permute-start.14 = (bf16[288,128]{1,0:T(8,128)(2,1)S(1)}, bf16[288,128]{1,0:T(8,128)(2,1)S(1)}, u32[]{:S(2)}, u32[]{:S(2)}) collective-permute-start(bf16[288,128]{1,0:T(8,128)(2,1)S(1)} %get-tuple-element.57), channel_id=1, source_target_pairs={{64,0},{192,4},{96,32},{224,36},{0,64},{128,68},{32,96},{160,100},... | collective-permute-start | bytes 221192 | tf_op jit(solution)/shard_map/ppermute | solution.py:209
  66.9 7.8 %collective-permute-start.15 = (bf16[288,128]{1,0:T(8,128)(2,1)S(1)}, bf16[288,128]{1,0:T(8,128)(2,1)S(1)}, u32[]{:S(2)}, u32[]{:S(2)}) collective-permute-start(bf16[288,128]{1,0:T(8,128)(2,1)S(1)} %get-tuple-element.58), channel_id=1, source_target_pairs={{32,0},{160,4},{64,32},{192,36},{96,64},{224,68},{0,96},{128,100},... | collective-permute-start | bytes 221192 | tf_op jit(solution)/shard_map/ppermute | solution.py:209
  69.1 9.6 %collective-permute-start.16 = (bf16[288,128]{1,0:T(8,128)(2,1)S(1)}, bf16[288,128]{1,0:T(8,128)(2,1)S(1)}, u32[]{:S(2)}, u32[]{:S(2)}) collective-permute-start(bf16[288,128]{1,0:T(8,128)(2,1)S(1)} %get-tuple-element.59), channel_id=1, source_target_pairs={{0,0},{128,4},{32,32},{160,36},{64,64},{192,68},{96,96},{224,100},... | collective-permute-start | bytes 221192 | tf_op jit(solution)/shard_map/ppermute | solution.py:209
  78.7 8.4 %collective-permute-start.18 = (bf16[288,512]{1,0:T(8,128)(2,1)S(1)}, bf16[288,512]{1,0:T(8,128)(2,1)S(1)}, u32[]{:S(2)}, u32[]{:S(2)}) collective-permute-start(bf16[288,512]{1,0:T(8,128)(2,1)S(1)} %constant_dynamic-update-slice_fusion.refs_0_), channel_id=1, source_target_pairs={{0,1},{1,2},{2,3},{3,0},{4,5},{5,6},{6,7},{7,4},{8,9},{9,10},{10,1... | collective-permute-start | bytes 884744 | tf_op jit(solution)/shard_map/ppermute | solution.py:215
  80.1 7.0 %collective-permute-start.19 = (bf16[288,512]{1,0:T(8,128)(2,1)S(1)}, bf16[288,512]{1,0:T(8,128)(2,1)S(1)}, u32[]{:S(2)}, u32[]{:S(2)}) collective-permute-start(bf16[288,512]{1,0:T(8,128)(2,1)S(1)} %constant_dynamic-update-slice_fusion.refs_0_), channel_id=1, source_target_pairs={{0,3},{1,0},{2,1},{3,2},{4,7},{5,4},{6,5},{7,6},{8,11},{9,8},{10,9... | collective-permute-start | bytes 884744 | tf_op jit(solution)/shard_map/ppermute | solution.py:215
  81.6 8.6 %collective-permute-start.17 = (bf16[288,512]{1,0:T(8,128)(2,1)S(1)}, bf16[288,512]{1,0:T(8,128)(2,1)S(1)}, u32[]{:S(2)}, u32[]{:S(2)}) collective-permute-start(bf16[288,512]{1,0:T(8,128)(2,1)S(1)} %constant_dynamic-update-slice_fusion.refs_0_), channel_id=1, source_target_pairs={{0,2},{1,3},{2,0},{3,1},{4,6},{5,7},{6,4},{7,5},{8,10},{9,11},{10,... | collective-permute-start | bytes 884744 | tf_op jit(solution)/shard_map/ppermute | solution.py:215
  88.6 4.4 %copy-start = (bf16[144,1536]{1,0:T(8,128)(2,1)S(1)}, bf16[144,1536]{1,0:T(8,128)(2,1)}, u32[]{:S(2)}) copy-start(bf16[144,1536]{1,0:T(8,128)(2,1)} %param.12) | copy-start | bytes 1327108
  91.1 1.9 %collective-permute-start.20 = (bf16[144,1536]{1,0:T(8,128)(2,1)S(1)}, bf16[144,1536]{1,0:T(8,128)(2,1)S(1)}, u32[]{:S(2)}, u32[]{:S(2)}) collective-permute-start(bf16[144,1536]{1,0:T(8,128)(2,1)S(1)} %get-tuple-element.66), channel_id=1, source_target_pairs={{0,4},{4,0},{1,5},{5,1},{2,6},{6,2},{3,7},{7,3},{8,12},{12,8},{9,1... | collective-permute-start | bytes 1327112 | tf_op jit(solution)/shard_map/ppermute | solution.py:219

commit v6 on v5

--- a/solution.py
+++ b/solution.py
@@ -226,11 +226,12 @@
     held = [to_owner(ready[j], j) for j in range(HEADS)]
     own = jnp.concatenate([m[:, : 2 * DH] for m in held], axis=0)
     near, back = shift(own, "x", NX, 1), shift(own, "x", NX, -1)
-    state = flash(False, held, [own])
+    half = own.shape[0] // 2
+    state = flash(False, held, [own, swap(own[:half]), swap(own[half:])])
     half = own.shape[0] // 2
     far = [shift(near[:half], "x", NX, 1), shift(back[half:], "x", NX, -1)]
     near, back, *state = lax.optimization_barrier((near, back, *state))
-    state = flash(False, held, [swap(own), near, back, swap(near), swap(back)], state)
+    state = flash(False, held, [near, back, swap(near), swap(back)], state)
     *far, a, b, c = lax.optimization_barrier((*far, *state))
     attended = flash(True, held, far + [swap(p) for p in far], (a, b, c))
     mine = jnp.concatenate([from_owner(attended[j], j) for j in range(HEADS)], axis=1)

time: 94 us -> 92.8 us (0.987)
  waiting for transfers between devices: 33.2 us -> 31.1 us
    ppermute x7, waiting for transfers between devices: 14.2 us -> 10.4 us  [shift(): lax.ppermute(value, axis, [(i, (i + step) % size) for i in range(size)])]
    ppermute x6 -> x7, waiting for transfers between devices: 3.1 us -> 4.9 us  [swap(): return lax.ppermute(value, 'row', [(0, 1), (1, 0)])]
    ppermute x6 -> x7, starting transfers between devices: 1.56 us -> 1.96 us  [swap(): return lax.ppermute(value, 'row', [(0, 1), (1, 0)])]
  transfers between devices with their start and end apart: 21 -> 22, of which waited for: 12 -> 14; matrix products, arithmetic and copies ran while one was open for 0% -> 0% of each run, Pallas kernels for 14% -> 15%
where the time goes in v6:
time: 92.8 us; the launch traced here: 92.7 us
  starting transfers between devices  39 us (42%)
  waiting for transfers between devices  31.1 us (34%)
  Pallas kernels  21.3 us (23%)
  other arithmetic  0.98 us (1%)
    pallas_call x3, Pallas kernels, flash(): pl.pallas_call(functools.partial(flash_kernel, not state, last, nq, n, mo...  15.4 us
    ppermute x4, starting transfers between devices, to_owner(): return lax.ppermute(value, ('z', 'row'), owner_pairs(j))  15 us
    ppermute x4, waiting for transfers between devices, to_owner(): return lax.ppermute(value, ('z', 'row'), owner_pairs(j))  11.9 us
    ppermute x4, starting transfers between devices, from_owner(): lax.ppermute(value, ('z', 'row'), [(b, a) for a, b in owner_pairs(j)])  11.7 us
    ppermute x7, waiting for transfers between devices, shift(): lax.ppermute(value, axis, [(i, (i + step) % size) for i in range(size)])  10.4 us
    ppermute x7, starting transfers between devices, shift(): lax.ppermute(value, axis, [(i, (i + step) % size) for i in range(size)])  10.2 us
    ppermute x7, waiting for transfers between devices, swap(): return lax.ppermute(value, 'row', [(0, 1), (1, 0)])  4.9 us
    ppermute x4, waiting for transfers between devices, from_owner(): lax.ppermute(value, ('z', 'row'), [(b, a) for a, b in owner_pairs(j)])  3.85 us
  transfers between devices with their start and end apart: 22, of which 14 were waited for; matrix products, arithmetic and copies ran while one was open for 0% of the time, Pallas kernels for 15%

profile of v6, /device:TPU:1, one launch (start us, length us, event | category | flops | bytes accessed | tf_op | source)
XLA Modules:
  0.0 92.7 jit_solution(14991545897805112266)
XLA Ops:
  0.0 2.8 %shard_map.73 = (bf16[288,384]{1,0:T(8,128)(2,1)}, bf16[288,384]{1,0:T(8,128)(2,1)}, bf16[288,384]{1,0:T(8,128)(2,1)}, bf16[288,384]{1,0:T(8,128)(2,1)}) custom-call(bf16[288,512]{1,0:T(8,128)(2,1)} %refs_0_.1, f32[1,512]{1,0:T(1,128)} %bitcast.4, bf16[288,512]{1,0:T(8,128)(2,1)} %refs_2_.1, bf16[288,512]{1,0:T(8,128)(2,1)} %refs_3_.1, f32[1,512]{1,0:T(1,128)} %bitcast.5), custom_call_target="tpu_custom_call" | custom-call | tf_op jit(solution)/shard_map/pallas_call | solution.py:59
  2.8 7.0 %collective-permute-start = (bf16[288,384]{1,0:T(8,128)(2,1)}, bf16[288,384]{1,0:T(8,128)(2,1)S(1)}, u32[]{:S(2)}, u32[]{:S(2)}) collective-permute-start(bf16[288,384]{1,0:T(8,128)(2,1)} %get-tuple-element.36), channel_id=1, source_target_pairs={{0,96},{4,224},{32,0},{36,128},{64,32},{68,160},{96,64},{100,192},... | collective-permute-start | bytes 663560 | tf_op jit(solution)/shard_map/ppermute | solution.py:205
  10.4 4.7 %collective-permute-start.2 = (bf16[288,384]{1,0:T(8,128)(2,1)}, bf16[288,384]{1,0:T(8,128)(2,1)S(1)}, u32[]{:S(2)}, u32[]{:S(2)}) collective-permute-start(bf16[288,384]{1,0:T(8,128)(2,1)} %get-tuple-element.38), channel_id=1, source_target_pairs={{0,32},{4,160},{32,64},{36,192},{64,96},{68,224},{96,0},{100,128},... | collective-permute-start | bytes 663560 | tf_op jit(solution)/shard_map/ppermute | solution.py:205
  15.1 2.8 %collective-permute-start.3 = (bf16[288,384]{1,0:T(8,128)(2,1)}, bf16[288,384]{1,0:T(8,128)(2,1)S(1)}, u32[]{:S(2)}, u32[]{:S(2)}) collective-permute-start(bf16[288,384]{1,0:T(8,128)(2,1)} %get-tuple-element.39), channel_id=1, source_target_pairs={{0,0},{4,128},{32,32},{36,160},{64,64},{68,192},{96,96},{100,224},... | collective-permute-start | bytes 663560 | tf_op jit(solution)/shard_map/ppermute | solution.py:205
  17.9 3.2 %collective-permute-done.refs_0_ = bf16[288,384]{1,0:T(8,128)(2,1)S(1)} collective-permute-done((bf16[288,384]{1,0:T(8,128)(2,1)}, bf16[288,384]{1,0:T(8,128)(2,1)S(1)}, u32[]{:S(2)}, u32[]{:S(2)}) %collective-permute-start) | collective-permute-done | bytes 221216 | tf_op jit(solution)/shard_map/ppermute | solution.py:205
  21.1 6.1 %collective-permute-done.1.refs_1_ = bf16[288,384]{1,0:T(8,128)(2,1)S(1)} collective-permute-done((bf16[288,384]{1,0:T(8,128)(2,1)}, bf16[288,384]{1,0:T(8,128)(2,1)S(1)}, u32[]{:S(2)}, u32[]{:S(2)}) %collective-permute-start.1) | collective-permute-done | bytes 221216 | tf_op jit(solution)/shard_map/ppermute | solution.py:205
  27.2 2.5 %collective-permute-done.2.refs_2_ = bf16[288,384]{1,0:T(8,128)(2,1)S(1)} collective-permute-done((bf16[288,384]{1,0:T(8,128)(2,1)}, bf16[288,384]{1,0:T(8,128)(2,1)S(1)}, u32[]{:S(2)}, u32[]{:S(2)}) %collective-permute-start.2) | collective-permute-done | bytes 221216 | tf_op jit(solution)/shard_map/ppermute | solution.py:205
  29.9 1.3 %collective-permute-start.4 = (bf16[1152,256]{1,0:T(8,128)(2,1)S(1)}, bf16[1152,256]{1,0:T(8,128)(2,1)S(1)}, u32[]{:S(2)}, u32[]{:S(2)}) collective-permute-start(bf16[1152,256]{1,0:T(8,128)(2,1)S(1)} %pad_maximum_fusion.refs_4_), channel_id=1, source_target_pairs={{0,8},{8,16},{16,24},{24,0},{1,9},{9,17},{17,25},{25,1},{2,10},{10... | collective-permute-start | bytes 1769480 | tf_op jit(solution)/shard_map/ppermute | solution.py:215
  31.1 1.5 %collective-permute-start.6 = (bf16[1152,256]{1,0:T(8,128)(2,1)S(1)}, bf16[1152,256]{1,0:T(8,128)(2,1)S(1)}, u32[]{:S(2)}, u32[]{:S(2)}) collective-permute-start(bf16[1152,256]{1,0:T(8,128)(2,1)S(1)} %pad_maximum_fusion.refs_4_), channel_id=1, source_target_pairs={{0,24},{8,0},{16,8},{24,16},{1,25},{9,1},{17,9},{25,17},{2,26},{10... | collective-permute-start | bytes 1769480 | tf_op jit(solution)/shard_map/ppermute | solution.py:215
  33.3 1.1 %collective-permute-done.8.refs_5_ = bf16[576,256]{1,0:T(8,128)(2,1)S(1)} collective-permute-done((bf16[576,256]{1,0:T(8,128)(2,1)S(1)}, bf16[576,256]{1,0:T(8,128)(2,1)S(1)}, u32[]{:S(2)}, u32[]{:S(2)}) %collective-permute-start.8) | collective-permute-done | bytes 294944 | tf_op jit(solution)/shard_map/ppermute | solution.py:219
  34.8 4.0 %shard_map.74 = (f32[1152,128]{1,0:T(8,128)S(1)}, f32[1152,128]{1,0:T(8,128)S(1)}, f32[1152,128]{1,0:T(8,128)S(1)}) custom-call(bf16[288,384]{1,0:T(8,128)(2,1)S(1)} %collective-permute-done.refs_0_, bf16[288,384]{1,0:T(8,128)(2,1)S(1)} %collective-permute-done.1.refs_1_, bf16[288,384]{1,0:T(8,128)(2,1)S(1)} %collective-permute-done.2.refs_2_, ...), custom_call_target="tpu_custom_call" | custom-call | flops 1000 | bytes 1000 | tf_op jit(solution)/shard_map/pallas_call | solution.py:130
  38.8 5.3 %collective-permute-done.4.refs_4_ = bf16[1152,256]{1,0:T(8,128)(2,1)S(1)} collective-permute-done((bf16[1152,256]{1,0:T(8,128)(2,1)S(1)}, bf16[1152,256]{1,0:T(8,128)(2,1)S(1)}, u32[]{:S(2)}, u32[]{:S(2)}) %collective-permute-start.4) | collective-permute-done | bytes 589856 | tf_op jit(solution)/shard_map/ppermute | solution.py:215
  44.9 1.3 %collective-permute-start.5 = (bf16[576,256]{1,0:T(8,128)(2,1)S(1)}, bf16[576,256]{1,0:T(8,128)(2,1)S(1)}, u32[]{:S(2)}, u32[]{:S(2)}) collective-permute-start(bf16[576,256]{1,0:T(8,128)(2,1)S(1)} %slice.32), channel_id=1, source_target_pairs={{0,8},{8,16},{16,24},{24,0},{1,9},{9,17},{17,25},{25,1},{2,10},{10... | collective-permute-start | bytes 884744 | tf_op jit(solution)/shard_map/ppermute | solution.py:215
  46.2 1.7 %collective-permute-start.7 = (bf16[576,256]{1,0:T(8,128)(2,1)S(1)}, bf16[576,256]{1,0:T(8,128)(2,1)S(1)}, u32[]{:S(2)}, u32[]{:S(2)}) collective-permute-start(bf16[576,256]{1,0:T(8,128)(2,1)S(1)} %slice.33), channel_id=1, source_target_pairs={{0,24},{8,0},{16,8},{24,16},{1,25},{9,1},{17,9},{25,17},{2,26},{10... | collective-permute-start | bytes 884744 | tf_op jit(solution)/shard_map/ppermute | solution.py:215
  48.0 7.1 %shard_map.75 = (f32[1152,128]{1,0:T(8,128)S(1)}, f32[1152,128]{1,0:T(8,128)S(1)}, f32[1152,128]{1,0:T(8,128)S(1)}) custom-call(bf16[288,384]{1,0:T(8,128)(2,1)S(1)} %collective-permute-done.refs_0_, bf16[288,384]{1,0:T(8,128)(2,1)S(1)} %collective-permute-done.1.refs_1_, bf16[288,384]{1,0:T(8,128)(2,1)S(1)} %collective-permute-done.2.refs_2_, ...), custom_call_target="tpu_custom_call" | custom-call | flops 1000 | bytes 1000 | tf_op jit(solution)/shard_map/pallas_call | solution.py:130
  55.1 0.8 collective-permute-start.12
  55.9 1.2 %collective-permute-done.12.refs_6_ = bf16[576,256]{1,0:T(8,128)(2,1)S(1)} collective-permute-done((bf16[576,256]{1,0:T(8,128)(2,1)S(1)}, bf16[576,256]{1,0:T(8,128)(2,1)S(1)}, u32[]{:S(2)}, u32[]{:S(2)}) %collective-permute-start.12) | collective-permute-done | bytes 294944 | tf_op jit(solution)/shard_map/ppermute | solution.py:219
  57.5 4.2 %shard_map.76 = (bf16[288,128]{1,0:T(8,128)(2,1)S(1)}, bf16[288,128]{1,0:T(8,128)(2,1)S(1)}, bf16[288,128]{1,0:T(8,128)(2,1)S(1)}, bf16[288,128]{1,0:T(8,128)(2,1)S(1)}) custom-call(bf16[288,384]{1,0:T(8,128)(2,1)S(1)} %collective-permute-done.refs_0_, bf16[288,384]{1,0:T(8,128)(2,1)S(1)} %collective-permute-done.1.refs_1_, ...), custom_call_target="tpu_custom_call" | custom-call | flops 1000 | bytes 1000 | tf_op jit(solution)/shard_map/pallas_call | solution.py:130
  61.8 3.9 %collective-permute-start.14 = (bf16[288,128]{1,0:T(8,128)(2,1)S(1)}, bf16[288,128]{1,0:T(8,128)(2,1)S(1)}, u32[]{:S(2)}, u32[]{:S(2)}) collective-permute-start(bf16[288,128]{1,0:T(8,128)(2,1)S(1)} %get-tuple-element.56), channel_id=1, source_target_pairs={{96,0},{224,4},{0,32},{128,36},{32,64},{160,68},{64,96},{192,100},... | collective-permute-start | bytes 221192 | tf_op jit(solution)/shard_map/ppermute | solution.py:209
  65.7 2.2 %collective-permute-start.16 = (bf16[288,128]{1,0:T(8,128)(2,1)S(1)}, bf16[288,128]{1,0:T(8,128)(2,1)S(1)}, u32[]{:S(2)}, u32[]{:S(2)}) collective-permute-start(bf16[288,128]{1,0:T(8,128)(2,1)S(1)} %get-tuple-element.58), channel_id=1, source_target_pairs={{32,0},{160,4},{64,32},{192,36},{96,64},{224,68},{0,96},{128,100},... | collective-permute-start | bytes 221192 | tf_op jit(solution)/shard_map/ppermute | solution.py:209
  67.8 5.7 %collective-permute-start.17 = (bf16[288,128]{1,0:T(8,128)(2,1)S(1)}, bf16[288,128]{1,0:T(8,128)(2,1)S(1)}, u32[]{:S(2)}, u32[]{:S(2)}) collective-permute-start(bf16[288,128]{1,0:T(8,128)(2,1)S(1)} %get-tuple-element.59), channel_id=1, source_target_pairs={{0,0},{128,4},{32,32},{160,36},{64,64},{192,68},{96,96},{224,100},... | collective-permute-start | bytes 221192 | tf_op jit(solution)/shard_map/ppermute | solution.py:209
  73.6 3.8 %collective-permute-done.17 = bf16[288,128]{1,0:T(8,128)(2,1)S(1)} collective-permute-done((bf16[288,128]{1,0:T(8,128)(2,1)S(1)}, bf16[288,128]{1,0:T(8,128)(2,1)S(1)}, u32[]{:S(2)}, u32[]{:S(2)}) %collective-permute-start.17) | collective-permute-done | bytes 73760 | tf_op jit(solution)/shard_map/ppermute | solution.py:209
  77.5 1.4 %collective-permute-start.19 = (bf16[288,512]{1,0:T(8,128)(2,1)S(1)}, bf16[288,512]{1,0:T(8,128)(2,1)S(1)}, u32[]{:S(2)}, u32[]{:S(2)}) collective-permute-start(bf16[288,512]{1,0:T(8,128)(2,1)S(1)} %constant_dynamic-update-slice_fusion.refs_0_), channel_id=1, source_target_pairs={{0,1},{1,2},{2,3},{3,0},{4,5},{5,6},{6,7},{7,4},{8,9},{9,10},{10,1... | collective-permute-start | bytes 884744 | tf_op jit(solution)/shard_map/ppermute | solution.py:215
  78.9 1.5 %collective-permute-start.20 = (bf16[288,512]{1,0:T(8,128)(2,1)S(1)}, bf16[288,512]{1,0:T(8,128)(2,1)S(1)}, u32[]{:S(2)}, u32[]{:S(2)}) collective-permute-start(bf16[288,512]{1,0:T(8,128)(2,1)S(1)} %constant_dynamic-update-slice_fusion.refs_0_), channel_id=1, source_target_pairs={{0,3},{1,0},{2,1},{3,2},{4,7},{5,4},{6,5},{7,6},{8,11},{9,8},{10,9... | collective-permute-start | bytes 884744 | tf_op jit(solution)/shard_map/ppermute | solution.py:215
  80.4 1.6 %collective-permute-start.18 = (bf16[288,512]{1,0:T(8,128)(2,1)S(1)}, bf16[288,512]{1,0:T(8,128)(2,1)S(1)}, u32[]{:S(2)}, u32[]{:S(2)}) collective-permute-start(bf16[288,512]{1,0:T(8,128)(2,1)S(1)} %constant_dynamic-update-slice_fusion.refs_0_), channel_id=1, source_target_pairs={{0,2},{1,3},{2,0},{3,1},{4,6},{5,7},{6,4},{7,5},{8,10},{9,11},{10,... | collective-permute-start | bytes 884744 | tf_op jit(solution)/shard_map/ppermute | solution.py:215
  81.9 0.8 shard_map.77.refs_2_
  82.8 3.2 %collective-permute-done.19.refs_0_ = bf16[288,512]{1,0:T(8,128)(2,1)S(1)} collective-permute-done((bf16[288,512]{1,0:T(8,128)(2,1)S(1)}, bf16[288,512]{1,0:T(8,128)(2,1)S(1)}, u32[]{:S(2)}, u32[]{:S(2)}) %collective-permute-start.19) | collective-permute-done | bytes 294944 | tf_op jit(solution)/shard_map/ppermute | solution.py:215
  85.9 1.5 %shard_map.78.refs_1_ = f32[288,1536]{1,0:T(8,128)S(1)} custom-call(bf16[2048,1536]{1,0:T(8,128)(2,1)S(1)} %bitcast.3, bf16[288,512]{1,0:T(8,128)(2,1)S(1)} %collective-permute-done.19.refs_0_, bf16[288,512]{1,0:T(8,128)(2,1)S(1)} %collective-permute-done.20.refs_1_, f32[288,1536]{1,0:T(8,128)S(1)} %shard_map.77.refs_2_), custom_call_target="tpu_custom_call" | custom-call | tf_op jit(solution)/shard_map/pallas_call | solution.py:182
  87.4 1.7 %collective-permute-done.18.refs_0_ = bf16[288,512]{1,0:T(8,128)(2,1)S(1)} collective-permute-done((bf16[288,512]{1,0:T(8,128)(2,1)S(1)}, bf16[288,512]{1,0:T(8,128)(2,1)S(1)}, u32[]{:S(2)}, u32[]{:S(2)}) %collective-permute-start.18) | collective-permute-done | bytes 294944 | tf_op jit(solution)/shard_map/ppermute | solution.py:215
  89.1 0.8 shard_map.79
  90.0 1.8 %collective-permute-done.21 = bf16[144,1536]{1,0:T(8,128)(2,1)S(1)} collective-permute-done((bf16[144,1536]{1,0:T(8,128)(2,1)S(1)}, bf16[144,1536]{1,0:T(8,128)(2,1)S(1)}, u32[]{:S(2)}, u32[]{:S(2)}) %collective-permute-start.21) | collective-permute-done | bytes 442400 | tf_op jit(solution)/shard_map/ppermute | solution.py:219
  91.8 0.9 add_convert_fusion
  (40 shorter events, 3.2 us)
Async XLA Ops:
  2.8 18.2 %collective-permute-start = (bf16[288,384]{1,0:T(8,128)(2,1)}, bf16[288,384]{1,0:T(8,128)(2,1)S(1)}, u32[]{:S(2)}, u32[]{:S(2)}) collective-permute-start(bf16[288,384]{1,0:T(8,128)(2,1)} %get-tuple-element.36), channel_id=1, source_target_pairs={{0,96},{4,224},{32,0},{36,128},{64,32},{68,160},{96,64},{100,192},... | collective-permute-start | bytes 663560 | tf_op jit(solution)/shard_map/ppermute | solution.py:205
  9.9 17.3 %collective-permute-start.1 = (bf16[288,384]{1,0:T(8,128)(2,1)}, bf16[288,384]{1,0:T(8,128)(2,1)S(1)}, u32[]{:S(2)}, u32[]{:S(2)}) collective-permute-start(bf16[288,384]{1,0:T(8,128)(2,1)} %get-tuple-element.37), channel_id=1, source_target_pairs={{0,64},{4,192},{32,96},{36,224},{64,0},{68,128},{96,32},{100,160},... | collective-permute-start | bytes 663560 | tf_op jit(solution)/shard_map/ppermute | solution.py:205
  10.4 19.3 %collective-permute-start.2 = (bf16[288,384]{1,0:T(8,128)(2,1)}, bf16[288,384]{1,0:T(8,128)(2,1)S(1)}, u32[]{:S(2)}, u32[]{:S(2)}) collective-permute-start(bf16[288,384]{1,0:T(8,128)(2,1)} %get-tuple-element.38), channel_id=1, source_target_pairs={{0,32},{4,160},{32,64},{36,192},{64,96},{68,224},{96,0},{100,128},... | collective-permute-start | bytes 663560 | tf_op jit(solution)/shard_map/ppermute | solution.py:205
  15.1 14.7 %collective-permute-start.3 = (bf16[288,384]{1,0:T(8,128)(2,1)}, bf16[288,384]{1,0:T(8,128)(2,1)S(1)}, u32[]{:S(2)}, u32[]{:S(2)}) collective-permute-start(bf16[288,384]{1,0:T(8,128)(2,1)} %get-tuple-element.39), channel_id=1, source_target_pairs={{0,0},{4,128},{32,32},{36,160},{64,64},{68,192},{96,96},{100,224},... | collective-permute-start | bytes 663560 | tf_op jit(solution)/shard_map/ppermute | solution.py:205
  29.9 14.2 %collective-permute-start.4 = (bf16[1152,256]{1,0:T(8,128)(2,1)S(1)}, bf16[1152,256]{1,0:T(8,128)(2,1)S(1)}, u32[]{:S(2)}, u32[]{:S(2)}) collective-permute-start(bf16[1152,256]{1,0:T(8,128)(2,1)S(1)} %pad_maximum_fusion.refs_4_), channel_id=1, source_target_pairs={{0,8},{8,16},{16,24},{24,0},{1,9},{9,17},{17,25},{25,1},{2,10},{10... | collective-permute-start | bytes 1769480 | tf_op jit(solution)/shard_map/ppermute | solution.py:215
  31.1 13.2 %collective-permute-start.6 = (bf16[1152,256]{1,0:T(8,128)(2,1)S(1)}, bf16[1152,256]{1,0:T(8,128)(2,1)S(1)}, u32[]{:S(2)}, u32[]{:S(2)}) collective-permute-start(bf16[1152,256]{1,0:T(8,128)(2,1)S(1)} %pad_maximum_fusion.refs_4_), channel_id=1, source_target_pairs={{0,24},{8,0},{16,8},{24,16},{1,25},{9,1},{17,9},{25,17},{2,26},{10... | collective-permute-start | bytes 1769480 | tf_op jit(solution)/shard_map/ppermute | solution.py:215
  32.7 1.7 %collective-permute-start.8 = (bf16[576,256]{1,0:T(8,128)(2,1)S(1)}, bf16[576,256]{1,0:T(8,128)(2,1)S(1)}, u32[]{:S(2)}, u32[]{:S(2)}) collective-permute-start(bf16[576,256]{1,0:T(8,128)(2,1)S(1)} %pad_maximum_fusion.1), channel_id=1, source_target_pairs={{0,4},{4,0},{1,5},{5,1},{2,6},{6,2},{3,7},{7,3},{8,12},{12,8},{9,1... | collective-permute-start | bytes 884744 | tf_op jit(solution)/shard_map/ppermute | solution.py:219
  32.8 2.0 %collective-permute-start.9 = (bf16[576,256]{1,0:T(8,128)(2,1)S(1)}, bf16[576,256]{1,0:T(8,128)(2,1)S(1)}, u32[]{:S(2)}, u32[]{:S(2)}) collective-permute-start(bf16[576,256]{1,0:T(8,128)(2,1)S(1)} %pad_maximum_fusion.2), channel_id=1, source_target_pairs={{0,4},{4,0},{1,5},{5,1},{2,6},{6,2},{3,7},{7,3},{8,12},{12,8},{9,1... | collective-permute-start | bytes 884744 | tf_op jit(solution)/shard_map/ppermute | solution.py:219
  34.8 47.2 %slice-start = ((s8[6291456]{0:T(1024)(128)(4,1)}), s8[4194304]{0:T(1024)(128)(4,1)S(1)}, s32[]{:S(2)}) async-start(s8[6291456]{0:T(1024)(128)(4,1)} %bitcast.2), calls=%async_computation | async-start | bytes 8388608
  44.4 3.6 %collective-permute-start.10 = (bf16[1152,256]{1,0:T(8,128)(2,1)S(1)}, bf16[1152,256]{1,0:T(8,128)(2,1)S(1)}, u32[]{:S(2)}, u32[]{:S(2)}) collective-permute-start(bf16[1152,256]{1,0:T(8,128)(2,1)S(1)} %collective-permute-done.4.refs_4_), channel_id=1, source_target_pairs={{0,4},{4,0},{1,5},{5,1},{2,6},{6,2},{3,7},{7,3},{8,12},{12,8},{9,1... | collective-permute-start | bytes 1769480 | tf_op jit(solution)/shard_map/ppermute | solution.py:219
  44.4 3.6 %collective-permute-start.11 = (bf16[1152,256]{1,0:T(8,128)(2,1)S(1)}, bf16[1152,256]{1,0:T(8,128)(2,1)S(1)}, u32[]{:S(2)}, u32[]{:S(2)}) collective-permute-start(bf16[1152,256]{1,0:T(8,128)(2,1)S(1)} %collective-permute-done.6.refs_5_), channel_id=1, source_target_pairs={{0,4},{4,0},{1,5},{5,1},{2,6},{6,2},{3,7},{7,3},{8,12},{12,8},{9,1... | collective-permute-start | bytes 1769480 | tf_op jit(solution)/shard_map/ppermute | solution.py:219
  44.9 10.2 %collective-permute-start.5 = (bf16[576,256]{1,0:T(8,128)(2,1)S(1)}, bf16[576,256]{1,0:T(8,128)(2,1)S(1)}, u32[]{:S(2)}, u32[]{:S(2)}) collective-permute-start(bf16[576,256]{1,0:T(8,128)(2,1)S(1)} %slice.32), channel_id=1, source_target_pairs={{0,8},{8,16},{16,24},{24,0},{1,9},{9,17},{17,25},{25,1},{2,10},{10... | collective-permute-start | bytes 884744 | tf_op jit(solution)/shard_map/ppermute | solution.py:215
  46.2 35.7 %slice-start.1 = ((s8[6291456]{0:T(1024)(128)(4,1)}), s8[2097152]{0:T(1024)(128)(4,1)S(1)}, s32[]{:S(2)}) async-start(s8[6291456]{0:T(1024)(128)(4,1)} %bitcast.2), calls=%async_computation.1 | async-start | bytes 4194304
  46.2 8.9 %collective-permute-start.7 = (bf16[576,256]{1,0:T(8,128)(2,1)S(1)}, bf16[576,256]{1,0:T(8,128)(2,1)S(1)}, u32[]{:S(2)}, u32[]{:S(2)}) collective-permute-start(bf16[576,256]{1,0:T(8,128)(2,1)S(1)} %slice.33), channel_id=1, source_target_pairs={{0,24},{8,0},{16,8},{24,16},{1,25},{9,1},{17,9},{25,17},{2,26},{10... | collective-permute-start | bytes 884744 | tf_op jit(solution)/shard_map/ppermute | solution.py:215
  55.1 2.0 %collective-permute-start.12 = (bf16[576,256]{1,0:T(8,128)(2,1)S(1)}, bf16[576,256]{1,0:T(8,128)(2,1)S(1)}, u32[]{:S(2)}, u32[]{:S(2)}) collective-permute-start(bf16[576,256]{1,0:T(8,128)(2,1)S(1)} %collective-permute-done.5.refs_4_), channel_id=1, source_target_pairs={{0,4},{4,0},{1,5},{5,1},{2,6},{6,2},{3,7},{7,3},{8,12},{12,8},{9,1... | collective-permute-start | bytes 884744 | tf_op jit(solution)/shard_map/ppermute | solution.py:219
  55.9 1.6 %collective-permute-start.13 = (bf16[576,256]{1,0:T(8,128)(2,1)S(1)}, bf16[576,256]{1,0:T(8,128)(2,1)S(1)}, u32[]{:S(2)}, u32[]{:S(2)}) collective-permute-start(bf16[576,256]{1,0:T(8,128)(2,1)S(1)} %collective-permute-done.7.refs_5_), channel_id=1, source_target_pairs={{0,4},{4,0},{1,5},{5,1},{2,6},{6,2},{3,7},{7,3},{8,12},{12,8},{9,1... | collective-permute-start | bytes 884744 | tf_op jit(solution)/shard_map/ppermute | solution.py:219
  61.8 11.8 %collective-permute-start.14 = (bf16[288,128]{1,0:T(8,128)(2,1)S(1)}, bf16[288,128]{1,0:T(8,128)(2,1)S(1)}, u32[]{:S(2)}, u32[]{:S(2)}) collective-permute-start(bf16[288,128]{1,0:T(8,128)(2,1)S(1)} %get-tuple-element.56), channel_id=1, source_target_pairs={{96,0},{224,4},{0,32},{128,36},{32,64},{160,68},{64,96},{192,100},... | collective-permute-start | bytes 221192 | tf_op jit(solution)/shard_map/ppermute | solution.py:209
  65.7 7.9 %collective-permute-start.15 = (bf16[288,128]{1,0:T(8,128)(2,1)S(1)}, bf16[288,128]{1,0:T(8,128)(2,1)S(1)}, u32[]{:S(2)}, u32[]{:S(2)}) collective-permute-start(bf16[288,128]{1,0:T(8,128)(2,1)S(1)} %get-tuple-element.57), channel_id=1, source_target_pairs={{64,0},{192,4},{96,32},{224,36},{0,64},{128,68},{32,96},{160,100},... | collective-permute-start | bytes 221192 | tf_op jit(solution)/shard_map/ppermute | solution.py:209
  65.7 7.9 %collective-permute-start.16 = (bf16[288,128]{1,0:T(8,128)(2,1)S(1)}, bf16[288,128]{1,0:T(8,128)(2,1)S(1)}, u32[]{:S(2)}, u32[]{:S(2)}) collective-permute-start(bf16[288,128]{1,0:T(8,128)(2,1)S(1)} %get-tuple-element.58), channel_id=1, source_target_pairs={{32,0},{160,4},{64,32},{192,36},{96,64},{224,68},{0,96},{128,100},... | collective-permute-start | bytes 221192 | tf_op jit(solution)/shard_map/ppermute | solution.py:209
  67.8 9.6 %collective-permute-start.17 = (bf16[288,128]{1,0:T(8,128)(2,1)S(1)}, bf16[288,128]{1,0:T(8,128)(2,1)S(1)}, u32[]{:S(2)}, u32[]{:S(2)}) collective-permute-start(bf16[288,128]{1,0:T(8,128)(2,1)S(1)} %get-tuple-element.59), channel_id=1, source_target_pairs={{0,0},{128,4},{32,32},{160,36},{64,64},{192,68},{96,96},{224,100},... | collective-permute-start | bytes 221192 | tf_op jit(solution)/shard_map/ppermute | solution.py:209
  77.5 8.5 %collective-permute-start.19 = (bf16[288,512]{1,0:T(8,128)(2,1)S(1)}, bf16[288,512]{1,0:T(8,128)(2,1)S(1)}, u32[]{:S(2)}, u32[]{:S(2)}) collective-permute-start(bf16[288,512]{1,0:T(8,128)(2,1)S(1)} %constant_dynamic-update-slice_fusion.refs_0_), channel_id=1, source_target_pairs={{0,1},{1,2},{2,3},{3,0},{4,5},{5,6},{6,7},{7,4},{8,9},{9,10},{10,1... | collective-permute-start | bytes 884744 | tf_op jit(solution)/shard_map/ppermute | solution.py:215
  78.9 7.1 %collective-permute-start.20 = (bf16[288,512]{1,0:T(8,128)(2,1)S(1)}, bf16[288,512]{1,0:T(8,128)(2,1)S(1)}, u32[]{:S(2)}, u32[]{:S(2)}) collective-permute-start(bf16[288,512]{1,0:T(8,128)(2,1)S(1)} %constant_dynamic-update-slice_fusion.refs_0_), channel_id=1, source_target_pairs={{0,3},{1,0},{2,1},{3,2},{4,7},{5,4},{6,5},{7,6},{8,11},{9,8},{10,9... | collective-permute-start | bytes 884744 | tf_op jit(solution)/shard_map/ppermute | solution.py:215
  80.4 8.7 %collective-permute-start.18 = (bf16[288,512]{1,0:T(8,128)(2,1)S(1)}, bf16[288,512]{1,0:T(8,128)(2,1)S(1)}, u32[]{:S(2)}, u32[]{:S(2)}) collective-permute-start(bf16[288,512]{1,0:T(8,128)(2,1)S(1)} %constant_dynamic-update-slice_fusion.refs_0_), channel_id=1, source_target_pairs={{0,2},{1,3},{2,0},{3,1},{4,6},{5,7},{6,4},{7,5},{8,10},{9,11},{10,... | collective-permute-start | bytes 884744 | tf_op jit(solution)/shard_map/ppermute | solution.py:215
  87.4 4.4 %copy-start = (bf16[144,1536]{1,0:T(8,128)(2,1)S(1)}, bf16[144,1536]{1,0:T(8,128)(2,1)}, u32[]{:S(2)}) copy-start(bf16[144,1536]{1,0:T(8,128)(2,1)} %param.12) | copy-start | bytes 1327108
  89.9 1.9 %collective-permute-start.21 = (bf16[144,1536]{1,0:T(8,128)(2,1)S(1)}, bf16[144,1536]{1,0:T(8,128)(2,1)S(1)}, u32[]{:S(2)}, u32[]{:S(2)}) collective-permute-start(bf16[144,1536]{1,0:T(8,128)(2,1)S(1)} %get-tuple-element.66), channel_id=1, source_target_pairs={{0,4},{4,0},{1,5},{5,1},{2,6},{6,2},{3,7},{7,3},{8,12},{12,8},{9,1... | collective-permute-start | bytes 1327112 | tf_op jit(solution)/shard_map/ppermute | solution.py:219

commit v7 on v6

--- a/solution.py
+++ b/solution.py
@@ -140,9 +140,10 @@
 def project_kernel(steps, first, last, w_hbm, *refs):
     n = len(steps)
     blocks, refs = refs[:n], refs[n:]
-    if not first:
-        acc_ref, refs = refs[0], refs[1:]
-    outs, (weight, tokens, sems) = refs[: 1 + last], refs[1 + last :]
+    acc_ref, refs = refs[0], refs[1:]
+    out_ref, weight, tokens, sems = refs
+    halves = range(2) if last is None else (last,)
+    used = slice(halves[0] * HALF, (halves[-1] + 1) * HALF)
     turn, col, core = [lax.axis_index(a) for a in ("z", "col", "row")]
     wide = HEADS * DH
     copies = []
@@ -156,41 +157,41 @@
         for j in range(HEADS):
             head = lax.rem(turn + SENDS[j], HEADS)
             cols = pl.ds(pl.multiple_of(head * DH, DH), DH)
-            for i in range(2):
+            for i in halves:
                 rows = pl.ds(pl.multiple_of(lax.rem(core + i, 2) * HALF, 16), HALF)
                 tokens[k, i * HALF : (i + 1) * HALF, cols] = blocks[k][rows, j * DH : (j + 1) * DH]
     for c in copies:
         c.wait()
-    total = None if first else acc_ref[...]
+    total = None if first else acc_ref[used, :]
     for k in range(n):
-        part = jnp.dot(tokens[k], weight[k], preferred_element_type=F32)
+        part = jnp.dot(tokens[k, used, :], weight[k], preferred_element_type=F32)
         total = part if total is None else total + part
-    if last:
-        outs[0][...] = total[:HALF]
-        outs[1][...] = total[HALF:].astype(BF)
+    if first:
+        out_ref[:HALF, :] = acc_ref[...].astype(F32) + total[:HALF]
+        out_ref[HALF:, :] = total[HALF:]
     else:
-        outs[0][...] = total
-
-
-def project(steps, last, weight, blocks, *total):
+        out_ref[...] = total.astype(out_ref.dtype)
+
+
+def project(steps, first, last, weight, blocks, total):
     n = len(steps)
     wide, width = HEADS * DH, weight.shape[1]
-    if last:
-        shapes = [jax.ShapeDtypeStruct((HALF, width), t) for t in (F32, BF)]
+    if last is None:
+        shape = jax.ShapeDtypeStruct((ROWS, width), F32)
     else:
-        shapes = [jax.ShapeDtypeStruct((ROWS, width), F32)]
+        shape = jax.ShapeDtypeStruct((HALF, width), BF if last else F32)
     return pl.pallas_call(
-        functools.partial(project_kernel, steps, not total, last),
-        out_shape=shapes,
-        in_specs=[ANY] + [VM] * (n + len(total)),
-        out_specs=[VM] * len(shapes),
+        functools.partial(project_kernel, steps, first, last),
+        out_shape=shape,
+        in_specs=[ANY] + [VM] * (n + 1),
+        out_specs=VM,
         scratch_shapes=[
             pltpu.VMEM((n, wide, width), BF),
             pltpu.VMEM((n, ROWS, wide), BF),
             pltpu.SemaphoreType.DMA((n,)),
         ],
         compiler_params=pltpu.CompilerParams(vmem_limit_bytes=VLIM),
-    )(weight, *blocks, *total)
+    )(weight, *blocks, total)
 
 
 def owner_pairs(j):
@@ -236,12 +237,13 @@
     attended = flash(True, held, far + [swap(p) for p in far], (a, b, c))
     mine = jnp.concatenate([from_owner(attended[j], j) for j in range(HEADS)], axis=1)
     far, near, back = [shift(mine, "col", NY, s) for s in (2, 1, 3)]
-    total = project((0,), False, out_weight, [mine])
-    near, back, *total = lax.optimization_barrier((near, back, *total))
-    total = project((1, 3), False, out_weight, [near, back], *total)
-    far, *total = lax.optimization_barrier((far, *total))
-    keep, send = project((2,), True, out_weight, [far], *total)
-    return (residual.astype(F32) + (keep + swap(send).astype(F32))).astype(BF)
+    total = project((0,), True, None, out_weight, [mine], residual)
+    near, back, total = lax.optimization_barrier((near, back, total))
+    total = project((1, 3), False, None, out_weight, [near, back], total)
+    far, total = lax.optimization_barrier((far, total))
+    send = swap(project((2,), False, 1, out_weight, [far], total))
+    keep = project((2,), False, 0, out_weight, [far], total)
+    return (keep + send.astype(F32)).astype(BF)
 
 
 def solution(mesh):

time: 92.8 us -> 92.5 us (level)
    pallas_call x3 -> x4, Pallas kernels: 3.1 us -> 3.44 us  [project(): pl.pallas_call(functools.partial(project_kernel, steps, first, last), out...]
where the time goes in v7:
time: 92.5 us; the launch traced here: 92.3 us
  starting transfers between devices  39 us (42%)
  waiting for transfers between devices  30.5 us (33%)
  Pallas kernels  21.6 us (23%)
    pallas_call x3, Pallas kernels, flash(): pl.pallas_call(functools.partial(flash_kernel, not state, last, nq, n, mo...  15.3 us
    ppermute x4, starting transfers between devices, to_owner(): return lax.ppermute(value, ('z', 'row'), owner_pairs(j))  15 us
    ppermute x4, waiting for transfers between devices, to_owner(): return lax.ppermute(value, ('z', 'row'), owner_pairs(j))  11.9 us
    ppermute x4, starting transfers between devices, from_owner(): lax.ppermute(value, ('z', 'row'), [(b, a) for a, b in owner_pairs(j)])  11.7 us
    ppermute x7, waiting for transfers between devices, shift(): lax.ppermute(value, axis, [(i, (i + step) % size) for i in range(size)])  10.4 us
    ppermute x7, starting transfers between devices, shift(): lax.ppermute(value, axis, [(i, (i + step) % size) for i in range(size)])  10.2 us
    ppermute x7, waiting for transfers between devices, swap(): return lax.ppermute(value, 'row', [(0, 1), (1, 0)])  4.32 us
    ppermute x4, waiting for transfers between devices, from_owner(): lax.ppermute(value, ('z', 'row'), [(b, a) for a, b in owner_pairs(j)])  3.85 us
  transfers between devices with their start and end apart: 22, of which 14 were waited for; matrix products, arithmetic and copies ran while one was open for 0% of the time, Pallas kernels for 15%

profile of v7, /device:TPU:1, one launch (start us, length us, event | category | flops | bytes accessed | tf_op | source)
XLA Modules:
  0.0 92.3 jit_solution(10969423020703383284)
XLA Ops:
  0.0 2.8 %shard_map.73 = (bf16[288,384]{1,0:T(8,128)(2,1)}, bf16[288,384]{1,0:T(8,128)(2,1)}, bf16[288,384]{1,0:T(8,128)(2,1)}, bf16[288,384]{1,0:T(8,128)(2,1)}) custom-call(bf16[288,512]{1,0:T(8,128)(2,1)} %refs_0_.1, f32[1,512]{1,0:T(1,128)} %bitcast.4, bf16[288,512]{1,0:T(8,128)(2,1)} %refs_2_.1, bf16[288,512]{1,0:T(8,128)(2,1)} %refs_3_.1, f32[1,512]{1,0:T(1,128)} %bitcast.5), custom_call_target="tpu_custom_call" | custom-call | tf_op jit(solution)/shard_map/pallas_call | solution.py:59
  2.8 7.0 %collective-permute-start = (bf16[288,384]{1,0:T(8,128)(2,1)}, bf16[288,384]{1,0:T(8,128)(2,1)S(1)}, u32[]{:S(2)}, u32[]{:S(2)}) collective-permute-start(bf16[288,384]{1,0:T(8,128)(2,1)} %get-tuple-element.34), channel_id=1, source_target_pairs={{0,96},{4,224},{32,0},{36,128},{64,32},{68,160},{96,64},{100,192},... | collective-permute-start | bytes 663560 | tf_op jit(solution)/shard_map/ppermute | solution.py:206
  10.4 4.7 %collective-permute-start.2 = (bf16[288,384]{1,0:T(8,128)(2,1)}, bf16[288,384]{1,0:T(8,128)(2,1)S(1)}, u32[]{:S(2)}, u32[]{:S(2)}) collective-permute-start(bf16[288,384]{1,0:T(8,128)(2,1)} %get-tuple-element.36), channel_id=1, source_target_pairs={{0,32},{4,160},{32,64},{36,192},{64,96},{68,224},{96,0},{100,128},... | collective-permute-start | bytes 663560 | tf_op jit(solution)/shard_map/ppermute | solution.py:206
  15.1 2.8 %collective-permute-start.3 = (bf16[288,384]{1,0:T(8,128)(2,1)}, bf16[288,384]{1,0:T(8,128)(2,1)S(1)}, u32[]{:S(2)}, u32[]{:S(2)}) collective-permute-start(bf16[288,384]{1,0:T(8,128)(2,1)} %get-tuple-element.37), channel_id=1, source_target_pairs={{0,0},{4,128},{32,32},{36,160},{64,64},{68,192},{96,96},{100,224},... | collective-permute-start | bytes 663560 | tf_op jit(solution)/shard_map/ppermute | solution.py:206
  17.9 3.2 %collective-permute-done.refs_0_ = bf16[288,384]{1,0:T(8,128)(2,1)S(1)} collective-permute-done((bf16[288,384]{1,0:T(8,128)(2,1)}, bf16[288,384]{1,0:T(8,128)(2,1)S(1)}, u32[]{:S(2)}, u32[]{:S(2)}) %collective-permute-start) | collective-permute-done | bytes 221216 | tf_op jit(solution)/shard_map/ppermute | solution.py:206
  21.1 6.1 %collective-permute-done.1.refs_1_ = bf16[288,384]{1,0:T(8,128)(2,1)S(1)} collective-permute-done((bf16[288,384]{1,0:T(8,128)(2,1)}, bf16[288,384]{1,0:T(8,128)(2,1)S(1)}, u32[]{:S(2)}, u32[]{:S(2)}) %collective-permute-start.1) | collective-permute-done | bytes 221216 | tf_op jit(solution)/shard_map/ppermute | solution.py:206
  27.2 2.5 %collective-permute-done.2.refs_2_ = bf16[288,384]{1,0:T(8,128)(2,1)S(1)} collective-permute-done((bf16[288,384]{1,0:T(8,128)(2,1)}, bf16[288,384]{1,0:T(8,128)(2,1)S(1)}, u32[]{:S(2)}, u32[]{:S(2)}) %collective-permute-start.2) | collective-permute-done | bytes 221216 | tf_op jit(solution)/shard_map/ppermute | solution.py:206
  29.9 1.3 %collective-permute-start.4 = (bf16[1152,256]{1,0:T(8,128)(2,1)S(1)}, bf16[1152,256]{1,0:T(8,128)(2,1)S(1)}, u32[]{:S(2)}, u32[]{:S(2)}) collective-permute-start(bf16[1152,256]{1,0:T(8,128)(2,1)S(1)} %pad_maximum_fusion.refs_4_), channel_id=1, source_target_pairs={{0,8},{8,16},{16,24},{24,0},{1,9},{9,17},{17,25},{25,1},{2,10},{10... | collective-permute-start | bytes 1769480 | tf_op jit(solution)/shard_map/ppermute | solution.py:216
  31.2 1.5 %collective-permute-start.6 = (bf16[1152,256]{1,0:T(8,128)(2,1)S(1)}, bf16[1152,256]{1,0:T(8,128)(2,1)S(1)}, u32[]{:S(2)}, u32[]{:S(2)}) collective-permute-start(bf16[1152,256]{1,0:T(8,128)(2,1)S(1)} %pad_maximum_fusion.refs_4_), channel_id=1, source_target_pairs={{0,24},{8,0},{16,8},{24,16},{1,25},{9,1},{17,9},{25,17},{2,26},{10... | collective-permute-start | bytes 1769480 | tf_op jit(solution)/shard_map/ppermute | solution.py:216
  33.3 1.1 %collective-permute-done.8.refs_5_ = bf16[576,256]{1,0:T(8,128)(2,1)S(1)} collective-permute-done((bf16[576,256]{1,0:T(8,128)(2,1)S(1)}, bf16[576,256]{1,0:T(8,128)(2,1)S(1)}, u32[]{:S(2)}, u32[]{:S(2)}) %collective-permute-start.8) | collective-permute-done | bytes 294944 | tf_op jit(solution)/shard_map/ppermute | solution.py:220
  34.8 4.0 %shard_map.74 = (f32[1152,128]{1,0:T(8,128)S(1)}, f32[1152,128]{1,0:T(8,128)S(1)}, f32[1152,128]{1,0:T(8,128)S(1)}) custom-call(bf16[288,384]{1,0:T(8,128)(2,1)S(1)} %collective-permute-done.refs_0_, bf16[288,384]{1,0:T(8,128)(2,1)S(1)} %collective-permute-done.1.refs_1_, bf16[288,384]{1,0:T(8,128)(2,1)S(1)} %collective-permute-done.2.refs_2_, ...), custom_call_target="tpu_custom_call" | custom-call | flops 1000 | bytes 1000 | tf_op jit(solution)/shard_map/pallas_call | solution.py:130
  38.8 5.3 %collective-permute-done.4.refs_4_ = bf16[1152,256]{1,0:T(8,128)(2,1)S(1)} collective-permute-done((bf16[1152,256]{1,0:T(8,128)(2,1)S(1)}, bf16[1152,256]{1,0:T(8,128)(2,1)S(1)}, u32[]{:S(2)}, u32[]{:S(2)}) %collective-permute-start.4) | collective-permute-done | bytes 589856 | tf_op jit(solution)/shard_map/ppermute | solution.py:216
  44.9 1.3 %collective-permute-start.5 = (bf16[576,256]{1,0:T(8,128)(2,1)S(1)}, bf16[576,256]{1,0:T(8,128)(2,1)S(1)}, u32[]{:S(2)}, u32[]{:S(2)}) collective-permute-start(bf16[576,256]{1,0:T(8,128)(2,1)S(1)} %slice.32), channel_id=1, source_target_pairs={{0,8},{8,16},{16,24},{24,0},{1,9},{9,17},{17,25},{25,1},{2,10},{10... | collective-permute-start | bytes 884744 | tf_op jit(solution)/shard_map/ppermute | solution.py:216
  46.2 1.7 %collective-permute-start.7 = (bf16[576,256]{1,0:T(8,128)(2,1)S(1)}, bf16[576,256]{1,0:T(8,128)(2,1)S(1)}, u32[]{:S(2)}, u32[]{:S(2)}) collective-permute-start(bf16[576,256]{1,0:T(8,128)(2,1)S(1)} %slice.33), channel_id=1, source_target_pairs={{0,24},{8,0},{16,8},{24,16},{1,25},{9,1},{17,9},{25,17},{2,26},{10... | collective-permute-start | bytes 884744 | tf_op jit(solution)/shard_map/ppermute | solution.py:216
  48.0 7.1 %shard_map.75 = (f32[1152,128]{1,0:T(8,128)S(1)}, f32[1152,128]{1,0:T(8,128)S(1)}, f32[1152,128]{1,0:T(8,128)S(1)}) custom-call(bf16[288,384]{1,0:T(8,128)(2,1)S(1)} %collective-permute-done.refs_0_, bf16[288,384]{1,0:T(8,128)(2,1)S(1)} %collective-permute-done.1.refs_1_, bf16[288,384]{1,0:T(8,128)(2,1)S(1)} %collective-permute-done.2.refs_2_, ...), custom_call_target="tpu_custom_call" | custom-call | flops 1000 | bytes 1000 | tf_op jit(solution)/shard_map/pallas_call | solution.py:130
  55.2 0.8 collective-permute-start.12
  55.9 1.2 %collective-permute-done.12.refs_6_ = bf16[576,256]{1,0:T(8,128)(2,1)S(1)} collective-permute-done((bf16[576,256]{1,0:T(8,128)(2,1)S(1)}, bf16[576,256]{1,0:T(8,128)(2,1)S(1)}, u32[]{:S(2)}, u32[]{:S(2)}) %collective-permute-start.12) | collective-permute-done | bytes 294944 | tf_op jit(solution)/shard_map/ppermute | solution.py:220
  57.5 4.2 %shard_map.76 = (bf16[288,128]{1,0:T(8,128)(2,1)S(1)}, bf16[288,128]{1,0:T(8,128)(2,1)S(1)}, bf16[288,128]{1,0:T(8,128)(2,1)S(1)}, bf16[288,128]{1,0:T(8,128)(2,1)S(1)}) custom-call(bf16[288,384]{1,0:T(8,128)(2,1)S(1)} %collective-permute-done.refs_0_, bf16[288,384]{1,0:T(8,128)(2,1)S(1)} %collective-permute-done.1.refs_1_, ...), custom_call_target="tpu_custom_call" | custom-call | flops 1000 | bytes 1000 | tf_op jit(solution)/shard_map/pallas_call | solution.py:130
  61.7 3.9 %collective-permute-start.14 = (bf16[288,128]{1,0:T(8,128)(2,1)S(1)}, bf16[288,128]{1,0:T(8,128)(2,1)S(1)}, u32[]{:S(2)}, u32[]{:S(2)}) collective-permute-start(bf16[288,128]{1,0:T(8,128)(2,1)S(1)} %get-tuple-element.54), channel_id=1, source_target_pairs={{96,0},{224,4},{0,32},{128,36},{32,64},{160,68},{64,96},{192,100},... | collective-permute-start | bytes 221192 | tf_op jit(solution)/shard_map/ppermute | solution.py:210
  65.6 2.2 %collective-permute-start.16 = (bf16[288,128]{1,0:T(8,128)(2,1)S(1)}, bf16[288,128]{1,0:T(8,128)(2,1)S(1)}, u32[]{:S(2)}, u32[]{:S(2)}) collective-permute-start(bf16[288,128]{1,0:T(8,128)(2,1)S(1)} %get-tuple-element.56), channel_id=1, source_target_pairs={{32,0},{160,4},{64,32},{192,36},{96,64},{224,68},{0,96},{128,100},... | collective-permute-start | bytes 221192 | tf_op jit(solution)/shard_map/ppermute | solution.py:210
  67.8 5.6 %collective-permute-start.17 = (bf16[288,128]{1,0:T(8,128)(2,1)S(1)}, bf16[288,128]{1,0:T(8,128)(2,1)S(1)}, u32[]{:S(2)}, u32[]{:S(2)}) collective-permute-start(bf16[288,128]{1,0:T(8,128)(2,1)S(1)} %get-tuple-element.57), channel_id=1, source_target_pairs={{0,0},{128,4},{32,32},{160,36},{64,64},{192,68},{96,96},{224,100},... | collective-permute-start | bytes 221192 | tf_op jit(solution)/shard_map/ppermute | solution.py:210
  73.6 3.8 %collective-permute-done.17 = bf16[288,128]{1,0:T(8,128)(2,1)S(1)} collective-permute-done((bf16[288,128]{1,0:T(8,128)(2,1)S(1)}, bf16[288,128]{1,0:T(8,128)(2,1)S(1)}, u32[]{:S(2)}, u32[]{:S(2)}) %collective-permute-start.17) | collective-permute-done | bytes 73760 | tf_op jit(solution)/shard_map/ppermute | solution.py:210
  77.4 1.4 %collective-permute-start.19 = (bf16[288,512]{1,0:T(8,128)(2,1)S(1)}, bf16[288,512]{1,0:T(8,128)(2,1)S(1)}, u32[]{:S(2)}, u32[]{:S(2)}) collective-permute-start(bf16[288,512]{1,0:T(8,128)(2,1)S(1)} %constant_dynamic-update-slice_fusion.refs_0_), channel_id=1, source_target_pairs={{0,1},{1,2},{2,3},{3,0},{4,5},{5,6},{6,7},{7,4},{8,9},{9,10},{10,1... | collective-permute-start | bytes 884744 | tf_op jit(solution)/shard_map/ppermute | solution.py:216
  78.8 1.5 %collective-permute-start.20 = (bf16[288,512]{1,0:T(8,128)(2,1)S(1)}, bf16[288,512]{1,0:T(8,128)(2,1)S(1)}, u32[]{:S(2)}, u32[]{:S(2)}) collective-permute-start(bf16[288,512]{1,0:T(8,128)(2,1)S(1)} %constant_dynamic-update-slice_fusion.refs_0_), channel_id=1, source_target_pairs={{0,3},{1,0},{2,1},{3,2},{4,7},{5,4},{6,5},{7,6},{8,11},{9,8},{10,9... | collective-permute-start | bytes 884744 | tf_op jit(solution)/shard_map/ppermute | solution.py:216
  80.3 1.6 %collective-permute-start.18 = (bf16[288,512]{1,0:T(8,128)(2,1)S(1)}, bf16[288,512]{1,0:T(8,128)(2,1)S(1)}, u32[]{:S(2)}, u32[]{:S(2)}) collective-permute-start(bf16[288,512]{1,0:T(8,128)(2,1)S(1)} %constant_dynamic-update-slice_fusion.refs_0_), channel_id=1, source_target_pairs={{0,2},{1,3},{2,0},{3,1},{4,6},{5,7},{6,4},{7,5},{8,10},{9,11},{10,... | collective-permute-start | bytes 884744 | tf_op jit(solution)/shard_map/ppermute | solution.py:216
  81.9 0.8 shard_map.77.refs_2_
  82.8 3.1 %collective-permute-done.19.refs_0_ = bf16[288,512]{1,0:T(8,128)(2,1)S(1)} collective-permute-done((bf16[288,512]{1,0:T(8,128)(2,1)S(1)}, bf16[288,512]{1,0:T(8,128)(2,1)S(1)}, u32[]{:S(2)}, u32[]{:S(2)}) %collective-permute-start.19) | collective-permute-done | bytes 294944 | tf_op jit(solution)/shard_map/ppermute | solution.py:216
  85.9 1.5 %shard_map.78.refs_1_ = f32[288,1536]{1,0:T(8,128)S(1)} custom-call(bf16[2048,1536]{1,0:T(8,128)(2,1)S(1)} %bitcast.3, bf16[288,512]{1,0:T(8,128)(2,1)S(1)} %collective-permute-done.19.refs_0_, bf16[288,512]{1,0:T(8,128)(2,1)S(1)} %collective-permute-done.20.refs_1_, f32[288,1536]{1,0:T(8,128)S(1)} %shard_map.77.refs_2_), custom_call_target="tpu_custom_call" | custom-call | tf_op jit(solution)/shard_map/pallas_call | solution.py:183
  87.4 1.7 %collective-permute-done.18.refs_0_ = bf16[288,512]{1,0:T(8,128)(2,1)S(1)} collective-permute-done((bf16[288,512]{1,0:T(8,128)(2,1)S(1)}, bf16[288,512]{1,0:T(8,128)(2,1)S(1)}, u32[]{:S(2)}, u32[]{:S(2)}) %collective-permute-start.18) | collective-permute-done | bytes 294944 | tf_op jit(solution)/shard_map/ppermute | solution.py:216
  89.7 0.6 shard_map.79
  90.3 1.2 %collective-permute-done.21 = bf16[144,1536]{1,0:T(8,128)(2,1)S(1)} collective-permute-done((bf16[144,1536]{1,0:T(8,128)(2,1)S(1)}, bf16[144,1536]{1,0:T(8,128)(2,1)S(1)}, u32[]{:S(2)}, u32[]{:S(2)}) %collective-permute-start.21) | collective-permute-done | bytes 442400 | tf_op jit(solution)/shard_map/ppermute | solution.py:220
  91.5 0.8 add_convert_fusion
  (41 shorter events, 3.8 us)
Async XLA Ops:
  2.8 18.2 %collective-permute-start = (bf16[288,384]{1,0:T(8,128)(2,1)}, bf16[288,384]{1,0:T(8,128)(2,1)S(1)}, u32[]{:S(2)}, u32[]{:S(2)}) collective-permute-start(bf16[288,384]{1,0:T(8,128)(2,1)} %get-tuple-element.34), channel_id=1, source_target_pairs={{0,96},{4,224},{32,0},{36,128},{64,32},{68,160},{96,64},{100,192},... | collective-permute-start | bytes 663560 | tf_op jit(solution)/shard_map/ppermute | solution.py:206
  9.9 17.3 %collective-permute-start.1 = (bf16[288,384]{1,0:T(8,128)(2,1)}, bf16[288,384]{1,0:T(8,128)(2,1)S(1)}, u32[]{:S(2)}, u32[]{:S(2)}) collective-permute-start(bf16[288,384]{1,0:T(8,128)(2,1)} %get-tuple-element.35), channel_id=1, source_target_pairs={{0,64},{4,192},{32,96},{36,224},{64,0},{68,128},{96,32},{100,160},... | collective-permute-start | bytes 663560 | tf_op jit(solution)/shard_map/ppermute | solution.py:206
  10.4 19.3 %collective-permute-start.2 = (bf16[288,384]{1,0:T(8,128)(2,1)}, bf16[288,384]{1,0:T(8,128)(2,1)S(1)}, u32[]{:S(2)}, u32[]{:S(2)}) collective-permute-start(bf16[288,384]{1,0:T(8,128)(2,1)} %get-tuple-element.36), channel_id=1, source_target_pairs={{0,32},{4,160},{32,64},{36,192},{64,96},{68,224},{96,0},{100,128},... | collective-permute-start | bytes 663560 | tf_op jit(solution)/shard_map/ppermute | solution.py:206
  15.1 14.7 %collective-permute-start.3 = (bf16[288,384]{1,0:T(8,128)(2,1)}, bf16[288,384]{1,0:T(8,128)(2,1)S(1)}, u32[]{:S(2)}, u32[]{:S(2)}) collective-permute-start(bf16[288,384]{1,0:T(8,128)(2,1)} %get-tuple-element.37), channel_id=1, source_target_pairs={{0,0},{4,128},{32,32},{36,160},{64,64},{68,192},{96,96},{100,224},... | collective-permute-start | bytes 663560 | tf_op jit(solution)/shard_map/ppermute | solution.py:206
  29.9 14.2 %collective-permute-start.4 = (bf16[1152,256]{1,0:T(8,128)(2,1)S(1)}, bf16[1152,256]{1,0:T(8,128)(2,1)S(1)}, u32[]{:S(2)}, u32[]{:S(2)}) collective-permute-start(bf16[1152,256]{1,0:T(8,128)(2,1)S(1)} %pad_maximum_fusion.refs_4_), channel_id=1, source_target_pairs={{0,8},{8,16},{16,24},{24,0},{1,9},{9,17},{17,25},{25,1},{2,10},{10... | collective-permute-start | bytes 1769480 | tf_op jit(solution)/shard_map/ppermute | solution.py:216
  31.2 13.2 %collective-permute-start.6 = (bf16[1152,256]{1,0:T(8,128)(2,1)S(1)}, bf16[1152,256]{1,0:T(8,128)(2,1)S(1)}, u32[]{:S(2)}, u32[]{:S(2)}) collective-permute-start(bf16[1152,256]{1,0:T(8,128)(2,1)S(1)} %pad_maximum_fusion.refs_4_), channel_id=1, source_target_pairs={{0,24},{8,0},{16,8},{24,16},{1,25},{9,1},{17,9},{25,17},{2,26},{10... | collective-permute-start | bytes 1769480 | tf_op jit(solution)/shard_map/ppermute | solution.py:216
  32.7 1.7 %collective-permute-start.8 = (bf16[576,256]{1,0:T(8,128)(2,1)S(1)}, bf16[576,256]{1,0:T(8,128)(2,1)S(1)}, u32[]{:S(2)}, u32[]{:S(2)}) collective-permute-start(bf16[576,256]{1,0:T(8,128)(2,1)S(1)} %pad_maximum_fusion.1), channel_id=1, source_target_pairs={{0,4},{4,0},{1,5},{5,1},{2,6},{6,2},{3,7},{7,3},{8,12},{12,8},{9,1... | collective-permute-start | bytes 884744 | tf_op jit(solution)/shard_map/ppermute | solution.py:220
  32.8 2.0 %collective-permute-start.9 = (bf16[576,256]{1,0:T(8,128)(2,1)S(1)}, bf16[576,256]{1,0:T(8,128)(2,1)S(1)}, u32[]{:S(2)}, u32[]{:S(2)}) collective-permute-start(bf16[576,256]{1,0:T(8,128)(2,1)S(1)} %pad_maximum_fusion.2), channel_id=1, source_target_pairs={{0,4},{4,0},{1,5},{5,1},{2,6},{6,2},{3,7},{7,3},{8,12},{12,8},{9,1... | collective-permute-start | bytes 884744 | tf_op jit(solution)/shard_map/ppermute | solution.py:220
  34.8 47.1 %slice-start = ((s8[6291456]{0:T(1024)(128)(4,1)}), s8[4194304]{0:T(1024)(128)(4,1)S(1)}, s32[]{:S(2)}) async-start(s8[6291456]{0:T(1024)(128)(4,1)} %bitcast.2), calls=%async_computation | async-start | bytes 8388608
  44.4 3.6 %collective-permute-start.10 = (bf16[1152,256]{1,0:T(8,128)(2,1)S(1)}, bf16[1152,256]{1,0:T(8,128)(2,1)S(1)}, u32[]{:S(2)}, u32[]{:S(2)}) collective-permute-start(bf16[1152,256]{1,0:T(8,128)(2,1)S(1)} %collective-permute-done.4.refs_4_), channel_id=1, source_target_pairs={{0,4},{4,0},{1,5},{5,1},{2,6},{6,2},{3,7},{7,3},{8,12},{12,8},{9,1... | collective-permute-start | bytes 1769480 | tf_op jit(solution)/shard_map/ppermute | solution.py:220
  44.4 3.6 %collective-permute-start.11 = (bf16[1152,256]{1,0:T(8,128)(2,1)S(1)}, bf16[1152,256]{1,0:T(8,128)(2,1)S(1)}, u32[]{:S(2)}, u32[]{:S(2)}) collective-permute-start(bf16[1152,256]{1,0:T(8,128)(2,1)S(1)} %collective-permute-done.6.refs_5_), channel_id=1, source_target_pairs={{0,4},{4,0},{1,5},{5,1},{2,6},{6,2},{3,7},{7,3},{8,12},{12,8},{9,1... | collective-permute-start | bytes 1769480 | tf_op jit(solution)/shard_map/ppermute | solution.py:220
  44.9 10.2 %collective-permute-start.5 = (bf16[576,256]{1,0:T(8,128)(2,1)S(1)}, bf16[576,256]{1,0:T(8,128)(2,1)S(1)}, u32[]{:S(2)}, u32[]{:S(2)}) collective-permute-start(bf16[576,256]{1,0:T(8,128)(2,1)S(1)} %slice.32), channel_id=1, source_target_pairs={{0,8},{8,16},{16,24},{24,0},{1,9},{9,17},{17,25},{25,1},{2,10},{10... | collective-permute-start | bytes 884744 | tf_op jit(solution)/shard_map/ppermute | solution.py:216
  46.2 35.7 %slice-start.1 = ((s8[6291456]{0:T(1024)(128)(4,1)}), s8[2097152]{0:T(1024)(128)(4,1)S(1)}, s32[]{:S(2)}) async-start(s8[6291456]{0:T(1024)(128)(4,1)} %bitcast.2), calls=%async_computation.1 | async-start | bytes 4194304
  46.2 8.9 %collective-permute-start.7 = (bf16[576,256]{1,0:T(8,128)(2,1)S(1)}, bf16[576,256]{1,0:T(8,128)(2,1)S(1)}, u32[]{:S(2)}, u32[]{:S(2)}) collective-permute-start(bf16[576,256]{1,0:T(8,128)(2,1)S(1)} %slice.33), channel_id=1, source_target_pairs={{0,24},{8,0},{16,8},{24,16},{1,25},{9,1},{17,9},{25,17},{2,26},{10... | collective-permute-start | bytes 884744 | tf_op jit(solution)/shard_map/ppermute | solution.py:216
  55.1 26.8 %copy-start = (bf16[144,1536]{1,0:T(8,128)(2,1)S(1)}, bf16[144,1536]{1,0:T(8,128)(2,1)}, u32[]{:S(2)}) copy-start(bf16[144,1536]{1,0:T(8,128)(2,1)} %refs_1_.1) | copy-start | bytes 1327108
  55.2 2.0 %collective-permute-start.12 = (bf16[576,256]{1,0:T(8,128)(2,1)S(1)}, bf16[576,256]{1,0:T(8,128)(2,1)S(1)}, u32[]{:S(2)}, u32[]{:S(2)}) collective-permute-start(bf16[576,256]{1,0:T(8,128)(2,1)S(1)} %collective-permute-done.5.refs_4_), channel_id=1, source_target_pairs={{0,4},{4,0},{1,5},{5,1},{2,6},{6,2},{3,7},{7,3},{8,12},{12,8},{9,1... | collective-permute-start | bytes 884744 | tf_op jit(solution)/shard_map/ppermute | solution.py:220
  55.9 1.6 %collective-permute-start.13 = (bf16[576,256]{1,0:T(8,128)(2,1)S(1)}, bf16[576,256]{1,0:T(8,128)(2,1)S(1)}, u32[]{:S(2)}, u32[]{:S(2)}) collective-permute-start(bf16[576,256]{1,0:T(8,128)(2,1)S(1)} %collective-permute-done.7.refs_5_), channel_id=1, source_target_pairs={{0,4},{4,0},{1,5},{5,1},{2,6},{6,2},{3,7},{7,3},{8,12},{12,8},{9,1... | collective-permute-start | bytes 884744 | tf_op jit(solution)/shard_map/ppermute | solution.py:220
  61.7 11.8 %collective-permute-start.14 = (bf16[288,128]{1,0:T(8,128)(2,1)S(1)}, bf16[288,128]{1,0:T(8,128)(2,1)S(1)}, u32[]{:S(2)}, u32[]{:S(2)}) collective-permute-start(bf16[288,128]{1,0:T(8,128)(2,1)S(1)} %get-tuple-element.54), channel_id=1, source_target_pairs={{96,0},{224,4},{0,32},{128,36},{32,64},{160,68},{64,96},{192,100},... | collective-permute-start | bytes 221192 | tf_op jit(solution)/shard_map/ppermute | solution.py:210
  65.6 7.9 %collective-permute-start.15 = (bf16[288,128]{1,0:T(8,128)(2,1)S(1)}, bf16[288,128]{1,0:T(8,128)(2,1)S(1)}, u32[]{:S(2)}, u32[]{:S(2)}) collective-permute-start(bf16[288,128]{1,0:T(8,128)(2,1)S(1)} %get-tuple-element.55), channel_id=1, source_target_pairs={{64,0},{192,4},{96,32},{224,36},{0,64},{128,68},{32,96},{160,100},... | collective-permute-start | bytes 221192 | tf_op jit(solution)/shard_map/ppermute | solution.py:210
  65.6 7.9 %collective-permute-start.16 = (bf16[288,128]{1,0:T(8,128)(2,1)S(1)}, bf16[288,128]{1,0:T(8,128)(2,1)S(1)}, u32[]{:S(2)}, u32[]{:S(2)}) collective-permute-start(bf16[288,128]{1,0:T(8,128)(2,1)S(1)} %get-tuple-element.56), channel_id=1, source_target_pairs={{32,0},{160,4},{64,32},{192,36},{96,64},{224,68},{0,96},{128,100},... | collective-permute-start | bytes 221192 | tf_op jit(solution)/shard_map/ppermute | solution.py:210
  67.8 9.6 %collective-permute-start.17 = (bf16[288,128]{1,0:T(8,128)(2,1)S(1)}, bf16[288,128]{1,0:T(8,128)(2,1)S(1)}, u32[]{:S(2)}, u32[]{:S(2)}) collective-permute-start(bf16[288,128]{1,0:T(8,128)(2,1)S(1)} %get-tuple-element.57), channel_id=1, source_target_pairs={{0,0},{128,4},{32,32},{160,36},{64,64},{192,68},{96,96},{224,100},... | collective-permute-start | bytes 221192 | tf_op jit(solution)/shard_map/ppermute | solution.py:210
  77.4 8.5 %collective-permute-start.19 = (bf16[288,512]{1,0:T(8,128)(2,1)S(1)}, bf16[288,512]{1,0:T(8,128)(2,1)S(1)}, u32[]{:S(2)}, u32[]{:S(2)}) collective-permute-start(bf16[288,512]{1,0:T(8,128)(2,1)S(1)} %constant_dynamic-update-slice_fusion.refs_0_), channel_id=1, source_target_pairs={{0,1},{1,2},{2,3},{3,0},{4,5},{5,6},{6,7},{7,4},{8,9},{9,10},{10,1... | collective-permute-start | bytes 884744 | tf_op jit(solution)/shard_map/ppermute | solution.py:216
  78.8 7.1 %collective-permute-start.20 = (bf16[288,512]{1,0:T(8,128)(2,1)S(1)}, bf16[288,512]{1,0:T(8,128)(2,1)S(1)}, u32[]{:S(2)}, u32[]{:S(2)}) collective-permute-start(bf16[288,512]{1,0:T(8,128)(2,1)S(1)} %constant_dynamic-update-slice_fusion.refs_0_), channel_id=1, source_target_pairs={{0,3},{1,0},{2,1},{3,2},{4,7},{5,4},{6,5},{7,6},{8,11},{9,8},{10,9... | collective-permute-start | bytes 884744 | tf_op jit(solution)/shard_map/ppermute | solution.py:216
  80.3 8.7 %collective-permute-start.18 = (bf16[288,512]{1,0:T(8,128)(2,1)S(1)}, bf16[288,512]{1,0:T(8,128)(2,1)S(1)}, u32[]{:S(2)}, u32[]{:S(2)}) collective-permute-start(bf16[288,512]{1,0:T(8,128)(2,1)S(1)} %constant_dynamic-update-slice_fusion.refs_0_), channel_id=1, source_target_pairs={{0,2},{1,3},{2,0},{3,1},{4,6},{5,7},{6,4},{7,5},{8,10},{9,11},{10,... | collective-permute-start | bytes 884744 | tf_op jit(solution)/shard_map/ppermute | solution.py:216
  89.6 1.9 %collective-permute-start.21 = (bf16[144,1536]{1,0:T(8,128)(2,1)S(1)}, bf16[144,1536]{1,0:T(8,128)(2,1)S(1)}, u32[]{:S(2)}, u32[]{:S(2)}) collective-permute-start(bf16[144,1536]{1,0:T(8,128)(2,1)S(1)} %shard_map.80), channel_id=1, source_target_pairs={{0,4},{4,0},{1,5},{5,1},{2,6},{6,2},{3,7},{7,3},{8,12},{12,8},{9,1... | collective-permute-start | bytes 1327112 | tf_op jit(solution)/shard_map/ppermute | solution.py:220
